TPU v7x, 128 devices: a whole 4x4x4 slice. The times are simulated.
128 devices in a mesh: row: 4 (over x_lo, core), col: 32 (over x_hi, y, z).
Axes of the slice: x: 4 (x_hi: 2, x_lo: 2; x = x_hi * 2 + x_lo), y: 4, z: 4, core: 2. Of those that a mesh axis runs over, the one named last changes fastest.
Arguments:
- latent: bfloat16 [32, 8, 64, 1536], P(None, 'row', 'col'), may hold values from -6 to 6
- out_grad: bfloat16 [32, 8, 64, 1536], P(None, 'row', 'col'), may hold values from -6 to 6
- w_in: bfloat16 [1536, 1536], replicated, may hold values from -0.15625 to 0.15625
- w_out: bfloat16 [1536, 1536], replicated, may hold values from -0.15625 to 0.15625
- w_select: bfloat16 [1536, 128], replicated, may hold values from -0.15625 to 0.15625
- w_dt: bfloat16 [1536, 96], replicated, may hold values from -0.625 to 0.625
- dt_bias: float32 [1536], replicated, may hold values from -4 to -1
- a_log: float32 [1536, 16], replicated, may hold values from -3 to 1
- d_skip: float32 [1536], replicated, may hold values from 0.5 to 1.5
- w_mod: bfloat16 [3072, 256], replicated, may hold values from -0.375 to 0.375
- t_index: int32 [1], replicated, may hold values from 0 to 999
- frame_order: int32 [32], replicated, may hold values from 0 to 31, each once
- row_order: int32 [8], replicated, may hold values from 0 to 7, each once
- col_order: int32 [64], replicated, may hold values from 0 to 63, each once
Outputs:
- branch_out: bfloat16 [32, 8, 64, 1536], P(None, 'row', 'col')
- latent_grad: bfloat16 [32, 8, 64, 1536], P(None, 'row', 'col')
- grad_w_in: float32 [1536, 1536], P(('row', 'col'))
- grad_w_out: float32 [1536, 1536], P(('row', 'col'))
- grad_w_select: float32 [1536, 128], P(('row', 'col'))
- grad_w_dt: float32 [1536, 96], P(('row', 'col'))
- grad_dt_bias: float32 [1536], P(('row', 'col'))
- grad_a_log: float32 [1536, 16], P(('row', 'col'))
- grad_d_skip: float32 [1536], P(('row', 'col'))
- grad_w_mod: float32 [3072, 256], P(('row', 'col'))
Inputs may be any that keep to these rules, and one draw needn't show every extreme that they name: `frame_order`: each frame index appears once. `row_order`: each row index appears once. `col_order`: each column index appears once.
All inputs are finite; a program needn't handle non-finite values.
Results may differ from a plain program's by a relative error of at most 0.015.
Values may be sent and summed in bfloat16 or wider, within the bound.
No kernel may reach another device: no remote copies, remote signals or barrier semaphores. Data moves between devices by JAX's collectives and lax.ppermute only.
A program may use at most 192 MiB of HBM per device.

v0:
```python
import math

import jax
import jax.numpy as jnp
from jax import lax
from jax.sharding import PartitionSpec as P


def time_features(step_index, width):
    halfway = width // 2
    frequency = jnp.exp(-math.log(10000.0) * jnp.arange(halfway, dtype=jnp.float32) / halfway)
    angles = step_index.astype(jnp.float32)[0] * frequency
    return jnp.concatenate([jnp.cos(angles), jnp.sin(angles)])


def modulate(inputs, shift_vec, scale_vec):
    widened = inputs.astype(jnp.float32)
    inverse = lax.rsqrt(jnp.mean(widened * widened, axis=-1, keepdims=True) + 1e-06)
    normed = widened * inverse
    return (normed, inverse, (normed * (1.0 + scale_vec) + shift_vec).astype(jnp.bfloat16))


def ssm_scan(values, spacing, input_map, output_map, rates):

    def advance(state, column):
        value_t, space_t, in_t, out_t = column
        state = (
            jnp.exp(space_t[:, None, :] * rates) * state
            + (space_t * value_t)[:, None, :] * in_t[:, :, None]
        )
        return (state, jnp.sum(state * out_t[:, :, None], axis=1))

    start = jnp.zeros((values.shape[1], rates.shape[0], values.shape[2]), jnp.float32)
    _, result = lax.scan(
        jax.checkpoint(advance), start, (values, spacing, input_map, output_map), unroll=8
    )
    return result


def direction_pass(activ, cotangent, params, scan_axis, visit_order):
    w_select, w_dt, dt_bias, a_log = params
    length = activ.shape[scan_axis]
    inner = activ.shape[-1]
    rank = w_dt.shape[1]
    states = a_log.shape[1]
    positions = jnp.arange(length, dtype=jnp.int32)
    inverse_order = jnp.sum(
        positions[None, :] * (visit_order[None, :] == positions[:, None]).astype(jnp.int32), axis=1
    )

    def arrange(array):
        return jnp.moveaxis(jnp.take(array, visit_order, axis=scan_axis), scan_axis, 0)

    def restore(array, shape):
        return jnp.take(
            jnp.moveaxis(array.reshape(shape), 0, scan_axis), inverse_order, axis=scan_axis
        )

    ordered = arrange(activ)
    shape = ordered.shape
    flat = ordered.reshape(-1, inner)
    select_out = jnp.dot(flat, w_select, preferred_element_type=jnp.float32)
    low_rank = select_out[:, :rank].astype(jnp.bfloat16)
    spacing_pre = (
        lax.dot_general(
            low_rank, w_dt, (((1,), (1,)), ((), ())), preferred_element_type=jnp.float32
        )
        + dt_bias
    )
    spacing = jax.nn.softplus(spacing_pre)
    rates = -jnp.exp(a_log).T
    seq_shape = (length, flat.shape[0] // length)
    values = flat.astype(jnp.float32).reshape(seq_shape + (inner,))
    spaced = spacing.reshape(seq_shape + (inner,))
    in_seq = select_out[:, rank : rank + states].reshape(seq_shape + (states,))
    out_seq = select_out[:, rank + states :].reshape(seq_shape + (states,))
    cot_seq = arrange(cotangent).astype(jnp.float32).reshape(seq_shape + (inner,))
    result, pullback = jax.vjp(ssm_scan, values, spaced, in_seq, out_seq, rates)
    grad_values, grad_spacing, grad_in, grad_out_map, grad_rates = pullback(cot_seq)
    grad_pre = grad_spacing.reshape(-1, inner) * jax.nn.sigmoid(spacing_pre)
    grad_bias = jnp.sum(grad_pre, axis=0)
    grad_pre_b = grad_pre.astype(jnp.bfloat16)
    grad_dt = lax.dot_general(
        grad_pre_b, low_rank, (((0,), (0,)), ((), ())), preferred_element_type=jnp.float32
    )
    grad_low = jnp.dot(grad_pre_b, w_dt, preferred_element_type=jnp.float32)
    grad_select_out = jnp.concatenate(
        [grad_low, grad_in.reshape(-1, states), grad_out_map.reshape(-1, states)], axis=1
    ).astype(jnp.bfloat16)
    grad_select = lax.dot_general(
        flat, grad_select_out, (((0,), (0,)), ((), ())), preferred_element_type=jnp.float32
    )
    grad_flat = grad_values.reshape(-1, inner) + lax.dot_general(
        grad_select_out, w_select, (((1,), (1,)), ((), ())), preferred_element_type=jnp.float32
    )
    grad_alog = (grad_rates * rates).T
    return (
        restore(result.astype(jnp.bfloat16), shape),
        restore(grad_flat.astype(jnp.bfloat16), shape),
        (grad_select, grad_dt, grad_bias, grad_alog),
    )


def local(
    latent,
    out_grad,
    w_in,
    w_out,
    w_select,
    w_dt,
    dt_bias,
    a_log,
    d_skip,
    w_mod,
    t_index,
    frame_order,
    row_order,
    col_order,
):
    frames, rows, cols, width = latent.shape
    inner = w_in.shape[1]
    features = jax.nn.silu(time_features(t_index, w_mod.shape[1])).astype(jnp.bfloat16)
    modulation = jnp.dot(w_mod, features, preferred_element_type=jnp.float32)
    scale_vec = modulation[width:]
    normed, inverse, shifted = modulate(latent, modulation[:width], scale_vec)
    shifted_flat = shifted.reshape(-1, width)
    pre_act = jnp.dot(shifted_flat, w_in, preferred_element_type=jnp.float32)
    activ_flat = jax.nn.silu(pre_act).astype(jnp.bfloat16)
    activ = activ_flat.reshape(frames, rows, cols, inner)
    grad_flat = out_grad.reshape(-1, width)
    params = (w_select, w_dt, dt_bias, a_log)
    cot_flat = lax.dot_general(
        grad_flat, w_out, (((1,), (1,)), ((), ())), preferred_element_type=jnp.float32
    ).astype(jnp.bfloat16)
    cot = cot_flat.reshape(frames, rows, cols, inner)
    mixed_time, back_time, grads_time = direction_pass(activ, cot, params, 0, frame_order)
    wide_in, wide_cot = (
        lax.all_to_all(activ, "col", split_axis=0, concat_axis=2, tiled=True),
        lax.all_to_all(cot, "col", split_axis=0, concat_axis=2, tiled=True),
    )
    part_wide, back_part_wide, grads_wide = direction_pass(wide_in, wide_cot, params, 2, col_order)
    mixed_wide, back_wide = (
        lax.all_to_all(part_wide, "col", split_axis=2, concat_axis=0, tiled=True),
        lax.all_to_all(back_part_wide, "col", split_axis=2, concat_axis=0, tiled=True),
    )
    tall_in, tall_cot = (
        lax.all_to_all(activ, "row", split_axis=0, concat_axis=1, tiled=True),
        lax.all_to_all(cot, "row", split_axis=0, concat_axis=1, tiled=True),
    )
    part_tall, back_part_tall, grads_tall = direction_pass(tall_in, tall_cot, params, 1, row_order)
    mixed_tall, back_tall = (
        lax.all_to_all(part_tall, "row", split_axis=1, concat_axis=0, tiled=True),
        lax.all_to_all(back_part_tall, "row", split_axis=1, concat_axis=0, tiled=True),
    )
    activ_wide = activ_flat.astype(jnp.float32)
    mixed_sum = (
        mixed_time.astype(jnp.float32)
        + mixed_tall.astype(jnp.float32)
        + mixed_wide.astype(jnp.float32)
    ).reshape(-1, inner) + d_skip * activ_wide
    mixed_flat = mixed_sum.astype(jnp.bfloat16)
    branch_out = (
        jnp.dot(mixed_flat, w_out, preferred_element_type=jnp.float32)
        .astype(jnp.bfloat16)
        .reshape(latent.shape)
    )
    grad_w_out = lax.dot_general(
        mixed_flat, grad_flat, (((0,), (0,)), ((), ())), preferred_element_type=jnp.float32
    )
    cot_wide = cot_flat.astype(jnp.float32)
    grad_d_skip = jnp.sum(cot_wide * activ_wide, axis=0)
    back_sum = (
        back_time.astype(jnp.float32)
        + back_tall.astype(jnp.float32)
        + back_wide.astype(jnp.float32)
    ).reshape(-1, inner) + d_skip * cot_wide
    sigmoid_pre = jax.nn.sigmoid(pre_act)
    grad_act = (back_sum * sigmoid_pre * (1.0 + pre_act * (1.0 - sigmoid_pre))).astype(jnp.bfloat16)
    grad_w_in = lax.dot_general(
        shifted_flat, grad_act, (((0,), (0,)), ((), ())), preferred_element_type=jnp.float32
    )
    grad_shifted = lax.dot_general(
        grad_act, w_in, (((1,), (1,)), ((), ())), preferred_element_type=jnp.float32
    )
    normed_flat = normed.reshape(-1, width)
    inverse_flat = inverse.reshape(-1, 1)
    grad_normed = grad_shifted * (1.0 + scale_vec)
    latent_grad = (
        (
            inverse_flat
            * (
                grad_normed
                - normed_flat * jnp.mean(grad_normed * normed_flat, axis=1, keepdims=True)
            )
        )
        .astype(jnp.bfloat16)
        .reshape(latent.shape)
    )
    grad_mod_vec = jnp.concatenate(
        [jnp.sum(grad_shifted, axis=0), jnp.sum(grad_shifted * normed_flat, axis=0)]
    )
    summed = jax.tree.map(
        lambda first, second, third: first + second + third, grads_time, grads_tall, grads_wide
    )
    grad_select, grad_dt, grad_bias, grad_alog = summed
    final_grads = (
        lax.psum_scatter(grad_w_in, ("row", "col"), scatter_dimension=0, tiled=True),
        lax.psum_scatter(grad_w_out, ("row", "col"), scatter_dimension=0, tiled=True),
        lax.psum_scatter(grad_select, ("row", "col"), scatter_dimension=0, tiled=True),
        lax.psum_scatter(grad_dt, ("row", "col"), scatter_dimension=0, tiled=True),
        lax.psum_scatter(grad_bias, ("row", "col"), scatter_dimension=0, tiled=True),
        lax.psum_scatter(grad_alog, ("row", "col"), scatter_dimension=0, tiled=True),
        lax.psum_scatter(grad_d_skip, ("row", "col"), scatter_dimension=0, tiled=True),
        lax.psum_scatter(grad_mod_vec, ("row", "col"), scatter_dimension=0, tiled=True),
    )
    mod_rows = final_grads[7][:, None] * features.astype(jnp.float32)[None, :]
    return (branch_out, latent_grad) + tuple(final_grads[:7]) + (mod_rows,)


def solution(mesh):
    return jax.shard_map(
        local,
        mesh=mesh,
        in_specs=(
            P(None, "row", "col", None),
            P(None, "row", "col", None),
            P(),
            P(),
            P(),
            P(),
            P(),
            P(),
            P(),
            P(),
            P(),
            P(),
            P(),
            P(),
        ),
        out_specs=(
            P(None, "row", "col", None),
            P(None, "row", "col", None),
            P(("row", "col"), None),
            P(("row", "col"), None),
            P(("row", "col"), None),
            P(("row", "col"), None),
            P(("row", "col")),
            P(("row", "col"), None),
            P(("row", "col")),
            P(("row", "col"), None),
        ),
        check_vma=False,
    )
```

profile of v0, /device:TPU:1, one launch (start us, length us, event | category | flops | bytes accessed | tf_op | source)
XLA Modules:
  0.0 1827.8 jit_solution(1241527394648825882)
XLA Ops:
  37.8 37.4 %while.80 = (s32[]{:T(128)}, f32[4,16,1536]{2,1,0:T(8,128)S(1)}, bf16[4,8,4,1536]{3,2,1,0:T(4,128)(2,1)}, f32[4,8,4,16,1536]{4,3,2,1,0:T(8,128)}, f32[4,8,4,1536...) while((s32[]{:T(128)}, f32[4,16,1536]{2,1,0:T(8,128)S(1)}, ...), condition=%wide.region_10.12_spmd.clone, body=%wide.region_1.11_spmd.clone.sunk | while | flops 12681225 | bytes 18482436 | solution.py:34
  80.0 82.4 %while.82 = (s32[]{:T(128)}, f32[16,1536]{1,0:T(8,128)}, f32[4,16,1536]{2,1,0:T(8,128)}, f32[4,8,4,1536]{3,2,1,0:T(4,128)}, f32[4,8,4,1536]{3,2,1,0:T(4,128)}, /...) while((s32[]{:T(128)}, f32[16,1536]{1,0:T(8,128)}, ...), condition=%wide.region_73.77_spmd.clone, body=%wide.region_32.76_spmd.clone.sunk | while | flops 15162377 | bytes 34088564 | solution.py:34
  180.9 11.1 all-to-all-start.6
  373.4 9.4 all-to-all-start.2
  385.0 7.9 all-to-all-done.2
  411.4 44.4 %while.81 = (s32[]{:T(128)}, f32[2,16,1536]{2,1,0:T(8,128)S(1)}, bf16[8,8,2,1536]{3,2,1,0:T(2,128)(2,1)}, f32[8,8,2,16,1536]{4,3,2,1,0:T(8,128)}, f32[8,8,2,1536...) while((s32[]{:T(128)}, f32[2,16,1536]{2,1,0:T(8,128)S(1)}, ...), condition=%wide.region_30.34_spmd.clone, body=%wide.region_21.33_spmd.clone.sunk | while | flops 4964361 | bytes 9898359 | solution.py:34
  459.4 104.0 %while.83 = (s32[]{:T(128)}, f32[16,1536]{1,0:T(8,128)S(1)}, f32[2,16,1536]{2,1,0:T(8,128)S(1)}, f32[8,8,2,1536]{3,2,1,0:T(2,128)}, f32[8,8,2,1536]{3,2,1,0:T(2,...) while((s32[]{:T(128)}, f32[16,1536]{1,0:T(8,128)S(1)}, ...), condition=%wide.region_147.151_spmd.clone, body=%wide.region_106.150_spmd.clone.sunk | while | flops 7593481 | bytes 13899596 | solution.py:34
  608.1 8.6 all-to-all-done.3
  638.4 392.6 %fusion.197 = (f32[16,1536]{1,0:T(8,128)S(1)}, f32[16,1536]{1,0:T(8,128)S(1)}, f32[16,128]{1,0:T(8,128)S(1)}, f32[16,96]{1,0:T(8,128)S(1)}, f32[16,16]{1,0:T(8,128)S(1)}) fusion(f32[1536,1536]{1,0:T(8,128)} %fusion.214, f32[1536,1536]{1,0:T(8,128)} %fusion.215, f32[1536,128]{1,0:T(8,128)S(1)} %copy-done.42, f32[1536,96]{1,0:T(8,128)S(1)} %copy-done.43, ...), kind=kCustom, calls=%all-reduce-scatter.5 | all-reduce-scatter fusion | flops 6782977 | bytes 20560896
  1034.1 12.6 collective-permute-start.157
  1061.9 7.7 collective-permute-start.154
  1069.6 13.7 collective-permute-start.153
  1083.3 7.7 collective-permute-start.152
  1165.1 8.8 collective-permute-done.128
  1336.3 7.4 collective-permute-done.69
  1345.7 9.1 collective-permute-done.68
  1374.7 9.1 collective-permute-done.65
  1385.7 8.8 collective-permute-done.64
  1491.6 68.6 %all-reduce.13 = (f32[1536]{0:T(1024)S(1)}, f32[1536]{0:T(1024)S(1)}, f32[3072]{0:T(1024)S(1)}) all-reduce(f32[1536]{0:T(1024)S(1)} %add_add_fusion, f32[1536]{0:T(1024)S(1)} %copy-done.302, f32[3072]{0:T(1024)S(1)} %pad_maximum_fusion.9), channel_id=6, replica_groups=mesh['row'=4,'col'=32] {'row','col'}, use_global_device_ids=true, to_apply=%region_156.160.clone | all-reduce | flops 6144 | bytes 49152
  1583.7 24.6 %concatenate.178 = f32[524,16]{1,0:T(8,128)S(1)} concatenate(f32[12,16]{1,0:T(8,128)} %copy-done.249, f32[16,16]{1,0:T(8,128)} %copy-done.247, f32[16,16]{1,0:T(8,128)} %copy-done.248, f32[16,16]{1,0:T(8,128)} %copy-done.250, f32[16,16]{1,0:T(8,128)} %copy-done.251, f32[16,16]{1,0:T(8,128)} %copy-done.252, f32[16,16]{1,0:T(8,128)} %copy-done.253, f32[16,16]{1,0:T(8,128)} %copy-done.254, ...), dimensions={0} | concatenate | bytes 67072
  1619.9 24.6 %concatenate.177 = f32[524,96]{1,0:T(8,128)S(1)} concatenate(f32[12,96]{1,0:T(8,128)} %copy-done.264, f32[16,96]{1,0:T(8,128)} %copy-done.275, f32[16,96]{1,0:T(8,128)} %copy-done.277, f32[16,96]{1,0:T(8,128)} %copy-done.280, f32[16,96]{1,0:T(8,128)} %copy-done.282, f32[16,96]{1,0:T(8,128)} %copy-done.284, f32[16,96]{1,0:T(8,128)} %copy-done.285, f32[16,96]{1,0:T(8,128)} %copy-done.286, ...), dimensions={0} | concatenate | bytes 402432
  1659.8 24.6 %concatenate.176 = f32[524,128]{1,0:T(8,128)S(1)} concatenate(f32[12,128]{1,0:T(8,128)} %copy-done.262, f32[16,128]{1,0:T(8,128)} %collective-permute-done.94, f32[16,128]{1,0:T(8,128)} %collective-permute-done.93, f32[16,128]{1,0:T(8,128)} %collective-permute-done.92, f32[16,128]{1,0:T(8,128)} %collective-permute-done.91, f32[16,128]{1,0:T(8,128)} %collective-permute-done.90, ...), dimensions={0} | concatenate | bytes 536576
  1699.5 50.2 %concatenate.174 = f32[524,1536]{1,0:T(8,128)} concatenate(f32[12,1536]{1,0:T(8,128)S(1)} %collective-permute-done.31, f32[16,1536]{1,0:T(8,128)S(1)} %collective-permute-done.30, f32[16,1536]{1,0:T(8,128)S(1)} %collective-permute-done.29, f32[16,1536]{1,0:T(8,128)S(1)} %collective-permute-done.28, f32[16,1536]{1,0:T(8,128)S(1)} %collective-permute-done.27, ...), dimensions={0} | concatenate | bytes 6438912
  1774.2 51.8 %concatenate.175 = f32[524,1536]{1,0:T(8,128)} concatenate(f32[12,1536]{1,0:T(8,128)S(1)} %collective-permute-done.63, f32[16,1536]{1,0:T(8,128)S(1)} %copy-done.190, f32[16,1536]{1,0:T(8,128)S(1)} %copy-done.196, f32[16,1536]{1,0:T(8,128)} %copy-done.198, f32[16,1536]{1,0:T(8,128)} %copy-done.200, f32[16,1536]{1,0:T(8,128)} %copy-done.201, f32[16,1536]{1,0:T(8,128)} %copy-done.203, ...), dimensions={0} | concatenate | bytes 6438912
  (2696 shorter events, 1053.5 us)
Async XLA Ops:
  13.2 157.6 %all-to-all-start.4 = ((bf16[32,2,2,1536]{3,2,1,0:T(2,128)(2,1)}), bf16[32,2,2,1536]{3,2,1,0:T(2,128)(2,1)}, u32[]{:S(2)}, u32[]{:S(2)}) async-start(bf16[32,2,2,1536]{3,2,1,0:T(2,128)(2,1)} %reshape.1461), calls=%async_computation.4 | async-start | bytes 786432 | tf_op jit(solution)/shard_map/all_to_all | solution.py:148
  180.9 192.5 %all-to-all-start.6 = ((bf16[32,2,2,1536]{3,2,1,0:T(2,128)(2,1)}), bf16[32,2,2,1536]{3,2,1,0:T(2,128)(2,1)}, u32[]{:S(2)}, u32[]{:S(2)}) async-start(bf16[32,2,2,1536]{3,2,1,0:T(2,128)(2,1)} %reshape.1461), calls=%async_computation.6 | async-start | bytes 786432 | tf_op jit(solution)/shard_map/all_to_all | solution.py:139
  392.9 183.8 %all-to-all-start.5 = ((bf16[8,8,2,1536]{3,2,0,1:T(2,128)(2,1)}), bf16[8,8,2,1536]{3,2,0,1:T(2,128)(2,1)}, u32[]{:S(2)}, u32[]{:S(2)}) async-start(bf16[8,8,2,1536]{3,2,0,1:T(2,128)(2,1)} %fusion.176), calls=%async_computation.5 | async-start | bytes 786432 | tf_op jit(solution)/shard_map/all_to_all | solution.py:153
  1034.1 49.2 %collective-permute-start.157 = (f32[16,16]{1,0:T(8,128)S(1)}, f32[16,16]{1,0:T(8,128)S(1)}, u32[]{:S(2)}, u32[]{:S(2)}) collective-permute-start(f32[16,16]{1,0:T(8,128)S(1)} %get-tuple-element.1692), channel_id=1, source_target_pairs={{0,30},{1,31},{2,32},{3,33},{4,34},{5,35},{6,36},{7,37},{8,38},{9,... | collective-permute-start | bytes 3080
  1048.7 42.3 %collective-permute-start.156 = (f32[16,16]{1,0:T(8,128)S(1)}, f32[16,16]{1,0:T(8,128)S(1)}, u32[]{:S(2)}, u32[]{:S(2)}) collective-permute-start(f32[16,16]{1,0:T(8,128)S(1)} %get-tuple-element.1692), channel_id=1, source_target_pairs={{0,29},{1,30},{2,31},{3,32},{4,33},{5,34},{6,35},{7,36},{8,37},{9,... | collective-permute-start | bytes 3080
  1126.9 49.0 %collective-permute-start.127 = (f32[12,96]{1,0:T(8,128)S(1)}, f32[12,96]{1,0:T(8,128)S(1)}, u32[]{:S(2)}, u32[]{:S(2)}) collective-permute-start(f32[12,96]{1,0:T(8,128)S(1)} %slice.1741), channel_id=1, source_target_pairs={{0,32},{1,33},{2,34},{3,35},{4,36},{5,37},{6,38},{7,39},{8,40},{9,... | collective-permute-start | bytes 13832
  1281.5 118.9 %collective-permute-start.30 = (f32[16,1536]{1,0:T(8,128)S(1)}, f32[16,1536]{1,0:T(8,128)S(1)}, u32[]{:S(2)}, u32[]{:S(2)}) collective-permute-start(f32[16,1536]{1,0:T(8,128)S(1)} %get-tuple-element.1688), channel_id=1, source_target_pairs={{0,31},{1,32},{2,33},{3,34},{4,35},{5,36},{6,37},{7,38},{8,39},{9,... | collective-permute-start | bytes 294920
  1283.4 118.9 %collective-permute-start.29 = (f32[16,1536]{1,0:T(8,128)S(1)}, f32[16,1536]{1,0:T(8,128)S(1)}, u32[]{:S(2)}, u32[]{:S(2)}) collective-permute-start(f32[16,1536]{1,0:T(8,128)S(1)} %get-tuple-element.1688), channel_id=1, source_target_pairs={{0,30},{1,31},{2,32},{3,33},{4,34},{5,35},{6,36},{7,37},{8,38},{9,... | collective-permute-start | bytes 294920
  1307.0 89.5 %collective-permute-start.31 = (f32[12,1536]{1,0:T(8,128)S(1)}, f32[12,1536]{1,0:T(8,128)S(1)}, u32[]{:S(2)}, u32[]{:S(2)}) collective-permute-start(f32[12,1536]{1,0:T(8,128)S(1)} %slice.1738), channel_id=1, source_target_pairs={{0,32},{1,33},{2,34},{3,35},{4,36},{5,37},{6,38},{7,39},{8,40},{9,... | collective-permute-start | bytes 221192
  1311.9 86.5 %collective-permute-start.63 = (f32[12,1536]{1,0:T(8,128)S(1)}, f32[12,1536]{1,0:T(8,128)S(1)}, u32[]{:S(2)}, u32[]{:S(2)}) collective-permute-start(f32[12,1536]{1,0:T(8,128)S(1)} %slice.1739), channel_id=1, source_target_pairs={{0,32},{1,33},{2,34},{3,35},{4,36},{5,37},{6,38},{7,39},{8,40},{9,... | collective-permute-start | bytes 221192
  1479.9 80.5 %collective-permute-start.61 = (f32[16,1536]{1,0:T(8,128)S(1)}, f32[16,1536]{1,0:T(8,128)S(1)}, u32[]{:S(2)}, u32[]{:S(2)}) collective-permute-start(f32[16,1536]{1,0:T(8,128)S(1)} %get-tuple-element.1689), channel_id=1, source_target_pairs={{0,30},{1,31},{2,32},{3,33},{4,34},{5,35},{6,36},{7,37},{8,38},{9,... | collective-permute-start | bytes 294920
  1482.1 81.6 %collective-permute-start.60 = (f32[16,1536]{1,0:T(8,128)S(1)}, f32[16,1536]{1,0:T(8,128)S(1)}, u32[]{:S(2)}, u32[]{:S(2)}) collective-permute-start(f32[16,1536]{1,0:T(8,128)S(1)} %get-tuple-element.1689), channel_id=1, source_target_pairs={{0,29},{1,30},{2,31},{3,32},{4,33},{5,34},{6,35},{7,36},{8,37},{9,... | collective-permute-start | bytes 294920
  1484.5 85.8 %collective-permute-start.59 = (f32[16,1536]{1,0:T(8,128)S(1)}, f32[16,1536]{1,0:T(8,128)S(1)}, u32[]{:S(2)}, u32[]{:S(2)}) collective-permute-start(f32[16,1536]{1,0:T(8,128)S(1)} %get-tuple-element.1689), channel_id=1, source_target_pairs={{0,28},{1,29},{2,30},{3,31},{4,32},{5,33},{6,34},{7,35},{8,36},{9,... | collective-permute-start | bytes 294920
  1486.5 85.8 %collective-permute-start.58 = (f32[16,1536]{1,0:T(8,128)S(1)}, f32[16,1536]{1,0:T(8,128)S(1)}, u32[]{:S(2)}, u32[]{:S(2)}) collective-permute-start(f32[16,1536]{1,0:T(8,128)S(1)} %get-tuple-element.1689), channel_id=1, source_target_pairs={{0,27},{1,28},{2,29},{3,30},{4,31},{5,32},{6,33},{7,34},{8,35},{9,... | collective-permute-start | bytes 294920
  1489.6 88.4 %collective-permute-start.57 = (f32[16,1536]{1,0:T(8,128)S(1)}, f32[16,1536]{1,0:T(8,128)S(1)}, u32[]{:S(2)}, u32[]{:S(2)}) collective-permute-start(f32[16,1536]{1,0:T(8,128)S(1)} %get-tuple-element.1689), channel_id=1, source_target_pairs={{0,26},{1,27},{2,28},{3,29},{4,30},{5,31},{6,32},{7,33},{8,34},{9,... | collective-permute-start | bytes 294920
  1560.3 48.0 %collective-permute-start.56 = (f32[16,1536]{1,0:T(8,128)S(1)}, f32[16,1536]{1,0:T(8,128)}, u32[]{:S(2)}, u32[]{:S(2)}) collective-permute-start(f32[16,1536]{1,0:T(8,128)S(1)} %get-tuple-element.1689), channel_id=1, source_target_pairs={{0,25},{1,26},{2,27},{3,28},{4,29},{5,30},{6,31},{7,32},{8,33},{9,... | collective-permute-start | bytes 294920
  1563.8 46.5 %collective-permute-start.55 = (f32[16,1536]{1,0:T(8,128)S(1)}, f32[16,1536]{1,0:T(8,128)}, u32[]{:S(2)}, u32[]{:S(2)}) collective-permute-start(f32[16,1536]{1,0:T(8,128)S(1)} %get-tuple-element.1689), channel_id=1, source_target_pairs={{0,24},{1,25},{2,26},{3,27},{4,28},{5,29},{6,30},{7,31},{8,32},{9,... | collective-permute-start | bytes 294920
  1570.3 42.9 %collective-permute-start.54 = (f32[16,1536]{1,0:T(8,128)S(1)}, f32[16,1536]{1,0:T(8,128)}, u32[]{:S(2)}, u32[]{:S(2)}) collective-permute-start(f32[16,1536]{1,0:T(8,128)S(1)} %get-tuple-element.1689), channel_id=1, source_target_pairs={{0,23},{1,24},{2,25},{3,26},{4,27},{5,28},{6,29},{7,30},{8,31},{9,... | collective-permute-start | bytes 294920
  1572.3 42.9 %collective-permute-start.53 = (f32[16,1536]{1,0:T(8,128)S(1)}, f32[16,1536]{1,0:T(8,128)}, u32[]{:S(2)}, u32[]{:S(2)}) collective-permute-start(f32[16,1536]{1,0:T(8,128)S(1)} %get-tuple-element.1689), channel_id=1, source_target_pairs={{0,22},{1,23},{2,24},{3,25},{4,26},{5,27},{6,28},{7,29},{8,30},{9,... | collective-permute-start | bytes 294920
  1684.4 65.3 %collective-permute-start.41 = (f32[16,1536]{1,0:T(8,128)S(1)}, f32[16,1536]{1,0:T(8,128)}, u32[]{:S(2)}, u32[]{:S(2)}) collective-permute-start(f32[16,1536]{1,0:T(8,128)S(1)} %get-tuple-element.1689), channel_id=1, source_target_pairs={{0,10},{1,11},{2,12},{3,13},{4,14},{5,15},{6,16},{7,17},{8,18},{9,... | collective-permute-start | bytes 294920
  1686.6 65.1 %collective-permute-start.40 = (f32[16,1536]{1,0:T(8,128)S(1)}, f32[16,1536]{1,0:T(8,128)}, u32[]{:S(2)}, u32[]{:S(2)}) collective-permute-start(f32[16,1536]{1,0:T(8,128)S(1)} %get-tuple-element.1689), channel_id=1, source_target_pairs={{0,9},{1,10},{2,11},{3,12},{4,13},{5,14},{6,15},{7,16},{8,17},{9,1... | collective-permute-start | bytes 294920
  1689.0 66.1 %collective-permute-start.39 = (f32[16,1536]{1,0:T(8,128)S(1)}, f32[16,1536]{1,0:T(8,128)}, u32[]{:S(2)}, u32[]{:S(2)}) collective-permute-start(f32[16,1536]{1,0:T(8,128)S(1)} %get-tuple-element.1689), channel_id=1, source_target_pairs={{0,8},{1,9},{2,10},{3,11},{4,12},{5,13},{6,14},{7,15},{8,16},{9,17... | collective-permute-start | bytes 294920
  1692.6 67.5 %collective-permute-start.38 = (f32[16,1536]{1,0:T(8,128)S(1)}, f32[16,1536]{1,0:T(8,128)}, u32[]{:S(2)}, u32[]{:S(2)}) collective-permute-start(f32[16,1536]{1,0:T(8,128)S(1)} %get-tuple-element.1689), channel_id=1, source_target_pairs={{0,7},{1,8},{2,9},{3,10},{4,11},{5,12},{6,13},{7,14},{8,15},{9,16}... | collective-permute-start | bytes 294920
  1695.0 67.5 %collective-permute-start.37 = (f32[16,1536]{1,0:T(8,128)S(1)}, f32[16,1536]{1,0:T(8,128)}, u32[]{:S(2)}, u32[]{:S(2)}) collective-permute-start(f32[16,1536]{1,0:T(8,128)S(1)} %get-tuple-element.1689), channel_id=1, source_target_pairs={{0,6},{1,7},{2,8},{3,9},{4,10},{5,11},{6,12},{7,13},{8,14},{9,15},... | collective-permute-start | bytes 294920
  (748 other events, 18757.2 us)
where the time goes:
time: 1860 us; the launch traced here: 1830 us
  local copies, waits for them, and re-layouts  494 us (27%)
  starting transfers between devices  487 us (26%)
  blocking collectives  461 us (25%)
  other arithmetic  204 us (11%)
  waiting for transfers between devices  127 us (7%)
  matrix products  39.4 us (2%)
    unnamed x2, blocking collectives  461 us
    unnamed x160, starting transfers between devices  438 us
    unnamed x559, local copies, waits for them, and re-layouts  196 us
    squeeze x80, local copies, waits for them, and re-layouts, ssm_scan(): lax.scan(jax.checkpoint(advance), start, (values, spacing, input_map, out...  99.5 us
    reduce_sum x104, other arithmetic, advance(): space_t[:, None, :] * rates  94.4 us
    unnamed x160, waiting for transfers between devices  93.3 us
    dynamic_update_slice x48, local copies, waits for them, and re-layouts, ssm_scan(): lax.scan(jax.checkpoint(advance), start, (values, spacing, input_map, out...  42.3 us
  transfers between devices with their start and end apart: 168, of which 23 were waited for; matrix products, arithmetic and copies ran while one was open for 35% of the time, Pallas kernels for 0%

commit v1 on v0

v1 whole, which is shorter than its diff:
```python
import functools
import math

import jax
import jax.numpy as jnp
from jax import lax
from jax.experimental import pallas as pl
from jax.experimental.pallas import tpu as pltpu
from jax.sharding import Mesh
from jax.sharding import PartitionSpec as P

BF = jnp.bfloat16
F32 = jnp.float32
LANES = 128
GROUP = 4
LOG2E = math.log2(math.e)
MEGA = 1024 * 1024
AXES = ("xl", "core", "xh", "y", "z")
ROW = ("xl", "core")
COL = ("xh", "y", "z")
NEAR = ("y", "z")
FAR = ("xl", "core", "xh")
NT = (((1,), (1,)), ((), ()))
TN = (((0,), (0,)), ((), ()))


def time_features(step_index, width):
    halfway = width // 2
    frequency = jnp.exp(-math.log(10000.0) * jnp.arange(halfway, dtype=jnp.float32) / halfway)
    angles = step_index.astype(jnp.float32)[0] * frequency
    return jnp.concatenate([jnp.cos(angles), jnp.sin(angles)])


def total(terms):
    return functools.reduce(lambda a, b: a + b, terms)


def call(kernel, name, out_shape, scratch, vmem, args, smem=()):
    spaces = [
        pl.BlockSpec(memory_space=pltpu.SMEM if i in smem else pltpu.VMEM) for i in range(len(args))
    ]
    return pl.pallas_call(
        kernel,
        out_shape=tuple(jax.ShapeDtypeStruct(s, d) for s, d in out_shape),
        in_specs=spaces,
        out_specs=(pl.BlockSpec(memory_space=pltpu.VMEM),) * len(out_shape),
        scratch_shapes=[pltpu.VMEM(s, d) for s, d in scratch],
        compiler_params=pltpu.CompilerParams(vmem_limit_bytes=vmem * MEGA),
        name=name,
    )(*args)


def cut(j):
    return slice(LANES * j, LANES * j + LANES)


def to_flat(ref, j, value, tiles):
    ref[pl.ds(j, value.shape[0], stride=tiles), :] = value


def from_flat(ref, j, tokens, tiles):
    return ref[pl.ds(j, tokens, stride=tiles), :]


def normalise(latent):
    wide = latent.astype(F32)
    inverse = lax.rsqrt(jnp.mean(wide * wide, axis=-1, keepdims=True) + 1e-06)
    return wide * inverse, inverse


def pre_kernel(
    latent_ref,
    grad_ref,
    w_in_ref,
    w_out_ref,
    w_mod_ref,
    feature_ref,
    own_ref,
    tall_ref,
    wide_ref,
    shifted_ref,
    pre_ref,
    mod_ref,
    flat_ref,
):
    tokens, width = latent_ref.shape
    tiles = w_in_ref.shape[1] // LANES
    modulation = lax.dot_general(
        feature_ref[...], w_mod_ref[...], NT, preferred_element_type=F32
    )
    mod_ref[...] = modulation
    normed, _ = normalise(latent_ref[...])
    shifted = (normed * (1.0 + modulation[:1, width:]) + modulation[:1, :width]).astype(BF)
    shifted_ref[...] = shifted
    pre_act = jnp.dot(shifted, w_in_ref[...], preferred_element_type=F32)
    pre_ref[...] = pre_act
    activ = (pre_act * jax.nn.sigmoid(pre_act)).astype(BF)
    cot = lax.dot_general(grad_ref[...], w_out_ref[...], NT, preferred_element_type=F32).astype(BF)
    for which, value in enumerate((activ, cot)):
        wide = value.astype(F32)
        for j in range(tiles):
            to_flat(flat_ref, j, wide[:, cut(j)], tiles)
        flat = flat_ref[...].astype(BF)
        for ref in (own_ref, tall_ref, wide_ref):
            parts = ref.shape[0]
            ref[:, which] = flat.reshape(parts, flat.shape[0] // parts, LANES)


def scan_kernel(
    length,
    row_of,
    order_ref,
    data_ref,
    wsel_ref,
    wdt_ref,
    bias_ref,
    alog_ref,
    sel_in_ref,
    dt_in_ref,
    vec_in_ref,
    out_ref,
    gsel_ref,
    gdt_ref,
    gvec_ref,
    pre_ref,
    dt_ref,
    xf_ref,
    x_row_ref,
    dt_row_ref,
    dx_row_ref,
    dy_row_ref,
    bb_ref,
    cb_ref,
    gb_ref,
    gc_ref,
    hist_ref,
    y8_ref,
    u8_ref,
    v8_ref,
    rate2_ref,
    rate_ref,
):
    tokens, inner = xf_ref.shape
    tiles = inner // LANES
    lines = tokens // length
    states = alog_ref.shape[0]
    rank = LANES - 2 * states
    flat_shape = (tokens * tiles, LANES)
    x_row_ref[...] = data_ref[:, 0].reshape(flat_shape).astype(F32)
    dy_row_ref[...] = data_ref[:, 1].reshape(flat_shape).astype(F32)
    for j in range(tiles):
        xf_ref[:, cut(j)] = from_flat(x_row_ref, j, tokens, tiles)
    x = xf_ref[...].astype(BF)
    select = jnp.dot(x, wsel_ref[...], preferred_element_type=F32)
    lane = lax.broadcasted_iota(jnp.int32, (tokens, LANES), 1)
    low = jnp.where(lane < rank, select, 0.0).astype(BF)
    pre = lax.dot_general(low, wdt_ref[...], NT, preferred_element_type=F32) + bias_ref[...]
    pre_ref[...] = pre
    spacing = jnp.maximum(pre, 0.0) + jnp.log1p(jnp.exp(-jnp.abs(pre)))
    dt_ref[...] = spacing
    for j in range(tiles):
        to_flat(dt_row_ref, j, spacing[:, cut(j)], tiles)
    dx_row_ref[...] = dt_row_ref[...] * x_row_ref[...]
    rates = -jnp.exp(alog_ref[...])
    rate_ref[...] = rates
    rate2_ref[...] = rates * LOG2E
    turned = select.T
    for token in range(tokens):
        at = pl.ds(token * states, states)
        column = slice(token, token + 1)
        bb_ref[at, :] = jnp.broadcast_to(turned[rank : rank + states, column], (states, LANES))
        cb_ref[at, :] = jnp.broadcast_to(turned[rank + states :, column], (states, LANES))
    gb_ref[...] = jnp.zeros_like(gb_ref)
    gc_ref[...] = jnp.zeros_like(gc_ref)
    zero = jnp.zeros((states, LANES), F32)
    hist_ref[pl.ds(0, states), :] = jnp.zeros((states, GROUP * LANES), F32)
    unroll = min(length, 8)

    def fold(value):
        return value[:8] + value[8:]

    for group in range(tiles // GROUP):
        first = group * GROUP
        cuts = [cut(first + j) for j in range(GROUP)]
        rate2 = [rate2_ref[:, c] for c in cuts]
        rate1 = [rate_ref[:, c] for c in cuts]

        def one_line(line, grads):
            def places(step):
                row = row_of(order_ref[step], line)
                at = pl.ds(pl.multiple_of(row * states, states), states)
                slot = pl.ds(pl.multiple_of((step + 1) * states, states), states)
                return row * tiles + first, pl.multiple_of(row * 8, 8), at, slot

            def forward(step, carry):
                row, eight, at, slot = places(step)
                bb, cb = bb_ref[at, :], cb_ref[at, :]
                new = []
                for j in range(GROUP):
                    dt = dt_row_ref[pl.ds(row + j, 1), :]
                    dx = dx_row_ref[pl.ds(row + j, 1), :]
                    h = jnp.exp2(rate2[j] * dt) * carry[j] + bb * dx
                    hist_ref[slot, cut(j)] = h
                    y8_ref[pl.ds(eight + 8 * tokens * j, 8), :] = fold(h * cb)
                    new.append(h)
                return tuple(new)

            lax.fori_loop(0, length, forward, (zero,) * GROUP, unroll=unroll)

            def backward(back_step, carry):
                step = length - 1 - back_step
                row, eight, at, slot = places(step)
                prev = pl.ds(pl.multiple_of(step * states, states), states)
                bb, cb = bb_ref[at, :], cb_ref[at, :]
                pend, acc = carry
                gb = gb_ref[at, :]
                gc = gc_ref[at, :]
                new, acc_new = [], []
                for j in range(GROUP):
                    dt = dt_row_ref[pl.ds(row + j, 1), :]
                    dx = dx_row_ref[pl.ds(row + j, 1), :]
                    dy = dy_row_ref[pl.ds(row + j, 1), :]
                    g = pend[j] + cb * dy
                    gc = gc + hist_ref[slot, cut(j)] * dy
                    u8_ref[pl.ds(eight + 8 * tokens * j, 8), :] = fold(g * bb)
                    gb = gb + g * dx
                    p = jnp.exp2(rate2[j] * dt) * g
                    w = p * hist_ref[prev, cut(j)]
                    v8_ref[pl.ds(eight + 8 * tokens * j, 8), :] = fold(w * rate1[j])
                    acc_new.append(acc[j] + w * dt)
                    new.append(p)
                gb_ref[at, :] = gb
                gc_ref[at, :] = gc
                return tuple(new), tuple(acc_new)

            start = ((zero,) * GROUP, grads)
            return lax.fori_loop(0, length, backward, start, unroll=unroll)[1]

        grads = lax.fori_loop(0, lines, one_line, (zero,) * GROUP)
        for j in range(GROUP):
            gvec_ref[:states, cuts[j]] = vec_in_ref[:states, cuts[j]] + grads[j] * rate1[j]

        def gather(block, carry):
            rows = pl.ds(pl.multiple_of(block * 8, 8), 8)

            def summed(ref, j):
                begin = block * 64 + 8 * tokens * j
                return total([ref[pl.ds(begin + r, 8, stride=8), :] for r in range(8)])

            for j in range(GROUP):
                c = cuts[j]
                u = summed(u8_ref, j)
                x_row_ref[pl.ds(block * 8 * tiles + first + j, 8, stride=tiles), :] = summed(y8_ref, j)
                grad_spacing = summed(v8_ref, j) + xf_ref[rows, c] * u
                pre_ref[rows, c] = grad_spacing * jax.nn.sigmoid(pre_ref[rows, c])
                dt_ref[rows, c] = dt_ref[rows, c] * u
            return carry

        lax.fori_loop(0, tokens // 8, gather, 0, unroll=2)

    out_shape = (out_ref.shape[0], out_ref.shape[2], LANES)
    out_ref[:, 0] = x_row_ref[...].astype(BF).reshape(out_shape)
    grad_pre = pre_ref[...]
    gvec_ref[states:, :] = vec_in_ref[states:, :]
    gvec_ref[states : states + 1, :] += jnp.sum(grad_pre, axis=0, keepdims=True)
    grad_pre_b = grad_pre.astype(BF)
    ones = jnp.ones((LANES, LANES), BF)

    def lane_total(ref):
        value = ref[...]
        top = value.astype(BF)
        rest = (value - top.astype(F32)).astype(BF)
        return jnp.dot(top, ones, preferred_element_type=F32) + jnp.dot(
            rest, ones, preferred_element_type=F32
        )

    shape = (tokens * states, LANES)
    state_at = lax.broadcasted_iota(jnp.int32, shape, 0) % states
    lane_at = lax.broadcasted_iota(jnp.int32, shape, 1)
    gb_ref[...] = jnp.where(lane_at == state_at + rank, lane_total(gb_ref), 0.0) + jnp.where(
        lane_at == state_at + rank + states, lane_total(gc_ref), 0.0
    )
    grad_maps = total([gb_ref[pl.ds(n, tokens, stride=states), :] for n in range(states)])
    grad_low = jnp.dot(grad_pre_b, wdt_ref[...], preferred_element_type=F32)
    grad_select_out = (grad_low + grad_maps).astype(BF)
    back = dt_ref[...] + lax.dot_general(
        grad_select_out, wsel_ref[...], NT, preferred_element_type=F32
    )
    for j in range(tiles):
        to_flat(x_row_ref, j, back[:, cut(j)], tiles)
    out_ref[:, 1] = x_row_ref[...].astype(BF).reshape(out_shape)
    gsel_ref[...] = sel_in_ref[...] + lax.dot_general(
        x, grad_select_out, TN, preferred_element_type=F32
    )
    gdt_ref[...] = dt_in_ref[...] + lax.dot_general(
        grad_pre_b, low, TN, preferred_element_type=F32
    )


def direction(name, length, row_of, order, data, params, grads):
    inner = params[0].shape[0]
    tiles = inner // LANES
    tokens = data.shape[0] * data.shape[2] // tiles
    states = params[3].shape[0]
    plane = ((tokens, inner), F32)
    flat = ((tokens * tiles, LANES), F32)
    maps = ((tokens * states, LANES), F32)
    eights = ((tokens * 8 * GROUP, LANES), F32)
    out, *grads = call(
        functools.partial(scan_kernel, length, row_of),
        name,
        [(data.shape, BF)] + [(g.shape, F32) for g in grads],
        [plane] * 3
        + [flat] * 4
        + [maps] * 4
        + [(((length + 1) * states, GROUP * LANES), F32)]
        + [eights] * 3
        + [((states, inner), F32)] * 2,
        40,
        (order, data, *params, *grads),
        smem=(0,),
    )
    return out, grads


def post_kernel(
    own_ref,
    time_ref,
    tall_ref,
    wide_ref,
    pre_ref,
    latent_ref,
    mod_ref,
    skip_ref,
    w_in_ref,
    w_out_ref,
    gsel_ref,
    gdt_ref,
    gvec_ref,
    branch_ref,
    latent_grad_ref,
    send_ref,
    sum_ref,
    own_row_ref,
    mixed_ref,
    back_ref,
    turned_ref,
    first_ref,
    second_ref,
):
    tokens, width = latent_ref.shape
    inner = w_in_ref.shape[1]
    tiles = inner // LANES
    flat_shape = (tokens * tiles, LANES)
    near, _, near_rows, _ = send_ref.shape
    far = inner // (near * 12)
    states = gvec_ref.shape[0] - 8
    rank = LANES - 2 * states
    grad_skip = []
    for which, target in ((0, mixed_ref), (1, back_ref)):
        sum_ref[...] = total(
            [ref[:, which].reshape(flat_shape).astype(F32) for ref in (time_ref, tall_ref, wide_ref)]
        )
        own_row_ref[which] = own_ref[0, which].astype(F32)
        for j in range(tiles):
            mine = own_row_ref[which, pl.ds(j, tokens, stride=tiles), :]
            target[:, cut(j)] = from_flat(sum_ref, j, tokens, tiles) + skip_ref[:, cut(j)] * mine
            if which:
                other = own_row_ref[0, pl.ds(j, tokens, stride=tiles), :]
                grad_skip.append(jnp.sum(mine * other, axis=0, keepdims=True))
    mixed = mixed_ref[...].astype(BF)
    branch_ref[...] = jnp.dot(mixed, w_out_ref[...], preferred_element_type=F32).astype(BF)
    pre_act = pre_ref[...]
    gate = jax.nn.sigmoid(pre_act)
    grad_act = (back_ref[...] * gate * (1.0 + pre_act * (1.0 - gate))).astype(BF)
    grad_shifted = lax.dot_general(grad_act, w_in_ref[...], NT, preferred_element_type=F32)
    normed, inverse = normalise(latent_ref[...])
    grad_normed = grad_shifted * (1.0 + mod_ref[:1, width:])
    product = jnp.mean(grad_normed * normed, axis=1, keepdims=True)
    latent_grad_ref[...] = (inverse * (grad_normed - normed * product)).astype(BF)
    grad_vec = jnp.concatenate(
        [
            jnp.sum(grad_shifted, axis=0, keepdims=True),
            jnp.sum(grad_shifted * normed, axis=0, keepdims=True),
        ],
        axis=1,
    )
    turned_ref[0] = mixed.astype(F32).T
    turned_ref[1] = grad_act.astype(F32).T
    turned_ref[2] = gsel_ref[...]
    row_at = lax.broadcasted_iota(jnp.int32, (LANES, 2 * width), 0)
    spread = jnp.broadcast_to(grad_vec, (LANES, 2 * width))
    first_ref[...] = jnp.where(row_at == LANES - 14, spread, 0.0).T
    second_ref[...] = jnp.where(row_at == LANES - 13, spread, 0.0).T
    at = lax.broadcasted_iota(jnp.int32, (LANES, inner), 0)
    skips = jnp.concatenate(grad_skip, axis=1)
    vectors = jnp.concatenate(
        [
            jnp.zeros((rank, inner), F32),
            gvec_ref[...],
            jnp.zeros((states - 8, inner), F32),
        ],
        axis=0,
    )
    vectors = vectors + jnp.where(at == rank + states + 1, jnp.broadcast_to(skips, at.shape), 0.0)
    turned_ref[3] = gdt_ref[...] + vectors.T
    for m in range(near):
        send_ref[m, 1] = turned_ref[1, pl.ds(m * near_rows, near_rows), :].astype(BF)
        for which in (0, 2, 3):
            pieces = []
            for i in range(12):
                piece = turned_ref[which, pl.ds(m * 12 + i, far, stride=near * 12), :]
                if which == 3:
                    begin = m * 24 + i
                    piece = (
                        piece
                        + first_ref[pl.ds(begin, far, stride=near * 24), :]
                        + second_ref[pl.ds(begin + 12, far, stride=near * 24), :]
                    )
                pieces.append(piece)
            send_ref[m, which] = jnp.concatenate(pieces, axis=0).astype(BF)


def middle_kernel(recv_ref, grad_ref, shifted_ref, send_ref, left_ref, out_ref, half_ref):
    near, _, rows, tokens = recv_ref.shape
    far = send_ref.shape[0]
    width = grad_ref.shape[1]
    tiles = width // LANES
    chunk = width // far
    own = rows // far
    for s in range(near):
        left_ref[:, cut(s)] = recv_ref[s, 0]
    product = jnp.dot(left_ref[...], grad_ref[...], preferred_element_type=F32)
    for j in range(tiles):
        half_ref[...] = product[:, cut(j)]
        for o in range(far):
            out_ref[o, pl.ds(j, own, stride=tiles), :] = half_ref[pl.ds(o, own, stride=far), :]
    base = own * tiles
    for which in (2, 3):
        half_ref[...] = total([recv_ref[s, which].astype(F32) for s in range(near)])
        for o in range(far):
            out_ref[o, pl.ds(base, own), :] = half_ref[pl.ds(o, own, stride=far), :]
        base += own
    for s in range(near):
        left_ref[:, cut(s)] = recv_ref[s, 1]
    product = jnp.dot(left_ref[...], shifted_ref[...], preferred_element_type=F32)
    turned = jnp.concatenate([product, jnp.zeros((LANES - rows, width), F32)], axis=0).T
    for o in range(far):
        out_ref[o, pl.ds(base, chunk), :] = turned[o * chunk : (o + 1) * chunk]
    base += chunk
    rest = out_ref.shape[1] - base
    for o in range(far):
        out_ref[o, pl.ds(base, rest), :] = jnp.zeros((rest, LANES), F32)
    send_ref[...] = out_ref[...].astype(BF)


def last_kernel(recv_ref, feature_ref, gwo_ref, gsel_ref, small_ref, gmod_ref, send_ref, sum_ref):
    far = recv_ref.shape[0]
    near = send_ref.shape[0]
    own, width = gwo_ref.shape
    tiles = width // LANES
    sum_ref[...] = total([recv_ref[o].astype(F32) for o in range(far)])
    for j in range(tiles):
        gwo_ref[:, cut(j)] = sum_ref[pl.ds(j, own, stride=tiles), :]
    base = own * tiles
    gsel_ref[...] = sum_ref[pl.ds(base, own), :]
    small = sum_ref[pl.ds(base + own, own), :]
    small_ref[...] = small
    features = feature_ref[:1, :].astype(F32)
    gmod_ref[:own, :] = small[:, LANES - 14 : LANES - 13] * features
    gmod_ref[own:, :] = small[:, LANES - 13 : LANES - 12] * features
    base += 2 * own
    for m in range(near):
        send_ref[m, :own] = sum_ref[pl.ds(base + m * own, own), :]
        send_ref[m, own:] = jnp.zeros((send_ref.shape[1] - own, LANES), F32)


def join_kernel(recv_ref, gwi_ref):
    near = recv_ref.shape[0]
    own, width = gwi_ref.shape
    part = width // near
    for m in range(near):
        gwi_ref[:, part * m : part * (m + 1)] = recv_ref[m, :own, :part]


def exchange(value, axes):
    return lax.all_to_all(value, axes, split_axis=0, concat_axis=0, tiled=True)


def local(
    latent,
    out_grad,
    w_in,
    w_out,
    w_select,
    w_dt,
    dt_bias,
    a_log,
    d_skip,
    w_mod,
    t_index,
    frame_order,
    row_order,
    col_order,
):
    frames, rows, cols, width = latent.shape
    inner = w_in.shape[1]
    tokens = frames * rows * cols
    tiles = inner // LANES
    states = a_log.shape[1]
    n_row, n_col = lax.axis_size(ROW), lax.axis_size(COL)
    near, far = lax.axis_size(NEAR), lax.axis_size(FAR)
    own = width // (near * far)
    flat_latent = latent.reshape(tokens, width)
    flat_grad = out_grad.reshape(tokens, width)
    features = jax.nn.silu(time_features(t_index, w_mod.shape[1])).astype(BF)
    feature_rows = jnp.broadcast_to(features[None, :], (8, features.shape[0]))

    def packed(parts):
        return ((parts, 2, tokens * tiles // parts, LANES), BF)

    grad_near = lax.all_gather(flat_grad, NEAR, axis=0, tiled=True)
    data_own, data_tall, data_wide, shifted, pre_act, modulation = call(
        pre_kernel,
        "norm_project",
        [
            packed(1),
            packed(n_row),
            packed(n_col),
            ((tokens, width), BF),
            ((tokens, inner), F32),
            ((8, 2 * width), F32),
        ],
        [((tokens * tiles, LANES), F32)],
        48,
        (flat_latent, flat_grad, w_in, w_out, w_mod, feature_rows),
    )
    data_wide = exchange(data_wide, COL)
    data_tall = exchange(data_tall, ROW)
    shifted_near = lax.all_gather(shifted, NEAR, axis=0, tiled=True)
    params = (
        w_select,
        jnp.pad(w_dt, ((0, 0), (0, LANES - w_dt.shape[1]))),
        dt_bias[None, :],
        a_log.T,
    )
    grads = [
        jnp.zeros((inner, LANES), F32),
        jnp.zeros((inner, LANES), F32),
        jnp.zeros((states + 8, inner), F32),
    ]
    area = rows * cols

    def time_row(at, line):
        return at * area + line

    def wide_row(at, line):
        chunk = frames // n_col * area
        return (
            lax.div(at, cols) * chunk
            + lax.rem(at, cols)
            + lax.div(line, rows) * area
            + lax.rem(line, rows) * cols
        )

    def tall_row(at, line):
        chunk = frames // n_row * area
        return (
            lax.div(at, rows) * chunk
            + lax.rem(at, rows) * cols
            + lax.div(line, cols) * area
            + lax.rem(line, cols)
        )

    out_time, grads = direction(
        "scan_time", frames, time_row, frame_order, data_own, params, grads
    )
    out_wide, grads = direction(
        "scan_width", cols * n_col, wide_row, col_order, data_wide, params, grads
    )
    out_wide = exchange(out_wide, COL)
    out_tall, grads = direction(
        "scan_height", rows * n_row, tall_row, row_order, data_tall, params, grads
    )
    out_tall = exchange(out_tall, ROW)
    branch, latent_grad, near_send = call(
        post_kernel,
        "sum_project",
        [
            ((tokens, width), BF),
            ((tokens, width), BF),
            ((near, 4, inner // near, LANES), BF),
        ],
        [
            ((tokens * tiles, LANES), F32),
            ((2, tokens * tiles, LANES), F32),
            ((tokens, inner), F32),
            ((tokens, inner), F32),
            ((4, inner, LANES), F32),
            ((2 * width, LANES), F32),
            ((2 * width, LANES), F32),
        ],
        48,
        (
            data_own,
            out_time,
            out_tall,
            out_wide,
            pre_act,
            flat_latent,
            modulation,
            d_skip[None, :],
            w_in,
            w_out,
            *grads,
        ),
    )
    near_recv = exchange(near_send, NEAR)
    piece = own * tiles + 2 * own + width // far
    piece = -(-piece // 16) * 16
    far_send = call(
        middle_kernel,
        "weight_grads",
        [((far, piece, LANES), BF)],
        [
            ((inner // near, near * tokens), BF),
            ((far, piece, LANES), F32),
            ((inner // near, LANES), F32),
        ],
        48,
        (near_recv, grad_near, shifted_near),
    )[0]
    far_recv = exchange(far_send, FAR)
    grad_w_out, grad_select, small, grad_mod, last_send = call(
        last_kernel,
        "weight_sums",
        [
            ((own, width), F32),
            ((own, LANES), F32),
            ((own, LANES), F32),
            ((2 * own, features.shape[0]), F32),
            ((near, 16, LANES), F32),
        ],
        [((piece, LANES), F32)],
        16,
        (far_recv, feature_rows),
    )
    last_recv = exchange(last_send, NEAR)
    grad_w_in = call(join_kernel, "weight_rows", [((own, width), F32)], [], 16, (last_recv,))[0]
    rank = w_dt.shape[1]
    return (
        branch.reshape(latent.shape),
        latent_grad.reshape(latent.shape),
        grad_w_in,
        grad_w_out,
        grad_select,
        small[:, :rank],
        small[:, rank + states],
        small[:, rank : rank + states],
        small[:, rank + states + 1],
        grad_mod,
    )


def solution(mesh):
    n_row, n_col = mesh.shape["row"], mesh.shape["col"]
    split = Mesh(mesh.devices.reshape(n_row // 2, 2, 2, 4, n_col // 8), AXES)
    tokens = P(None, ROW, COL, None)
    matrix = P(ROW + COL, None)
    vector = P(ROW + COL)
    return jax.shard_map(
        local,
        mesh=split,
        in_specs=(tokens, tokens) + (P(),) * 12,
        out_specs=(
            tokens,
            tokens,
            matrix,
            matrix,
            matrix,
            matrix,
            vector,
            matrix,
            vector,
            matrix,
        ),
        check_vma=False,
    )
```

time: 1860 us -> 244 us (0.13); the launches traced: 1830 us -> 242 us
  starting transfers between devices: 487 us -> 14.9 us
  local copies, waits for them, and re-layouts: 494 us -> 33.2 us
  blocking collectives: 461 us -> 82.7 us
  other arithmetic: 204 us -> 0.06 us
  waiting for transfers between devices: 127 us -> 16.9 us
  Pallas kernels: 0 us -> 79.6 us
  matrix products: 39.4 us -> 0 us
    unnamed x2 -> x0, blocking collectives: 461 us -> none
    unnamed x160 -> x0, starting transfers between devices: 438 us -> none
    unnamed x559 -> x65, local copies, waits for them, and re-layouts: 196 us -> 23.7 us
    reduce_sum x149 -> x0, other arithmetic: 131 us -> none  [the longest x104 94.4 us: advance(): space_t[:, None, :] * rates]
    squeeze x80 -> x0, local copies, waits for them, and re-layouts: 99.5 us -> none  [ssm_scan(): lax.scan(jax.checkpoint(advance), start, (values, spacing, input_map, out...]
    unnamed x160 -> x2, waiting for transfers between devices: 93.3 us -> 0.03 us
    all_to_all x0 -> x4, blocking collectives: none -> 82.7 us  [exchange(): return lax.all_to_all(value, axes, split_axis=0, concat_axis=0, tiled=True)]
    pallas_call x0 -> x8, Pallas kernels: none -> 79.6 us  [call(): pl.pallas_call(kernel, out_shape=tuple((jax.ShapeDtypeStruct(s, d) for s,...]
  transfers between devices with their start and end apart: 168 -> 5, of which waited for: 23 -> 2; matrix products, arithmetic and copies ran while one was open for 35% -> 4% of each run, Pallas kernels for 0% -> 29%
where the time goes in v1:
time: 244 us; the launch traced here: 242 us
  blocking collectives  82.7 us (34%)
  Pallas kernels  79.6 us (33%)
  local copies, waits for them, and re-layouts  33.2 us (14%)
  waiting for transfers between devices  16.9 us (7%)
  starting transfers between devices  14.9 us (6%)
  between operations  14.9 us (6%)
    all_to_all x4, blocking collectives, exchange(): return lax.all_to_all(value, axes, split_axis=0, concat_axis=0, tiled=True)  82.7 us
    pallas_call x8, Pallas kernels, call(): pl.pallas_call(kernel, out_shape=tuple((jax.ShapeDtypeStruct(s, d) for s,...  79.6 us
    unnamed x65, local copies, waits for them, and re-layouts  23.7 us
    all_to_all x3, waiting for transfers between devices, exchange(): return lax.all_to_all(value, axes, split_axis=0, concat_axis=0, tiled=True)  16.9 us
    all_to_all x3, starting transfers between devices, exchange(): return lax.all_to_all(value, axes, split_axis=0, concat_axis=0, tiled=True)  14.8 us
  transfers between devices with their start and end apart: 5, of which 2 were waited for; matrix products, arithmetic and copies ran while one was open for 4% of the time, Pallas kernels for 29%

profile of v1, /device:TPU:1, one launch (start us, length us, event | category | flops | bytes accessed | tf_op | source)
XLA Modules:
  0.0 242.2 jit_solution(1214588254498427897)
XLA Ops:
  7.2 1.9 reshape.59.grad_ref
  9.2 1.1 reshape.58.latent_ref
  12.1 1.4 copy-done.2
  13.5 6.7 %norm_project.1 = (bf16[1,2,1536,128]{3,2,1,0:T(8,128)(2,1)S(1)}, bf16[4,2,384,128]{3,2,1,0:T(8,128)(2,1)S(1)}, bf16[32,2,48,128]{3,2,1,0:T(8,128)(2,1)S(1)}, bf...) custom-call(bf16[128,1536]{1,0:T(8,128)(2,1)S(1)} %reshape.58.latent_ref, ...), custom_call_target="tpu_custom_call" | custom-call | tf_op jit(solution)/shard_map/norm_project/pallas_call | solution.py:42
  22.6 24.5 %all_to_all.35.data_ref = bf16[32,2,48,128]{3,2,1,0:T(8,128)(2,1)S(1)} all-to-all(bf16[32,2,48,128]{3,2,1,0:T(8,128)(2,1)S(1)} %get-tuple-element.39), channel_id=1, replica_groups=mesh['xl'=2,'core'=2,'xh'=2,'y'=4,'z'=4] {'xh','y','z'}, dimensions={0} | all-to-all | bytes 1572864 | tf_op jit(solution)/shard_map/all_to_all | solution.py:487
  47.2 6.6 %all-to-all-start = ((bf16[4,2,384,128]{3,2,1,0:T(8,128)(2,1)}), bf16[4,2,384,128]{3,2,1,0:T(8,128)(2,1)S(1)}, u32[]{:S(2)}, u32[]{:S(2)}) async-start(bf16[4,2,384,128]{3,2,1,0:T(8,128)(2,1)} %copy-done.11), calls=%async_computation | async-start | bytes 1572864 | tf_op jit(solution)/shard_map/all_to_all | solution.py:487
  56.8 18.2 %scan_time.1 = (bf16[1,2,1536,128]{3,2,1,0:T(8,128)(2,1)S(1)}, f32[1536,128]{1,0:T(8,128)S(1)}, f32[1536,128]{1,0:T(8,128)S(1)}, f32[24,1536]{1,0:T(8,128)S(1)}) custom-call(s32[32]{0:T(128)S(1)} %copy-done.27, bf16[1,2,1536,128]{3,2,1,0:T(8,128)(2,1)S(1)} %get-tuple-element.36.data_ref.own_ref, bf16[1536,128]{1,0:T(8,128)(2,1)S(1)} %copy-done.1, ...), custom_call_target="tpu_custom_call" | custom-call | tf_op jit(solution)/shard_map/scan_time/pallas_call | solution.py:42
  77.5 17.9 %scan_width.1 = (bf16[32,2,48,128]{3,2,1,0:T(8,128)(2,1)S(1)}, f32[1536,128]{1,0:T(8,128)S(1)}, f32[1536,128]{1,0:T(8,128)S(1)}, f32[24,1536]{1,0:T(8,128)S(1)}) custom-call(s32[64]{0:T(128)S(1)} %copy-done.28, bf16[32,2,48,128]{3,2,1,0:T(8,128)(2,1)S(1)} %all_to_all.35.data_ref, bf16[1536,128]{1,0:T(8,128)(2,1)S(1)} %copy-done.1, ...), custom_call_target="tpu_custom_call" | custom-call | tf_op jit(solution)/shard_map/scan_width/pallas_call | solution.py:42
  99.6 1.1 copy-done.14
  100.8 1.1 copy-done.16
  103.5 17.2 %scan_height.1 = (bf16[4,2,384,128]{3,2,1,0:T(8,128)(2,1)S(1)}, f32[1536,128]{1,0:T(8,128)S(1)}, f32[1536,128]{1,0:T(8,128)S(1)}, f32[24,1536]{1,0:T(8,128)S(1)}) custom-call(s32[8]{0:T(128)S(1)} %copy-done.29, bf16[4,2,384,128]{3,2,1,0:T(8,128)(2,1)S(1)} %all-to-all-done.data_ref, bf16[1536,128]{1,0:T(8,128)(2,1)S(1)} %copy-done.1, ...), custom_call_target="tpu_custom_call" | custom-call | tf_op jit(solution)/shard_map/scan_height/pallas_call | solution.py:42
  121.6 14.1 %all_to_all.36.tall_ref = bf16[4,2,384,128]{3,2,1,0:T(8,128)(2,1)S(1)} all-to-all(bf16[4,2,384,128]{3,2,1,0:T(8,128)(2,1)S(1)} %get-tuple-element.46), channel_id=1, replica_groups=mesh['xl'=2,'core'=2,'xh'=2,'y'=4,'z'=4] {'xl','core'}, dimensions={0} | all-to-all | bytes 1572864 | tf_op jit(solution)/shard_map/all_to_all | solution.py:487
  135.7 4.6 %all-to-all-start.3 = ((bf16[32,2,48,128]{3,2,1,0:T(8,128)(2,1)}), bf16[32,2,48,128]{3,2,1,0:T(8,128)(2,1)S(1)}, u32[]{:S(2)}, u32[]{:S(2)}) async-start(bf16[32,2,48,128]{3,2,1,0:T(8,128)(2,1)} %copy-done.12), calls=%async_computation.3 | async-start | bytes 1572864 | tf_op jit(solution)/shard_map/all_to_all | solution.py:487
  141.1 14.8 %all-to-all-done.3.wide_ref = bf16[32,2,48,128]{3,2,1,0:T(8,128)(2,1)S(1)} async-done(((bf16[32,2,48,128]{3,2,1,0:T(8,128)(2,1)}), bf16[32,2,48,128]{3,2,1,0:T(8,128)(2,1)S(1)}, u32[]{:S(2)}, u32[]{:S(2)}) %all-to-all-start.3) | async-done | bytes 786464 | tf_op jit(solution)/shard_map/all_to_all | solution.py:487
  155.8 1.1 copy-done.7
  157.0 1.1 copy-done.9
  159.9 10.9 %sum_project.1 = (bf16[128,1536]{1,0:T(8,128)(2,1)S(1)}, bf16[128,1536]{1,0:T(8,128)(2,1)S(1)}, bf16[16,4,96,128]{3,2,1,0:T(8,128)(2,1)}) custom-call(bf16[1,2,1536,128]{3,2,1,0:T(8,128)(2,1)S(1)} %get-tuple-element.36.data_ref.own_ref, bf16[1,2,1536,128]{3,2,1,0:T(8,128)(2,1)S(1)} %copy-done.9, bf16[4,2,384,128]{3,2,1,0:T(8,128)(2,1)S(1)} %all_to_all.36.tall_ref, ...), custom_call_target="tpu_custom_call" | custom-call | tf_op jit(solution)/shard_map/sum_project/pallas_call | solution.py:42
  172.3 24.2 %all_to_all.37.recv_ref = bf16[16,4,96,128]{3,2,1,0:T(8,128)(2,1)S(1)} all-to-all(bf16[16,4,96,128]{3,2,1,0:T(8,128)(2,1)} %get-tuple-element.55), channel_id=1, replica_groups=mesh['xl'=2,'core'=2,'xh'=2,'y'=4,'z'=4] {'y','z'}, dimensions={0} | all-to-all | bytes 3145728 | tf_op jit(solution)/shard_map/all_to_all | solution.py:487
  196.6 7.1 %weight_grads.1 = bf16[8,368,128]{2,1,0:T(8,128)(2,1)S(1)} custom-call(bf16[16,4,96,128]{3,2,1,0:T(8,128)(2,1)S(1)} %all_to_all.37.recv_ref, bf16[2048,1536]{1,0:T(8,128)(2,1)} %all-gather.3.cloned.1.call-done.grad_ref, bf16[2048,1536]{1,0:T(8,128)(2,1)} %all-gather.5.cloned.1.call-done.shifted_ref), custom_call_target="tpu_custom_call" | custom-call | tf_op jit(solution)/shard_map/weight_grads/pallas_call | solution.py:42
  203.7 19.8 %all_to_all.38.recv_ref = bf16[8,368,128]{2,1,0:T(8,128)(2,1)S(1)} all-to-all(bf16[8,368,128]{2,1,0:T(8,128)(2,1)S(1)} %weight_grads.1), channel_id=1, replica_groups=mesh['xl'=2,'core'=2,'xh'=2,'y'=4,'z'=4] {'xl','core','xh'}, dimensions={0} | all-to-all | bytes 1507328 | tf_op jit(solution)/shard_map/all_to_all | solution.py:487
  224.3 3.6 %all-to-all-start.6 = ((f32[16,16,128]{2,1,0:T(8,128)}), f32[16,16,128]{2,1,0:T(8,128)S(1)}, u32[]{:S(2)}, u32[]{:S(2)}) async-start(f32[16,16,128]{2,1,0:T(8,128)} %get-tuple-element.57), calls=%async_computation.6 | async-start | bytes 262144 | tf_op jit(solution)/shard_map/all_to_all | solution.py:487
  229.7 1.4 slice.14
  231.1 1.5 slice_reduce_fusion
  232.5 2.1 all-to-all-done.6.recv_ref
  (79 shorter events, 23.1 us)
Async XLA Ops:
  7.2 189.4 %all-gather.3.cloned.1.call-start = ((), (), s32[]{:S(2)}) async-start(), calls=%async_computation.7 | async-start | bytes 6684672 | tf_op jit(solution)/shard_map/all_gather | solution.py:522
  9.1 187.4 %all-gather.5.cloned.1.call-start = ((), (), s32[]{:S(2)}) async-start(), calls=%async_computation.8 | async-start | bytes 6684672 | tf_op jit(solution)/shard_map/all_gather | solution.py:540
  11.1 1.0 copy-start
  12.1 1.4 copy-start.2
  13.5 40.3 %copy-start.30 = (bf16[1536,96]{0,1:T(8,128)(2,1)S(1)}, bf16[1536,96]{0,1:T(8,128)(2,1)}, u32[]{:S(2)}) copy-start(bf16[1536,96]{0,1:T(8,128)(2,1)} %param.19) | copy-start | bytes 884740
  13.5 41.2 %copy-start.31 = (f32[1536]{0:T(1024)S(1)}, f32[1536]{0:T(1024)}, u32[]{:S(2)}) copy-start(f32[1536]{0:T(1024)} %param.20) | copy-start | bytes 18436
  21.0 0.9 copy-start.11
  22.6 33.3 %copy-start.1 = (bf16[1536,128]{1,0:T(8,128)(2,1)S(1)}, bf16[1536,128]{1,0:T(8,128)(2,1)}, u32[]{:S(2)}) copy-start(bf16[1536,128]{1,0:T(8,128)(2,1)} %wsel_ref.5) | copy-start | bytes 1179652
  22.6 33.3 %copy-start.27 = (s32[32]{0:T(128)S(1)}, s32[32]{0:T(128)}, u32[]{:S(2)}) copy-start(s32[32]{0:T(128)} %order_ref.3) | copy-start | bytes 388
  47.2 51.6 %all-to-all-start = ((bf16[4,2,384,128]{3,2,1,0:T(8,128)(2,1)}), bf16[4,2,384,128]{3,2,1,0:T(8,128)(2,1)S(1)}, u32[]{:S(2)}, u32[]{:S(2)}) async-start(bf16[4,2,384,128]{3,2,1,0:T(8,128)(2,1)} %copy-done.11), calls=%async_computation | async-start | bytes 1572864 | tf_op jit(solution)/shard_map/all_to_all | solution.py:487
  95.4 0.9 copy-start.12
  96.3 0.9 copy-start.13
  99.6 1.1 copy-start.14
  100.8 1.2 copy-start.16
  101.9 0.9 copy-start.22
  120.7 0.9 copy-start.10
  121.6 14.1 %copy-start.23 = (f32[24,1536]{1,0:T(8,128)}, f32[24,1536]{1,0:T(8,128)S(1)}, u32[]{:S(2)}) copy-start(f32[24,1536]{1,0:T(8,128)S(1)} %get-tuple-element.52.gvec_ref) | copy-start | bytes 442372
  135.7 20.1 %all-to-all-start.3 = ((bf16[32,2,48,128]{3,2,1,0:T(8,128)(2,1)}), bf16[32,2,48,128]{3,2,1,0:T(8,128)(2,1)S(1)}, u32[]{:S(2)}, u32[]{:S(2)}) async-start(bf16[32,2,48,128]{3,2,1,0:T(8,128)(2,1)} %copy-done.12), calls=%async_computation.3 | async-start | bytes 1572864 | tf_op jit(solution)/shard_map/all_to_all | solution.py:487
  155.8 1.1 copy-start.7
  157.0 1.1 copy-start.9
  158.1 0.9 copy-start.24
  196.5 31.4 %copy-start.20 = (bf16[128,1536]{1,0:T(8,128)(2,1)S(1)}, bf16[128,1536]{1,0:T(8,128)(2,1)}, u32[]{:S(2)}) copy-start(bf16[128,1536]{1,0:T(8,128)(2,1)} %copy-done.19) | copy-start | bytes 1179652
  196.5 32.3 %copy-start.18 = (bf16[128,1536]{1,0:T(8,128)(2,1)S(1)}, bf16[128,1536]{1,0:T(8,128)(2,1)}, u32[]{:S(2)}) copy-start(bf16[128,1536]{1,0:T(8,128)(2,1)} %copy-done.17) | copy-start | bytes 1179652
  224.3 10.4 %all-to-all-start.6 = ((f32[16,16,128]{2,1,0:T(8,128)}), f32[16,16,128]{2,1,0:T(8,128)S(1)}, u32[]{:S(2)}, u32[]{:S(2)}) async-start(f32[16,16,128]{2,1,0:T(8,128)} %get-tuple-element.57), calls=%async_computation.6 | async-start | bytes 262144 | tf_op jit(solution)/shard_map/all_to_all | solution.py:487
  (13 other events, 10.4 us)
Sparse Core Ops, SparseCore 0:
  10.8 72.3 all-gather.2
  85.9 67.5 all-gather.4

commit v2 on v1

v2 whole, which is shorter than its diff:
```python
import functools
import math

import jax
import jax.numpy as jnp
from jax import lax
from jax.experimental import pallas as pl
from jax.experimental.pallas import tpu as pltpu
from jax.sharding import Mesh
from jax.sharding import PartitionSpec as P

BF = jnp.bfloat16
F32 = jnp.float32
LANES = 128
GROUP = 4
LOG2E = math.log2(math.e)
MEGA = 1024 * 1024
VMEM_ALL = 63
PIECES = 4
SLOT = 16
AXES = ("xl", "core", "xh", "y", "z")
ROW = ("xl", "core")
COL = ("xh", "y", "z")
NEAR = ("y", "z")
FAR = ("xl", "core", "xh")
FAR_SIZE = 8
NT = (((1,), (1,)), ((), ()))
TN = (((0,), (0,)), ((), ()))


def time_features(step_index, width):
    halfway = width // 2
    frequency = jnp.exp(-math.log(10000.0) * jnp.arange(halfway, dtype=jnp.float32) / halfway)
    angles = step_index.astype(jnp.float32)[0] * frequency
    return jnp.concatenate([jnp.cos(angles), jnp.sin(angles)])


def total(terms):
    return functools.reduce(lambda a, b: a + b, terms)


def call(kernel, name, out_shape, scratch, vmem, flops, args, smem=(), late=(), pieces=None, choose=None):
    moved = [i for i in range(len(args)) if i not in smem]
    pieces, choose = pieces or {}, choose or {}
    held_shape = {
        i: args[i].shape[:1] + args[i].shape[2:] if i in choose else args[i].shape for i in moved
    }
    cuts = []
    for i in moved:
        size = args[i].shape[0] // pieces.get(i, 1)
        cuts += [(i, n, pl.ds(n * size, size)) for n in range(pieces.get(i, 1))]

    def body(*refs):
        given, out = refs[: len(args)], refs[len(args) : len(args) + len(out_shape)]
        rest = refs[len(args) + len(out_shape) :]
        held, rest = rest[: len(moved)], rest[len(moved) :]
        made, rest = rest[: len(out_shape)], rest[len(out_shape) :]
        in_sem, out_sem = rest[-2:]
        views = [given[i] if i in smem else held[moved.index(i)] for i in range(len(args))]
        copies = {
            (i, n): pltpu.make_async_copy(
                given[i].at[at, choose[i]] if i in choose else given[i].at[at],
                views[i].at[at],
                in_sem.at[place],
            )
            for place, (i, n, at) in enumerate(cuts)
        }
        for copy in copies.values():
            copy.start()
        for (i, _), copy in copies.items():
            if i not in late:
                copy.wait()
        waits = (lambda i, n=0: copies[i, n].wait(),) if late else ()
        kernel(*waits, *views, *made, *rest[:-2])
        sent = [
            pltpu.make_async_copy(made[n], out[n], out_sem.at[n]) for n in range(len(out_shape))
        ]
        for copy in sent:
            copy.start()
        for copy in sent:
            copy.wait()

    spaces = [
        pl.BlockSpec(memory_space=pltpu.SMEM if i in smem else pltpu.HBM) for i in range(len(args))
    ]
    return pl.pallas_call(
        body,
        out_shape=tuple(jax.ShapeDtypeStruct(s, d) for s, d in out_shape),
        in_specs=spaces,
        out_specs=(pl.BlockSpec(memory_space=pltpu.HBM),) * len(out_shape),
        scratch_shapes=[pltpu.VMEM(held_shape[i], args[i].dtype) for i in moved]
        + [pltpu.VMEM(s, d) for s, d in out_shape]
        + [pltpu.VMEM(s, d) for s, d in scratch]
        + [pltpu.SemaphoreType.DMA((len(cuts),)), pltpu.SemaphoreType.DMA((len(out_shape),))],
        compiler_params=pltpu.CompilerParams(vmem_limit_bytes=vmem * MEGA),
        cost_estimate=cost(flops, args),
        name=name,
    )(*args)


def cost(flops, args):
    return pl.CostEstimate(
        flops=int(flops),
        bytes_accessed=sum(a.size * a.dtype.itemsize for a in args),
        transcendentals=0,
    )


def plain_call(kernel, name, out_shape, scratch, vmem, flops, args, smem=()):
    spaces = [
        pl.BlockSpec(memory_space=pltpu.SMEM if i in smem else pltpu.VMEM) for i in range(len(args))
    ]
    return pl.pallas_call(
        kernel,
        out_shape=tuple(jax.ShapeDtypeStruct(s, d) for s, d in out_shape),
        in_specs=spaces,
        out_specs=(pl.BlockSpec(memory_space=pltpu.VMEM),) * len(out_shape),
        scratch_shapes=[pltpu.VMEM(s, d) for s, d in scratch],
        compiler_params=pltpu.CompilerParams(vmem_limit_bytes=vmem * MEGA),
        cost_estimate=cost(flops, args),
        name=name,
    )(*args)


def cut(j):
    return slice(LANES * j, LANES * j + LANES)


def to_flat(ref, j, value, tiles):
    ref[pl.ds(j, value.shape[0], stride=tiles), :] = value


def from_flat(ref, j, tokens, tiles):
    return ref[pl.ds(j, tokens, stride=tiles), :]


def normalise(latent):
    wide = latent.astype(F32)
    inverse = lax.rsqrt(jnp.mean(wide * wide, axis=-1, keepdims=True) + 1e-06)
    return wide * inverse, inverse


def pre_kernel(
    wait,
    latent_ref,
    grad_ref,
    w_in_ref,
    w_out_ref,
    w_mod_ref,
    feature_ref,
    place_ref,
    own_ref,
    wide_ref,
    slot_0_ref,
    slot_1_ref,
    slot_2_ref,
    slot_3_ref,
    both_ref,
    pre_ref,
    mod_ref,
    flat_ref,
):
    tokens, width = latent_ref.shape
    tiles = w_in_ref.shape[1] // LANES
    modulation = lax.dot_general(
        feature_ref[...], w_mod_ref[...], NT, preferred_element_type=F32
    )
    mod_ref[...] = modulation
    normed, _ = normalise(latent_ref[...])
    shifted = (normed * (1.0 + modulation[:1, width:]) + modulation[:1, :width]).astype(BF)
    both_ref[0] = shifted
    both_ref[1] = grad_ref[...]
    wait(2)
    pre_act = jnp.dot(shifted, w_in_ref[...], preferred_element_type=F32)
    pre_ref[...] = pre_act
    activ = (pre_act * jax.nn.sigmoid(pre_act)).astype(BF)
    wait(3)
    cot = lax.dot_general(grad_ref[...], w_out_ref[...], NT, preferred_element_type=F32).astype(BF)
    for which, value in enumerate((activ, cot)):
        wide = value.astype(F32)
        for j in range(tiles):
            to_flat(flat_ref, j, wide[:, cut(j)], tiles)
        flat = flat_ref[...].astype(BF)
        own_ref[0, which] = flat
        wide_ref[:, which] = flat.reshape(wide_ref.shape[0], wide_ref.shape[2], LANES)
        for k, ref in enumerate((slot_0_ref, slot_1_ref, slot_2_ref, slot_3_ref)):
            chunk = ref.shape[2]
            begin = pl.multiple_of((place_ref[0] ^ k) * chunk, chunk)
            ref[0, which] = flat_ref[pl.ds(begin, chunk), :].astype(BF)


def parts_of(refs):
    begin, found = 0, []
    for ref in refs:
        size = ref.shape[0] * ref.shape[2]
        found.append((ref, slice(begin, begin + size)))
        begin += size
    return found


def read_part(ref, which):
    return ref[:, which].reshape(ref.shape[0] * ref.shape[2], LANES).astype(F32)


def write_part(ref, which, value):
    ref[:, which] = value.astype(BF).reshape(ref.shape[0], ref.shape[2], LANES)


def scan_kernel(
    length,
    row_of,
    pieces,
    order_ref,
    place_ref,
    *refs,
):
    data_refs, out_refs = refs[:pieces], refs[pieces + 4 : 2 * pieces + 4]
    scan_steps(
        length,
        row_of,
        order_ref,
        place_ref,
        data_refs,
        *refs[pieces : pieces + 4],
        out_refs,
        *refs[2 * pieces + 4 :],
    )


def scan_steps(
    length,
    row_of,
    order_ref,
    place_ref,
    data_refs,
    wsel_ref,
    wdt_ref,
    bias_ref,
    alog_ref,
    out_refs,
    x_ref,
    grad_pre_ref,
    low_ref,
    grad_low_ref,
    gvec_ref,
    pre_ref,
    dt_ref,
    xf_ref,
    x_row_ref,
    dt_row_ref,
    dx_row_ref,
    dy_row_ref,
    bb_ref,
    cb_ref,
    gb_ref,
    gc_ref,
    hist_ref,
    y8_ref,
    u8_ref,
    v8_ref,
    rate2_ref,
    rate_ref,
):
    tokens, inner = xf_ref.shape
    tiles = inner // LANES
    lines = tokens // length
    states = alog_ref.shape[0]
    rank = LANES - 2 * states
    for ref, at in parts_of(data_refs):
        x_row_ref[at, :] = read_part(ref, 0)
        dy_row_ref[at, :] = read_part(ref, 1)
    for j in range(tiles):
        xf_ref[:, cut(j)] = from_flat(x_row_ref, j, tokens, tiles)
    x = xf_ref[...].astype(BF)
    x_ref[...] = x
    select = jnp.dot(x, wsel_ref[...], preferred_element_type=F32)
    lane = lax.broadcasted_iota(jnp.int32, (tokens, LANES), 1)
    low = jnp.where(lane < rank, select, 0.0).astype(BF)
    low_ref[...] = low
    w_dt = jnp.concatenate([wdt_ref[...], jnp.zeros((2 * states, inner), BF)], axis=0)
    pre = jnp.dot(low, w_dt, preferred_element_type=F32) + bias_ref[...]
    pre_ref[...] = pre
    spacing = jnp.maximum(pre, 0.0) + jnp.log1p(jnp.exp(-jnp.abs(pre)))
    dt_ref[...] = spacing
    for j in range(tiles):
        to_flat(dt_row_ref, j, spacing[:, cut(j)], tiles)
    dx_row_ref[...] = dt_row_ref[...] * x_row_ref[...]
    rates = -jnp.exp(alog_ref[...])
    rate_ref[...] = rates
    rate2_ref[...] = rates * LOG2E
    turned = select.T
    for token in range(tokens):
        at = pl.ds(token * states, states)
        column = slice(token, token + 1)
        bb_ref[at, :] = jnp.broadcast_to(turned[rank : rank + states, column], (states, LANES))
        cb_ref[at, :] = jnp.broadcast_to(turned[rank + states :, column], (states, LANES))
    gb_ref[...] = jnp.zeros_like(gb_ref)
    gc_ref[...] = jnp.zeros_like(gc_ref)
    zero = jnp.zeros((states, LANES), F32)
    hist_ref[pl.ds(0, states), :] = jnp.zeros((states, GROUP * LANES), F32)
    unroll = min(length, 8)

    def fold(value):
        return value[:8] + value[8:]

    for group in range(tiles // GROUP):
        first = group * GROUP
        cuts = [cut(first + j) for j in range(GROUP)]
        rate2 = [rate2_ref[:, c] for c in cuts]
        rate1 = [rate_ref[:, c] for c in cuts]

        def one_line(line, grads):
            def places(step):
                row = row_of(order_ref[step], line, place_ref[0])
                at = pl.ds(pl.multiple_of(row * states, states), states)
                slot = pl.ds(pl.multiple_of((step + 1) * states, states), states)
                return row * tiles + first, pl.multiple_of(row * 8, 8), at, slot

            def forward(step, carry):
                row, at_8, at, slot = places(step)
                bb, cb = bb_ref[at, :], cb_ref[at, :]
                new = []
                for j in range(GROUP):
                    dt = dt_row_ref[pl.ds(row + j, 1), :]
                    dx = dx_row_ref[pl.ds(row + j, 1), :]
                    h = jnp.exp2(rate2[j] * dt) * carry[j] + bb * dx
                    hist_ref[slot, cut(j)] = h
                    y8_ref[pl.ds(at_8 + 8 * tokens * j, 8), :] = fold(h * cb)
                    new.append(h)
                return tuple(new)

            lax.fori_loop(0, length, forward, (zero,) * GROUP, unroll=unroll)

            def backward(back_step, carry):
                step = length - 1 - back_step
                row, at_8, at, slot = places(step)
                prev = pl.ds(pl.multiple_of(step * states, states), states)
                bb, cb = bb_ref[at, :], cb_ref[at, :]
                pend, acc = carry
                gb = gb_ref[at, :]
                gc = gc_ref[at, :]
                new, acc_new = [], []
                for j in range(GROUP):
                    dt = dt_row_ref[pl.ds(row + j, 1), :]
                    dx = dx_row_ref[pl.ds(row + j, 1), :]
                    dy = dy_row_ref[pl.ds(row + j, 1), :]
                    g = pend[j] + cb * dy
                    gc = gc + hist_ref[slot, cut(j)] * dy
                    u8_ref[pl.ds(at_8 + 8 * tokens * j, 8), :] = fold(g * bb)
                    gb = gb + g * dx
                    p = jnp.exp2(rate2[j] * dt) * g
                    w = p * hist_ref[prev, cut(j)]
                    v8_ref[pl.ds(at_8 + 8 * tokens * j, 8), :] = fold(w * rate1[j])
                    acc_new.append(acc[j] + w * dt)
                    new.append(p)
                gb_ref[at, :] = gb
                gc_ref[at, :] = gc
                return tuple(new), tuple(acc_new)

            start = ((zero,) * GROUP, grads)
            return lax.fori_loop(0, length, backward, start, unroll=unroll)[1]

        grads = lax.fori_loop(0, lines, one_line, (zero,) * GROUP)
        for j in range(GROUP):
            gvec_ref[:states, cuts[j]] = grads[j] * rate1[j]

        def gather(block, carry):
            rows = pl.ds(pl.multiple_of(block * 8, 8), 8)

            def summed(ref, j):
                begin = block * 64 + 8 * tokens * j
                return total([ref[pl.ds(begin + r, 8, stride=8), :] for r in range(8)])

            for j in range(GROUP):
                c = cuts[j]
                u = summed(u8_ref, j)
                x_row_ref[pl.ds(block * 8 * tiles + first + j, 8, stride=tiles), :] = summed(y8_ref, j)
                grad_spacing = summed(v8_ref, j) + xf_ref[rows, c] * u
                pre_ref[rows, c] = grad_spacing * jax.nn.sigmoid(pre_ref[rows, c])
                dt_ref[rows, c] = dt_ref[rows, c] * u
            return carry

        lax.fori_loop(0, tokens // 8, gather, 0, unroll=2)

    for ref, at in parts_of(out_refs):
        write_part(ref, 0, x_row_ref[at, :])
    grad_pre = pre_ref[...]
    gvec_ref[states:, :] = jnp.broadcast_to(
        jnp.sum(grad_pre, axis=0, keepdims=True), (8, inner)
    )
    grad_pre_b = grad_pre.astype(BF)
    grad_pre_ref[...] = grad_pre_b
    ones = jnp.ones((LANES, LANES), BF)

    def lane_total(ref):
        value = ref[...]
        top = value.astype(BF)
        rest = (value - top.astype(F32)).astype(BF)
        return jnp.dot(top, ones, preferred_element_type=F32) + jnp.dot(
            rest, ones, preferred_element_type=F32
        )

    shape = (tokens * states, LANES)
    state_at = lax.broadcasted_iota(jnp.int32, shape, 0) % states
    lane_at = lax.broadcasted_iota(jnp.int32, shape, 1)
    gb_ref[...] = jnp.where(lane_at == state_at + rank, lane_total(gb_ref), 0.0) + jnp.where(
        lane_at == state_at + rank + states, lane_total(gc_ref), 0.0
    )
    grad_maps = total([gb_ref[pl.ds(n, tokens, stride=states), :] for n in range(states)])
    grad_low = lax.dot_general(grad_pre_b, w_dt, NT, preferred_element_type=F32)
    grad_select_out = (grad_low + grad_maps).astype(BF)
    grad_low_ref[...] = grad_select_out
    back = dt_ref[...] + lax.dot_general(
        grad_select_out, wsel_ref[...], NT, preferred_element_type=F32
    )
    for j in range(tiles):
        to_flat(x_row_ref, j, back[:, cut(j)], tiles)
    for ref, at in parts_of(out_refs):
        write_part(ref, 1, x_row_ref[at, :])


def direction(name, length, row_of, order, place, data, params):
    inner = params[0].shape[0]
    tiles = inner // LANES
    tokens = sum(d.shape[0] * d.shape[2] for d in data) // tiles
    states = params[3].shape[0]
    plane = ((tokens, inner), F32)
    flat = ((tokens * tiles, LANES), F32)
    maps = ((tokens * states, LANES), F32)
    eights = ((tokens * 8 * GROUP, LANES), F32)
    results = call(
        functools.partial(scan_kernel, length, row_of, len(data)),
        name,
        [(d.shape, BF) for d in data]
        + [((tokens, inner), BF)] * 2
        + [((tokens, LANES), BF)] * 2
        + [((states + 8, inner), F32)],
        [plane] * 3
        + [flat] * 4
        + [maps] * 4
        + [(((length + 1) * states, GROUP * LANES), F32)]
        + [eights] * 3
        + [((states, inner), F32)] * 2,
        VMEM_ALL,
        2e10,
        (order, place, *data, *params),
        smem=(0, 1),
    )
    return results[: len(data)], results[len(data) :]


def small_kernel(own_ref, *refs):
    found, refs = [refs[5 * d : 5 * d + 5] for d in range(3)], refs[15:]
    send_ref, row_ref, turned_ref = refs
    inner = found[0][0].shape[1]
    tiles = inner // LANES
    tokens = own_ref.shape[2] // tiles
    own = inner // send_ref.shape[0]
    states = found[0][4].shape[0] - 8
    rank = LANES - 2 * states
    row_ref[...] = own_ref[0, 0].astype(F32) * own_ref[0, 1].astype(F32)
    skips = jnp.concatenate(
        [
            jnp.sum(from_flat(row_ref, j, tokens, tiles), axis=0, keepdims=True)
            for j in range(tiles)
        ],
        axis=1,
    )
    x, grad_pre, low, grad_low = [
        jnp.concatenate([d[i][...] for d in found], axis=0) for i in range(4)
    ]
    summed = total([d[4][...] for d in found])
    at = lax.broadcasted_iota(jnp.int32, (LANES, inner), 0)
    vectors = jnp.concatenate(
        [jnp.zeros((rank, inner), F32), summed, jnp.zeros((states - 8, inner), F32)], axis=0
    )
    vectors = jnp.where(at > rank + states, 0.0, vectors) + jnp.where(
        at == rank + states + 1, jnp.broadcast_to(skips, at.shape), 0.0
    )
    turned_ref[0, :inner] = lax.dot_general(x, grad_low, TN, preferred_element_type=F32)
    turned_ref[1, :inner] = vectors.T + lax.dot_general(
        grad_pre, low, TN, preferred_element_type=F32
    )
    turned_ref[:, inner:] = jnp.zeros((2, SLOT - own, LANES), F32)
    for d in range(send_ref.shape[0]):
        for which in (0, 1):
            send_ref[d, which * SLOT : (which + 1) * SLOT] = turned_ref[
                which, d * own : d * own + SLOT
            ].astype(BF)


def spread_rows(ref, which, m, own, near):
    return jnp.concatenate(
        [ref[which, pl.ds(m * own + i, FAR_SIZE, stride=near * own), :] for i in range(own)],
        axis=0,
    ).astype(BF)


def post_kernel(
    wait,
    place_ref,
    own_ref,
    time_ref,
    wide_ref,
    slot_0_ref,
    slot_1_ref,
    slot_2_ref,
    slot_3_ref,
    pre_ref,
    latent_ref,
    mod_ref,
    skip_ref,
    w_in_ref,
    mixed_out_ref,
    normed_grad_ref,
    send_ref,
    sum_ref,
    own_row_ref,
    plane_ref,
    turned_ref,
    vec_ref,
):
    tokens, width = latent_ref.shape
    inner = w_in_ref.shape[1]
    tiles = inner // LANES
    flat_shape = (tokens * tiles, LANES)
    near = send_ref.shape[0]
    near_rows = inner // near
    own = near_rows // FAR_SIZE

    def summed(which):
        sum_ref[...] = time_ref[0, which].astype(F32) + wide_ref[:, which].reshape(
            flat_shape
        ).astype(F32)
        for k, ref in enumerate((slot_0_ref, slot_1_ref, slot_2_ref, slot_3_ref)):
            chunk = ref.shape[2]
            at = pl.ds(pl.multiple_of((place_ref[0] ^ k) * chunk, chunk), chunk)
            sum_ref[at, :] += ref[0, which].astype(F32)
        own_row_ref[...] = own_ref[0, which].astype(F32)
        for j in range(tiles):
            mine = from_flat(own_row_ref, j, tokens, tiles)
            plane_ref[:, cut(j)] = from_flat(sum_ref, j, tokens, tiles) + skip_ref[:, cut(j)] * mine

    summed(1)
    pre_act = pre_ref[...]
    gate = jax.nn.sigmoid(pre_act)
    grad_act = (plane_ref[...] * gate * (1.0 + pre_act * (1.0 - gate))).astype(BF)
    summed(0)
    mixed = plane_ref[...].astype(BF)
    mixed_out_ref[...] = mixed
    wait(12)
    grad_shifted = lax.dot_general(grad_act, w_in_ref[...], NT, preferred_element_type=F32)
    normed, _ = normalise(latent_ref[...])
    normed_grad_ref[...] = grad_shifted * (1.0 + mod_ref[:1, width:])
    grad_vec = jnp.concatenate(
        [
            jnp.sum(grad_shifted, axis=0, keepdims=True),
            jnp.sum(grad_shifted * normed, axis=0, keepdims=True),
        ],
        axis=1,
    )
    devices = near * FAR_SIZE
    part = 2 * own
    shape = (devices, 2 * width)
    block_at = lax.broadcasted_iota(jnp.int32, shape, 0) * part
    column_at = lax.broadcasted_iota(jnp.int32, shape, 1)
    mine = (column_at >= block_at) & (column_at < block_at + part)
    chosen = jnp.where(mine, jnp.broadcast_to(grad_vec, shape), 0.0)
    top = chosen.astype(BF)
    rest = (chosen - top.astype(F32)).astype(BF)
    lane_at = lax.broadcasted_iota(jnp.int32, (2 * width, LANES), 1)
    place = lax.broadcasted_iota(jnp.int32, (2 * width, LANES), 0) % part
    choose = jnp.where(lane_at == place, 1.0, 0.0).astype(BF)
    vec_ref[...] = jnp.dot(top, choose, preferred_element_type=F32) + jnp.dot(
        rest, choose, preferred_element_type=F32
    )
    turned_ref[0] = mixed.astype(F32).T
    turned_ref[1] = grad_act.astype(F32).T
    for m in range(near):
        send_ref[m, :near_rows] = spread_rows(turned_ref, 0, m, own, near)
        send_ref[m, near_rows : 2 * near_rows] = turned_ref[
            1, pl.ds(m * near_rows, near_rows), :
        ].astype(BF)
        send_ref[m, 2 * near_rows :] = jnp.concatenate(
            [vec_ref[pl.ds(m, FAR_SIZE, stride=near), :], jnp.zeros((8, LANES), F32)], axis=0
        ).astype(BF)


def finish_kernel(
    mixed_ref, normed_grad_ref, latent_ref, w_out_ref, branch_ref, latent_grad_ref
):
    branch_ref[...] = jnp.dot(
        mixed_ref[...], w_out_ref[...], preferred_element_type=F32
    ).astype(BF)
    normed, inverse = normalise(latent_ref[...])
    grad_normed = normed_grad_ref[...]
    product = jnp.mean(grad_normed * normed, axis=1, keepdims=True)
    latent_grad_ref[...] = (inverse * (grad_normed - normed * product)).astype(BF)


def long_product(wait, at, left, right_ref):
    size = right_ref.shape[0] // PIECES
    tokens, width = right_ref.shape[1:]
    terms = []
    for n in range(PIECES):
        wait(at, n)
        rows = slice(n * size * tokens, (n + 1) * size * tokens)
        right = right_ref[n * size : (n + 1) * size].reshape(size * tokens, width)
        terms.append(jnp.dot(left[:, rows], right, preferred_element_type=F32))
    return total(terms)


def in_grad_kernel(wait, recv_ref, both_ref, small_ref, all_ref, right_ref, rows_ref):
    near = recv_ref.shape[0]
    rows = right_ref.shape[0]
    width = both_ref.shape[2]
    own = rows // FAR_SIZE
    for s in range(near):
        right_ref[:, cut(s)] = recv_ref[s, rows : 2 * rows]
    all_ref[:, SLOT:] = small_ref[...]
    product = long_product(wait, 1, right_ref, both_ref)
    turned = jnp.concatenate([product, jnp.zeros((LANES - rows, width), F32)], axis=0).T
    rows_ref[:width] = turned
    rows_ref[width:] = jnp.zeros((rows_ref.shape[0] - width, LANES), F32)
    for d in range(all_ref.shape[0]):
        all_ref[d, :SLOT] = rows_ref[pl.ds(d * own, SLOT), :].astype(BF)


def out_grad_kernel(wait, place_ref, recv_ref, both_ref, *refs):
    far_refs = refs[:FAR_SIZE]
    left_ref, out_ref, half_ref = refs[FAR_SIZE:]
    near = recv_ref.shape[0]
    rows = left_ref.shape[0]
    far = FAR_SIZE
    tiles = both_ref.shape[2] // LANES
    own = rows // far
    for s in range(near):
        left_ref[:, cut(s)] = recv_ref[s, :rows]
    vec = total([recv_ref[s, 2 * rows :].astype(F32) for s in range(near)])
    base = own * tiles
    for o in range(far):
        out_ref[o, base:, :] = jnp.broadcast_to(vec[o : o + 1], (SLOT, LANES))
    product = long_product(wait, 2, left_ref, both_ref)
    for j in range(tiles):
        half_ref[...] = product[:, cut(j)]
        for o in range(far):
            out_ref[o, pl.ds(j, own, stride=tiles), :] = half_ref[pl.ds(o, own, stride=far), :]
    for k, ref in enumerate(far_refs):
        ref[...] = out_ref[place_ref[0] ^ k].astype(BF)


def last_kernel(all_ref, feature_ref, *refs):
    far_refs = refs[:FAR_SIZE]
    gwo_ref, gwi_ref, gsel_ref, small_ref, gmod_ref, sum_ref, rest_ref = refs[FAR_SIZE:]
    far = FAR_SIZE
    own, width = gwo_ref.shape
    tiles = width // LANES
    near = all_ref.shape[0] // far
    part = width // near
    sum_ref[...] = total([ref[...].astype(F32) for ref in far_refs])
    for j in range(tiles):
        gwo_ref[:, cut(j)] = sum_ref[pl.ds(j, own, stride=tiles), :]
    vec = sum_ref[own * tiles : own * tiles + 8, :].T
    gmod_ref[...] = vec[: 2 * own, :1] * feature_ref[:1, :].astype(F32)
    rest = []
    for m in range(near):
        block = total([all_ref[o * near + m].astype(F32) for o in range(far)])
        gwi_ref[:, part * m : part * (m + 1)] = block[:own, :part]
        rest.append(block[SLOT:])
    rest_ref[...] = total(rest)
    gsel_ref[...] = rest_ref[:own, :]
    small_ref[...] = rest_ref[SLOT : SLOT + own, :]


def permute(value, axes, k):
    if k == 0:
        return value
    return lax.ppermute(value, axes, [(i, i ^ k) for i in range(lax.axis_size(axes))])


def exchange(value, axes):
    return lax.all_to_all(value, axes, split_axis=0, concat_axis=0, tiled=True)


def local(
    latent,
    out_grad,
    w_in,
    w_out,
    w_select,
    w_dt,
    dt_bias,
    a_log,
    d_skip,
    w_mod,
    t_index,
    frame_order,
    row_order,
    col_order,
):
    frames, rows, cols, width = latent.shape
    inner = w_in.shape[1]
    tokens = frames * rows * cols
    tiles = inner // LANES
    states = a_log.shape[1]
    n_row, n_col = lax.axis_size(ROW), lax.axis_size(COL)
    near, far = lax.axis_size(NEAR), lax.axis_size(FAR)
    own = width // (near * far)
    flat_latent = latent.reshape(tokens, width)
    flat_grad = out_grad.reshape(tokens, width)
    features = jax.nn.silu(time_features(t_index, w_mod.shape[1])).astype(BF)
    feature_rows = jnp.broadcast_to(features[None, :], (8, features.shape[0]))

    def packed(parts):
        return ((parts, 2, tokens * tiles // parts, LANES), BF)

    slot = ((1, 2, tokens * tiles // n_row, LANES), BF)
    place = lax.axis_index(ROW).astype(jnp.int32)[None]
    far_place = lax.axis_index(FAR).astype(jnp.int32)[None]
    data_own, data_wide, *slots, both, pre_act, modulation = call(
        pre_kernel,
        "norm_project",
        [
            packed(1),
            packed(n_col),
            slot,
            slot,
            slot,
            slot,
            ((2, tokens, width), BF),
            ((tokens, inner), F32),
            ((8, 2 * width), F32),
        ],
        [((tokens * tiles, LANES), F32)],
        VMEM_ALL,
        7e9,
        (flat_latent, flat_grad, w_in, w_out, w_mod, feature_rows, place),
        smem=(6,),
        late=(2, 3),
    )
    data_wide = exchange(data_wide, COL)
    slots = [permute(value, ROW, k) for k, value in enumerate(slots)]
    both_near = lax.all_gather(both, NEAR, axis=0, tiled=False)
    params = (
        w_select,
        w_dt.T,
        dt_bias[None, :],
        a_log.T,
    )
    area = rows * cols

    def time_row(at, line, place):
        return at * area + line

    def wide_row(at, line, place):
        chunk = frames // n_col * area
        return (
            lax.div(at, cols) * chunk
            + lax.rem(at, cols)
            + lax.div(line, rows) * area
            + lax.rem(line, rows) * cols
        )

    def tall_row(at, line, place):
        chunk = frames // n_row * area
        return (
            (lax.div(at, rows) ^ place) * chunk
            + lax.rem(at, rows) * cols
            + lax.div(line, cols) * area
            + lax.rem(line, cols)
        )

    out_tall, grads_tall = direction(
        "scan_height", rows * n_row, tall_row, row_order, place, slots, params
    )
    out_slots = [permute(value, ROW, k) for k, value in enumerate(out_tall)]
    data_wide, _ = lax.optimization_barrier((data_wide, out_tall))
    (out_wide,), grads_wide = direction(
        "scan_width", cols * n_col, wide_row, col_order, place, [data_wide], params
    )
    data_time, out_slots, _ = lax.optimization_barrier((data_own, out_slots, out_wide))
    out_wide = exchange(out_wide, COL)
    (out_time,), grads_time = direction(
        "scan_time", frames, time_row, frame_order, place, [data_time], params
    )
    mixed, normed_grad, near_send = call(
        post_kernel,
        "sum_project",
        [
            ((tokens, inner), BF),
            ((tokens, width), F32),
            ((near, 2 * inner // near + 16, LANES), BF),
        ],
        [
            ((tokens * tiles, LANES), F32),
            ((tokens * tiles, LANES), F32),
            ((tokens, inner), F32),
            ((2, inner, LANES), F32),
            ((near * far, LANES), F32),
        ],
        VMEM_ALL,
        8e9,
        (
            place,
            data_own,
            out_time,
            out_wide,
            *out_slots,
            pre_act,
            flat_latent,
            modulation,
            d_skip[None, :],
            w_in,
        ),
        smem=(0,),
        late=(12,),
    )
    near_recv = exchange(near_send, NEAR)
    data_own, _ = lax.optimization_barrier((data_own, near_send))
    small_send = call(
        small_kernel,
        "small_sums",
        [((near * far, 2 * SLOT, LANES), BF)],
        [((tokens * tiles, LANES), F32), ((2, inner + SLOT - own, LANES), F32)],
        VMEM_ALL,
        3e9,
        (data_own, *grads_time, *grads_wide, *grads_tall),
    )[0]
    branch, latent_grad = plain_call(
        finish_kernel,
        "out_project",
        [((tokens, width), BF), ((tokens, width), BF)],
        [],
        24,
        2e9,
        (mixed, normed_grad, flat_latent, w_out),
    )
    piece = own * tiles + SLOT
    all_send = call(
        in_grad_kernel,
        "in_weight_grad",
        [((near * far, 3 * SLOT, LANES), BF)],
        [((inner // near, near * tokens), BF), ((width + SLOT - own, LANES), F32)],
        VMEM_ALL,
        3e9,
        (near_recv, both_near, small_send),
        late=(1,),
        pieces={1: PIECES},
        choose={1: 0},
    )[0]
    all_recv = exchange(all_send, FAR + NEAR)
    far_send = call(
        out_grad_kernel,
        "out_weight_grad",
        [((piece, LANES), BF)] * far,
        [
            ((inner // near, near * tokens), BF),
            ((far, piece, LANES), F32),
            ((inner // near, LANES), F32),
        ],
        VMEM_ALL,
        4e9,
        (far_place, near_recv, both_near),
        smem=(0,),
        late=(2,),
        pieces={2: PIECES},
        choose={2: 1},
    )
    far_recv = [permute(value, FAR, k) for k, value in enumerate(far_send)]
    grad_w_out, grad_w_in, grad_select, small, grad_mod = plain_call(
        last_kernel,
        "weight_sums",
        [
            ((own, width), F32),
            ((own, width), F32),
            ((own, LANES), F32),
            ((own, LANES), F32),
            ((2 * own, features.shape[0]), F32),
        ],
        [((piece, LANES), F32), ((2 * SLOT, LANES), F32)],
        16,
        1e9,
        (all_recv, feature_rows, *far_recv),
    )
    rank = w_dt.shape[1]
    return (
        branch.reshape(latent.shape),
        latent_grad.reshape(latent.shape),
        grad_w_in,
        grad_w_out,
        grad_select,
        small[:, :rank],
        small[:, rank + states],
        small[:, rank : rank + states],
        small[:, rank + states + 1],
        grad_mod,
    )


def solution(mesh):
    n_row, n_col = mesh.shape["row"], mesh.shape["col"]
    split = Mesh(mesh.devices.reshape(n_row // 2, 2, 2, 4, n_col // 8), AXES)
    tokens = P(None, ROW, COL, None)
    matrix = P(ROW + COL, None)
    vector = P(ROW + COL)
    return jax.shard_map(
        local,
        mesh=split,
        in_specs=(tokens, tokens) + (P(),) * 12,
        out_specs=(
            tokens,
            tokens,
            matrix,
            matrix,
            matrix,
            matrix,
            vector,
            matrix,
            vector,
            matrix,
        ),
        check_vma=False,
    )
```

time: 244 us -> 198 us (0.81)
  blocking collectives: 82.7 us -> 0 us
  starting transfers between devices: 14.9 us -> 49.6 us
  Pallas kernels: 79.6 us -> 98.3 us
  local copies, waits for them, and re-layouts: 33.2 us -> 16.4 us
    all_to_all x4 -> x0, blocking collectives: 82.7 us -> none  [exchange(): return lax.all_to_all(value, axes, split_axis=0, concat_axis=0, tiled=True)]
    all_to_all x3 -> x4, starting transfers between devices: 14.8 us -> 35.3 us  [exchange(): return lax.all_to_all(value, axes, split_axis=0, concat_axis=0, tiled=True)]
    pallas_call x8 -> x10, Pallas kernels: 79.6 us -> 98.3 us  [the longest x8 95.1 us: call(): pl.pallas_call(body, out_shape=tuple((jax.ShapeDtypeStruct(s, d) for s, d...]
    unnamed x65 -> x24, local copies, waits for them, and re-layouts: 23.7 us -> 6.22 us
    ppermute x0 -> x13, starting transfers between devices: none -> 14.2 us  [permute(): lax.ppermute(value, axes, [(i, i ^ k) for i in range(lax.axis_size(axes))])]
    ppermute x0 -> x13, waiting for transfers between devices: none -> 8.97 us  [permute(): lax.ppermute(value, axes, [(i, i ^ k) for i in range(lax.axis_size(axes))])]
    all_to_all x3 -> x4, waiting for transfers between devices: 16.9 us -> 9.02 us  [exchange(): return lax.all_to_all(value, axes, split_axis=0, concat_axis=0, tiled=True)]
  transfers between devices with their start and end apart: 5 -> 18, of which waited for: 2 -> 2; matrix products, arithmetic and copies ran while one was open for 4% -> 2% of each run, Pallas kernels for 29% -> 41%
where the time goes in v2:
time: 198 us; the launch traced here: 197 us
  Pallas kernels  98.3 us (50%)
  starting transfers between devices  49.6 us (25%)
  waiting for transfers between devices  18 us (9%)
  local copies, waits for them, and re-layouts  16.4 us (8%)
  between operations  15 us (8%)
    pallas_call x8, Pallas kernels, call(): pl.pallas_call(body, out_shape=tuple((jax.ShapeDtypeStruct(s, d) for s, d...  95.1 us
    all_to_all x4, starting transfers between devices, exchange(): return lax.all_to_all(value, axes, split_axis=0, concat_axis=0, tiled=True)  35.3 us
    ppermute x13, starting transfers between devices, permute(): lax.ppermute(value, axes, [(i, i ^ k) for i in range(lax.axis_size(axes))])  14.2 us
    all_to_all x4, waiting for transfers between devices, exchange(): return lax.all_to_all(value, axes, split_axis=0, concat_axis=0, tiled=True)  9.02 us
    ppermute x13, waiting for transfers between devices, permute(): lax.ppermute(value, axes, [(i, i ^ k) for i in range(lax.axis_size(axes))])  8.97 us
    unnamed x24, local copies, waits for them, and re-layouts  6.22 us
  transfers between devices with their start and end apart: 18, of which 2 were waited for; matrix products, arithmetic and copies ran while one was open for 2% of the time, Pallas kernels for 41%

profile of v2, /device:TPU:1, one launch (start us, length us, event | category | flops | bytes accessed | tf_op | source)
XLA Modules:
  0.0 197.3 jit_solution(10971231727348662988)
XLA Ops:
  7.2 1.9 reshape.58.refs_0_.refs_9_.latent_ref
  9.1 1.9 reshape.59.refs_1_
  12.3 9.6 %norm_project.1 = (bf16[1,2,1536,128]{3,2,1,0:T(8,128)(2,1)}, bf16[32,2,48,128]{3,2,1,0:T(8,128)(2,1)}, bf16[1,2,384,128]{3,2,1,0:T(8,128)(2,1)}, bf16[1,2,384,1...) custom-call(bf16[128,1536]{1,0:T(8,128)(2,1)} %reshape.58.refs_0_.re, ...), custom_call_target="tpu_custom_call" | custom-call | flops 7000000000 | bytes 11800580 | tf_op jit(solution)/shard_map/norm_project/pallas_call | solution.py:86
  22.0 1.5 collective-permute-start
  25.2 10.6 %all-to-all-start = ((bf16[32,2,48,128]{3,2,1,0:T(8,128)(2,1)}), bf16[32,2,48,128]{3,2,1,0:T(8,128)(2,1)S(1)}, u32[]{:S(2)}, u32[]{:S(2)}) async-start(bf16[32,2,48,128]{3,2,1,0:T(8,128)(2,1)} %get-tuple-element.74), calls=%async_computation | async-start | bytes 1572864 | tf_op jit(solution)/shard_map/all_to_all | solution.py:682
  37.0 19.8 %scan_height.1 = (bf16[1,2,384,128]{3,2,1,0:T(8,128)(2,1)}, bf16[1,2,384,128]{3,2,1,0:T(8,128)(2,1)}, bf16[1,2,384,128]{3,2,1,0:T(8,128)(2,1)}, bf16[1,2,384,128...) custom-call(s32[8]{0:T(128)} %refs_0_.3, ...), custom_call_target="tpu_custom_call" | custom-call | flops 20000000000 | bytes 1579044 | tf_op jit(solution)/shard_map/scan_height/pallas_call | solution.py:86
  60.0 20.8 %scan_width.1 = (bf16[32,2,48,128]{3,2,1,0:T(8,128)(2,1)}, bf16[128,1536]{1,0:T(8,128)(2,1)}, bf16[128,1536]{1,0:T(8,128)(2,1)}, bf16[128,128]{1,0:T(8,128)(2,1)...) custom-call(s32[64]{0:T(128)} %refs_0_.4, s32[1]{0:T(128)} %bitcast.refs_6_.refs_1_.refs_0_, ...), custom_call_target="tpu_custom_call" | custom-call | flops 20000000000 | bytes 1579268 | tf_op jit(solution)/shard_map/scan_width/pallas_call | solution.py:86
  80.8 9.6 %all-to-all-start.1 = ((bf16[32,2,48,128]{3,2,1,0:T(8,128)(2,1)}), bf16[32,2,48,128]{3,2,1,0:T(8,128)(2,1)S(1)}, u32[]{:S(2)}, u32[]{:S(2)}) async-start(bf16[32,2,48,128]{3,2,1,0:T(8,128)(2,1)} %get-tuple-element.76), calls=%async_computation.1 | async-start | bytes 1572864 | tf_op jit(solution)/shard_map/all_to_all | solution.py:682
  90.4 21.1 %scan_time.1 = (bf16[1,2,1536,128]{3,2,1,0:T(8,128)(2,1)}, bf16[128,1536]{1,0:T(8,128)(2,1)}, bf16[128,1536]{1,0:T(8,128)(2,1)}, bf16[128,128]{1,0:T(8,128)(2,1)...) custom-call(s32[32]{0:T(128)} %refs_0_.5, s32[1]{0:T(128)} %bitcast.refs_6_.refs_1_.refs_0_, ...), custom_call_target="tpu_custom_call" | custom-call | flops 20000000000 | bytes 1579140 | tf_op jit(solution)/shard_map/scan_time/pallas_call | solution.py:86
  112.5 8.5 %sum_project.1 = (bf16[128,1536]{1,0:T(8,128)(2,1)}, f32[128,1536]{1,0:T(8,128)}, bf16[16,208,128]{2,1,0:T(8,128)(2,1)}) custom-call(s32[1]{0:T(128)} %bitcast.refs_6_.refs_1_.refs_0_, bf16[1,2,1536,128]{3,2,1,0:T(8,128)(2,1)} %get-tuple-element.91.refs_2_.refs_1_.refs_0_, bf16[1,2,1536,128]{3,2,1,0:T(8,128)(2,1)} %get-tuple-element.78.refs_2_, ...), custom_call_target="tpu_custom_call" | custom-call | flops 8000000000 | bytes 9148420 | tf_op jit(solution)/shard_map/sum_project/pallas_call | solution.py:86
  121.1 6.7 %all-to-all-start.2 = ((bf16[16,208,128]{2,1,0:T(8,128)(2,1)}), bf16[16,208,128]{2,1,0:T(8,128)(2,1)S(1)}, u32[]{:S(2)}, u32[]{:S(2)}) async-start(bf16[16,208,128]{2,1,0:T(8,128)(2,1)} %get-tuple-element.89), calls=%async_computation.2 | async-start | bytes 1703936 | tf_op jit(solution)/shard_map/all_to_all | solution.py:682
  127.7 4.3 %small_sums.1.refs_2_ = bf16[128,32,128]{2,1,0:T(8,128)(2,1)} custom-call(bf16[1,2,1536,128]{3,2,1,0:T(8,128)(2,1)} %get-tuple-element.91.refs_2_.refs_1_.refs_0_, bf16[128,1536]{1,0:T(8,128)(2,1)} %get-tuple-element.92.refs_1_, bf16[128,1536]{1,0:T(8,128)(2,1)} %get-tuple-element.93.refs_2_, bf16[128,128]{1,0:T(8,128)(2,1)} %get-tuple-element.94.refs_3_, ...), custom_call_target="tpu_custom_call" | custom-call | flops 3000000000 | bytes 3784704 | tf_op jit(solution)/shard_map/small_sums/pallas_call | solution.py:86
  132.1 9.0 %all-to-all-done.2.refs_0_.refs_1_ = bf16[16,208,128]{2,1,0:T(8,128)(2,1)S(1)} async-done(((bf16[16,208,128]{2,1,0:T(8,128)(2,1)}), bf16[16,208,128]{2,1,0:T(8,128)(2,1)S(1)}, u32[]{:S(2)}, u32[]{:S(2)}) %all-to-all-start.2) | async-done | bytes 852000 | tf_op jit(solution)/shard_map/all_to_all | solution.py:682
  142.0 6.2 %in_weight_grad.1 = bf16[128,48,128]{2,1,0:T(8,128)(2,1)} custom-call(bf16[16,208,128]{2,1,0:T(8,128)(2,1)} %copy-done.6, bf16[16,2,128,1536]{3,2,1,0:T(8,128)(2,1)} %bitcast.7, bf16[128,32,128]{2,1,0:T(8,128)(2,1)} %small_sums.1.refs_2_), custom_call_target="tpu_custom_call" | custom-call | flops 3000000000 | bytes 14483456 | tf_op jit(solution)/shard_map/in_weight_grad/pallas_call | solution.py:86
  148.2 8.5 %all-to-all-start.3 = ((bf16[128,48,128]{2,1,0:T(8,128)(2,1)}), bf16[128,48,128]{2,1,0:T(8,128)(2,1)}, u32[]{:S(2)}, u32[]{:S(2)}) async-start(bf16[128,48,128]{2,1,0:T(8,128)(2,1)} %in_weight_grad.1), calls=%async_computation.3 | async-start | bytes 3145728 | tf_op jit(solution)/shard_map/all_to_all | solution.py:682
  156.7 4.7 %out_weight_grad.1 = (bf16[160,128]{1,0:T(8,128)(2,1)}, bf16[160,128]{1,0:T(8,128)(2,1)}, bf16[160,128]{1,0:T(8,128)(2,1)}, bf16[160,128]{1,0:T(8,128)(2,1)}, bf...) custom-call(s32[1]{0:T(128)} %bitcast.5.refs_0_, ...), custom_call_target="tpu_custom_call" | custom-call | flops 4000000000 | bytes 13434884 | tf_op jit(solution)/shard_map/out_weight_grad/pallas_call | solution.py:86
  161.4 3.0 %collective-permute-start.6 = (bf16[160,128]{1,0:T(8,128)(2,1)}, bf16[160,128]{1,0:T(8,128)(2,1)S(1)}, u32[]{:S(2)}, u32[]{:S(2)}) collective-permute-start(bf16[160,128]{1,0:T(8,128)(2,1)} %get-tuple-element.108), channel_id=1, source_target_pairs={{0,16},{16,0},{32,48},{48,32},{64,80},{80,64},{96,112},{112,96},{1... | collective-permute-start | bytes 122888 | tf_op jit(solution)/shard_map/ppermute | solution.py:678
  166.4 1.8 collective-permute-start.10
  168.2 8.9 %collective-permute-done.6.refs_1_ = bf16[160,128]{1,0:T(8,128)(2,1)S(1)} collective-permute-done((bf16[160,128]{1,0:T(8,128)(2,1)}, bf16[160,128]{1,0:T(8,128)(2,1)S(1)}, u32[]{:S(2)}, u32[]{:S(2)}) %collective-permute-start.6) | collective-permute-done | bytes 40992 | tf_op jit(solution)/shard_map/ppermute | solution.py:678
  177.1 1.4 collective-permute-start.11
  179.1 2.3 %copy-done.2 = bf16[1536,1536]{1,0:T(8,128)(2,1)S(1)} copy-done((bf16[1536,1536]{1,0:T(8,128)(2,1)S(1)}, bf16[1536,1536]{1,0:T(8,128)(2,1)}, u32[]{:S(2)}) %copy-start.2) | copy-done | bytes 4718616
  185.3 2.3 %weight_sums.1 = (f32[12,1536]{1,0:T(8,128)}, f32[12,1536]{1,0:T(8,128)}, f32[12,128]{1,0:T(8,128)}, f32[12,128]{1,0:T(8,128)}, f32[24,256]{1,0:T(8,128)}) custom-call(bf16[128,48,128]{2,1,0:T(8,128)(2,1)} %all-to-all-done.3.all_ref, bf16[8,256]{1,0:T(8,128)(2,1)S(1)} %copy-done.1, bf16[160,128]{1,0:T(8,128)(2,1)S(1)} %copy-done.5, ...), custom_call_target="tpu_custom_call" | custom-call | flops 1000000000 | bytes 1904640 | tf_op jit(solution)/shard_map/weight_sums/pallas_call | solution.py:113
  187.6 1.5 slice_reduce_fusion
  189.1 1.4 slice.14
  (58 shorter events, 15.1 us)
Async XLA Ops:
  7.2 133.9 %all-gather.3.cloned.1.call-start = ((), (), s32[]{:S(2)}) async-start(), calls=%async_computation.4 | async-start | bytes 13369344 | tf_op jit(solution)/shard_map/all_gather | solution.py:743
  12.3 23.5 %copy-start.9 = (f32[1536]{0:T(1024)S(1)}, f32[1536]{0:T(1024)}, u32[]{:S(2)}) copy-start(f32[1536]{0:T(1024)} %param.20) | copy-start | bytes 18436
  12.3 24.1 %copy-start.10 = (f32[1536]{0:T(1024)S(1)}, f32[1536]{0:T(1024)}, u32[]{:S(2)}) copy-start(f32[1536]{0:T(1024)} %param.22) | copy-start | bytes 18436
  22.0 15.0 %collective-permute-start = (bf16[1,2,384,128]{3,2,1,0:T(8,128)(2,1)}, bf16[1,2,384,128]{3,2,1,0:T(8,128)(2,1)}, u32[]{:S(2)}, u32[]{:S(2)}) collective-permute-start(bf16[1,2,384,128]{3,2,1,0:T(8,128)(2,1)} %get-tuple-element.67), channel_id=1, source_target_pairs={{0,32},{32,0},{64,96},{96,64},{1,33},{33,1},{65,97},{97,65},{2,34}... | collective-permute-start | bytes 589832 | tf_op jit(solution)/shard_map/ppermute | solution.py:678
  23.5 13.5 %collective-permute-start.1 = (bf16[1,2,384,128]{3,2,1,0:T(8,128)(2,1)}, bf16[1,2,384,128]{3,2,1,0:T(8,128)(2,1)}, u32[]{:S(2)}, u32[]{:S(2)}) collective-permute-start(bf16[1,2,384,128]{3,2,1,0:T(8,128)(2,1)} %get-tuple-element.68), channel_id=1, source_target_pairs={{0,64},{32,96},{64,0},{96,32},{1,65},{33,97},{65,1},{97,33},{2,66}... | collective-permute-start | bytes 589832 | tf_op jit(solution)/shard_map/ppermute | solution.py:678
  24.8 12.2 %collective-permute-start.2 = (bf16[1,2,384,128]{3,2,1,0:T(8,128)(2,1)}, bf16[1,2,384,128]{3,2,1,0:T(8,128)(2,1)}, u32[]{:S(2)}, u32[]{:S(2)}) collective-permute-start(bf16[1,2,384,128]{3,2,1,0:T(8,128)(2,1)} %get-tuple-element.69), channel_id=1, source_target_pairs={{0,96},{32,64},{64,32},{96,0},{1,97},{33,65},{65,33},{97,1},{2,98}... | collective-permute-start | bytes 589832 | tf_op jit(solution)/shard_map/ppermute | solution.py:678
  25.2 33.9 %all-to-all-start = ((bf16[32,2,48,128]{3,2,1,0:T(8,128)(2,1)}), bf16[32,2,48,128]{3,2,1,0:T(8,128)(2,1)S(1)}, u32[]{:S(2)}, u32[]{:S(2)}) async-start(bf16[32,2,48,128]{3,2,1,0:T(8,128)(2,1)} %get-tuple-element.74), calls=%async_computation | async-start | bytes 1572864 | tf_op jit(solution)/shard_map/all_to_all | solution.py:682
  56.9 33.5 %collective-permute-start.3 = (bf16[1,2,384,128]{3,2,1,0:T(8,128)(2,1)}, bf16[1,2,384,128]{3,2,1,0:T(8,128)(2,1)S(1)}, u32[]{:S(2)}, u32[]{:S(2)}) collective-permute-start(bf16[1,2,384,128]{3,2,1,0:T(8,128)(2,1)} %get-tuple-element.71), channel_id=1, source_target_pairs={{0,32},{32,0},{64,96},{96,64},{1,33},{33,1},{65,97},{97,65},{2,34}... | collective-permute-start | bytes 589832 | tf_op jit(solution)/shard_map/ppermute | solution.py:678
  57.4 33.0 %collective-permute-start.4 = (bf16[1,2,384,128]{3,2,1,0:T(8,128)(2,1)}, bf16[1,2,384,128]{3,2,1,0:T(8,128)(2,1)}, u32[]{:S(2)}, u32[]{:S(2)}) collective-permute-start(bf16[1,2,384,128]{3,2,1,0:T(8,128)(2,1)} %get-tuple-element.72), channel_id=1, source_target_pairs={{0,64},{32,96},{64,0},{96,32},{1,65},{33,97},{65,1},{97,33},{2,66}... | collective-permute-start | bytes 589832 | tf_op jit(solution)/shard_map/ppermute | solution.py:678
  57.8 32.6 %collective-permute-start.5 = (bf16[1,2,384,128]{3,2,1,0:T(8,128)(2,1)}, bf16[1,2,384,128]{3,2,1,0:T(8,128)(2,1)}, u32[]{:S(2)}, u32[]{:S(2)}) collective-permute-start(bf16[1,2,384,128]{3,2,1,0:T(8,128)(2,1)} %get-tuple-element.73), channel_id=1, source_target_pairs={{0,96},{32,64},{64,32},{96,0},{1,97},{33,65},{65,33},{97,1},{2,98}... | collective-permute-start | bytes 589832 | tf_op jit(solution)/shard_map/ppermute | solution.py:678
  80.8 30.8 %all-to-all-start.1 = ((bf16[32,2,48,128]{3,2,1,0:T(8,128)(2,1)}), bf16[32,2,48,128]{3,2,1,0:T(8,128)(2,1)S(1)}, u32[]{:S(2)}, u32[]{:S(2)}) async-start(bf16[32,2,48,128]{3,2,1,0:T(8,128)(2,1)} %get-tuple-element.76), calls=%async_computation.1 | async-start | bytes 1572864 | tf_op jit(solution)/shard_map/all_to_all | solution.py:682
  90.4 21.2 %copy-start.11 = (bf16[1,2,384,128]{3,2,1,0:T(8,128)(2,1)}, bf16[1,2,384,128]{3,2,1,0:T(8,128)(2,1)S(1)}, u32[]{:S(2)}) copy-start(bf16[1,2,384,128]{3,2,1,0:T(8,128)(2,1)S(1)} %collective-permute-done.3.refs_5_) | copy-start | bytes 589828
  121.1 20.0 %all-to-all-start.2 = ((bf16[16,208,128]{2,1,0:T(8,128)(2,1)}), bf16[16,208,128]{2,1,0:T(8,128)(2,1)S(1)}, u32[]{:S(2)}, u32[]{:S(2)}) async-start(bf16[16,208,128]{2,1,0:T(8,128)(2,1)} %get-tuple-element.89), calls=%async_computation.2 | async-start | bytes 1703936 | tf_op jit(solution)/shard_map/all_to_all | solution.py:682
  148.2 37.1 %all-to-all-start.3 = ((bf16[128,48,128]{2,1,0:T(8,128)(2,1)}), bf16[128,48,128]{2,1,0:T(8,128)(2,1)}, u32[]{:S(2)}, u32[]{:S(2)}) async-start(bf16[128,48,128]{2,1,0:T(8,128)(2,1)} %in_weight_grad.1), calls=%async_computation.3 | async-start | bytes 3145728 | tf_op jit(solution)/shard_map/all_to_all | solution.py:682
  156.7 22.4 %copy-start = (bf16[128,1536]{1,0:T(8,128)(2,1)S(1)}, bf16[128,1536]{1,0:T(8,128)(2,1)}, u32[]{:S(2)}) copy-start(bf16[128,1536]{1,0:T(8,128)(2,1)} %reshape.58.refs_0_.refs_9_.latent_ref) | copy-start | bytes 1179652
  156.7 22.4 %copy-start.4 = (bf16[128,1536]{1,0:T(8,128)(2,1)S(1)}, bf16[128,1536]{1,0:T(8,128)(2,1)}, u32[]{:S(2)}) copy-start(bf16[128,1536]{1,0:T(8,128)(2,1)} %get-tuple-element.85.mixed_ref) | copy-start | bytes 1179652
  161.4 23.9 %copy-start.1 = (bf16[8,256]{1,0:T(8,128)(2,1)S(1)}, bf16[8,256]{1,0:T(8,128)(2,1)}, u32[]{:S(2)}) copy-start(bf16[8,256]{1,0:T(8,128)(2,1)} %broadcast_in_dim.19.refs_5_.feature_ref) | copy-start | bytes 12292
  161.4 15.7 %collective-permute-start.6 = (bf16[160,128]{1,0:T(8,128)(2,1)}, bf16[160,128]{1,0:T(8,128)(2,1)S(1)}, u32[]{:S(2)}, u32[]{:S(2)}) collective-permute-start(bf16[160,128]{1,0:T(8,128)(2,1)} %get-tuple-element.108), channel_id=1, source_target_pairs={{0,16},{16,0},{32,48},{48,32},{64,80},{80,64},{96,112},{112,96},{1... | collective-permute-start | bytes 122888 | tf_op jit(solution)/shard_map/ppermute | solution.py:678
  164.4 14.2 %collective-permute-start.7 = (bf16[160,128]{1,0:T(8,128)(2,1)}, bf16[160,128]{1,0:T(8,128)(2,1)S(1)}, u32[]{:S(2)}, u32[]{:S(2)}) collective-permute-start(bf16[160,128]{1,0:T(8,128)(2,1)} %get-tuple-element.109), channel_id=1, source_target_pairs={{0,32},{16,48},{32,0},{48,16},{64,96},{80,112},{96,64},{112,80},{1... | collective-permute-start | bytes 122888 | tf_op jit(solution)/shard_map/ppermute | solution.py:678
  165.0 20.3 %collective-permute-start.8 = (bf16[160,128]{1,0:T(8,128)(2,1)}, bf16[160,128]{1,0:T(8,128)(2,1)S(1)}, u32[]{:S(2)}, u32[]{:S(2)}) collective-permute-start(bf16[160,128]{1,0:T(8,128)(2,1)} %get-tuple-element.110), channel_id=1, source_target_pairs={{0,48},{16,32},{32,16},{48,0},{64,112},{80,96},{96,80},{112,64},{1... | collective-permute-start | bytes 122888 | tf_op jit(solution)/shard_map/ppermute | solution.py:678
  166.0 19.3 %collective-permute-start.9 = (bf16[160,128]{1,0:T(8,128)(2,1)}, bf16[160,128]{1,0:T(8,128)(2,1)S(1)}, u32[]{:S(2)}, u32[]{:S(2)}) collective-permute-start(bf16[160,128]{1,0:T(8,128)(2,1)} %get-tuple-element.111), channel_id=1, source_target_pairs={{0,64},{16,80},{32,96},{48,112},{64,0},{80,16},{96,32},{112,48},{1... | collective-permute-start | bytes 122888 | tf_op jit(solution)/shard_map/ppermute | solution.py:678
  166.4 18.9 %collective-permute-start.10 = (bf16[160,128]{1,0:T(8,128)(2,1)}, bf16[160,128]{1,0:T(8,128)(2,1)S(1)}, u32[]{:S(2)}, u32[]{:S(2)}) collective-permute-start(bf16[160,128]{1,0:T(8,128)(2,1)} %get-tuple-element.112), channel_id=1, source_target_pairs={{0,80},{16,64},{32,112},{48,96},{64,16},{80,0},{96,48},{112,32},{1... | collective-permute-start | bytes 122888 | tf_op jit(solution)/shard_map/ppermute | solution.py:678
  177.1 8.2 %collective-permute-start.11 = (bf16[160,128]{1,0:T(8,128)(2,1)}, bf16[160,128]{1,0:T(8,128)(2,1)S(1)}, u32[]{:S(2)}, u32[]{:S(2)}) collective-permute-start(bf16[160,128]{1,0:T(8,128)(2,1)} %get-tuple-element.113), channel_id=1, source_target_pairs={{0,96},{16,112},{32,64},{48,80},{64,32},{80,48},{96,0},{112,16},{1... | collective-permute-start | bytes 122888 | tf_op jit(solution)/shard_map/ppermute | solution.py:678
  178.5 6.8 %collective-permute-start.12 = (bf16[160,128]{1,0:T(8,128)(2,1)}, bf16[160,128]{1,0:T(8,128)(2,1)S(1)}, u32[]{:S(2)}, u32[]{:S(2)}) collective-permute-start(bf16[160,128]{1,0:T(8,128)(2,1)} %get-tuple-element.114), channel_id=1, source_target_pairs={{0,112},{16,96},{32,80},{48,64},{64,48},{80,32},{96,16},{112,0},{1... | collective-permute-start | bytes 122888 | tf_op jit(solution)/shard_map/ppermute | solution.py:678
  (6 other events, 8.9 us)
Sparse Core Ops, SparseCore 0:
  22.1 109.1 all-gather.2

commit v3 on v2

--- a/solution.py
+++ b/solution.py
@@ -12,7 +12,8 @@
 BF = jnp.bfloat16
 F32 = jnp.float32
 LANES = 128
-GROUP = 4
+GROUP = 6
+EIGHT = 9
 LOG2E = math.log2(math.e)
 MEGA = 1024 * 1024
 VMEM_ALL = 63
@@ -39,7 +40,7 @@
     return functools.reduce(lambda a, b: a + b, terms)
 
 
-def call(kernel, name, out_shape, scratch, vmem, flops, args, smem=(), late=(), pieces=None, choose=None):
+def call(kernel, name, out_shape, scratch, vmem, flops, args, smem=(), late=(), pieces=None, choose=None, early=()):
     moved = [i for i in range(len(args)) if i not in smem]
     pieces, choose = pieces or {}, choose or {}
     held_shape = {
@@ -71,12 +72,19 @@
             if i not in late:
                 copy.wait()
         waits = (lambda i, n=0: copies[i, n].wait(),) if late else ()
-        kernel(*waits, *views, *made, *rest[:-2])
-        sent = [
-            pltpu.make_async_copy(made[n], out[n], out_sem.at[n]) for n in range(len(out_shape))
-        ]
-        for copy in sent:
+        sent = []
+
+        def send(n, plane=None):
+            at = (slice(None), plane) if plane is not None else (slice(None),)
+            place = 2 * n + (plane or 0)
+            copy = pltpu.make_async_copy(made[n].at[at], out[n].at[at], out_sem.at[place])
             copy.start()
+            sent.append(copy)
+
+        kernel(*waits, *((send,) if early else ()), *views, *made, *rest[:-2])
+        for n in range(len(out_shape)):
+            if n not in early:
+                send(n)
         for copy in sent:
             copy.wait()
 
@@ -91,7 +99,7 @@
         scratch_shapes=[pltpu.VMEM(held_shape[i], args[i].dtype) for i in moved]
         + [pltpu.VMEM(s, d) for s, d in out_shape]
         + [pltpu.VMEM(s, d) for s, d in scratch]
-        + [pltpu.SemaphoreType.DMA((len(cuts),)), pltpu.SemaphoreType.DMA((len(out_shape),))],
+        + [pltpu.SemaphoreType.DMA((len(cuts),)), pltpu.SemaphoreType.DMA((2 * len(out_shape),))],
         compiler_params=pltpu.CompilerParams(vmem_limit_bytes=vmem * MEGA),
         cost_estimate=cost(flops, args),
         name=name,
@@ -142,6 +150,7 @@
 
 def pre_kernel(
     wait,
+    send,
     latent_ref,
     grad_ref,
     w_in_ref,
@@ -158,6 +167,7 @@
     both_ref,
     pre_ref,
     mod_ref,
+    cot_ref,
     flat_ref,
 ):
     tokens, width = latent_ref.shape
@@ -166,17 +176,20 @@
         feature_ref[...], w_mod_ref[...], NT, preferred_element_type=F32
     )
     mod_ref[...] = modulation
+    send(8)
     normed, _ = normalise(latent_ref[...])
     shifted = (normed * (1.0 + modulation[:1, width:]) + modulation[:1, :width]).astype(BF)
     both_ref[0] = shifted
+    wait(1)
     both_ref[1] = grad_ref[...]
+    send(6)
     wait(2)
     pre_act = jnp.dot(shifted, w_in_ref[...], preferred_element_type=F32)
     pre_ref[...] = pre_act
+    send(7)
     activ = (pre_act * jax.nn.sigmoid(pre_act)).astype(BF)
-    wait(3)
-    cot = lax.dot_general(grad_ref[...], w_out_ref[...], NT, preferred_element_type=F32).astype(BF)
-    for which, value in enumerate((activ, cot)):
+
+    def pack(which, value):
         wide = value.astype(F32)
         for j in range(tiles):
             to_flat(flat_ref, j, wide[:, cut(j)], tiles)
@@ -187,6 +200,15 @@
             chunk = ref.shape[2]
             begin = pl.multiple_of((place_ref[0] ^ k) * chunk, chunk)
             ref[0, which] = flat_ref[pl.ds(begin, chunk), :].astype(BF)
+        for n in range(6):
+            send(n, which)
+
+    pack(0, activ)
+    wait(3)
+    cot = lax.dot_general(grad_ref[...], w_out_ref[...], NT, preferred_element_type=F32).astype(BF)
+    cot_ref[...] = cot
+    send(9)
+    pack(1, cot)
 
 
 def parts_of(refs):
@@ -210,6 +232,8 @@
     length,
     row_of,
     pieces,
+    wait,
+    send,
     order_ref,
     place_ref,
     *refs,
@@ -224,7 +248,21 @@
         *refs[pieces : pieces + 4],
         out_refs,
         *refs[2 * pieces + 4 :],
-    )
+        functools.partial(wait_for, wait, 2 + pieces),
+        functools.partial(send_from, send, pieces),
+    )
+
+
+def wait_for(wait, first, n):
+    wait(first + n)
+
+
+def send_from(send, pieces, n):
+    if n < 2:
+        for k in range(pieces):
+            send(k, n)
+    else:
+        send(pieces + n - 2)
 
 
 def scan_steps(
@@ -255,11 +293,14 @@
     gb_ref,
     gc_ref,
     hist_ref,
+    keep_ref,
     y8_ref,
     u8_ref,
     v8_ref,
     rate2_ref,
     rate_ref,
+    wait,
+    send,
 ):
     tokens, inner = xf_ref.shape
     tiles = inner // LANES
@@ -273,18 +314,23 @@
         xf_ref[:, cut(j)] = from_flat(x_row_ref, j, tokens, tiles)
     x = xf_ref[...].astype(BF)
     x_ref[...] = x
+    send(2)
+    wait(0)
     select = jnp.dot(x, wsel_ref[...], preferred_element_type=F32)
     lane = lax.broadcasted_iota(jnp.int32, (tokens, LANES), 1)
     low = jnp.where(lane < rank, select, 0.0).astype(BF)
     low_ref[...] = low
+    send(4)
+    wait(1)
     w_dt = jnp.concatenate([wdt_ref[...], jnp.zeros((2 * states, inner), BF)], axis=0)
-    pre = jnp.dot(low, w_dt, preferred_element_type=F32) + bias_ref[...]
+    pre = jnp.dot(low, w_dt, preferred_element_type=F32) + bias_ref[:1, :]
     pre_ref[...] = pre
     spacing = jnp.maximum(pre, 0.0) + jnp.log1p(jnp.exp(-jnp.abs(pre)))
     dt_ref[...] = spacing
     for j in range(tiles):
-        to_flat(dt_row_ref, j, spacing[:, cut(j)], tiles)
-    dx_row_ref[...] = dt_row_ref[...] * x_row_ref[...]
+        at = slice(j * tokens, (j + 1) * tokens)
+        dt_row_ref[at, :] = spacing[:, cut(j)]
+        dx_row_ref[at, :] = spacing[:, cut(j)] * xf_ref[:, cut(j)]
     rates = -jnp.exp(alog_ref[...])
     rate_ref[...] = rates
     rate2_ref[...] = rates * LOG2E
@@ -314,18 +360,20 @@
                 row = row_of(order_ref[step], line, place_ref[0])
                 at = pl.ds(pl.multiple_of(row * states, states), states)
                 slot = pl.ds(pl.multiple_of((step + 1) * states, states), states)
-                return row * tiles + first, pl.multiple_of(row * 8, 8), at, slot
+                return row, row * EIGHT, at, slot
 
             def forward(step, carry):
                 row, at_8, at, slot = places(step)
                 bb, cb = bb_ref[at, :], cb_ref[at, :]
                 new = []
                 for j in range(GROUP):
-                    dt = dt_row_ref[pl.ds(row + j, 1), :]
-                    dx = dx_row_ref[pl.ds(row + j, 1), :]
-                    h = jnp.exp2(rate2[j] * dt) * carry[j] + bb * dx
+                    dt = dt_row_ref[pl.ds(row + (first + j) * tokens, 1), :]
+                    dx = dx_row_ref[pl.ds(row + (first + j) * tokens, 1), :]
+                    decay = jnp.exp2(rate2[j] * dt)
+                    keep_ref[slot, cut(j)] = decay
+                    h = decay * carry[j] + bb * dx
                     hist_ref[slot, cut(j)] = h
-                    y8_ref[pl.ds(at_8 + 8 * tokens * j, 8), :] = fold(h * cb)
+                    y8_ref[pl.ds(at_8 + EIGHT * tokens * j, 8), :] = fold(h * cb)
                     new.append(h)
                 return tuple(new)
 
@@ -341,16 +389,16 @@
                 gc = gc_ref[at, :]
                 new, acc_new = [], []
                 for j in range(GROUP):
-                    dt = dt_row_ref[pl.ds(row + j, 1), :]
-                    dx = dx_row_ref[pl.ds(row + j, 1), :]
-                    dy = dy_row_ref[pl.ds(row + j, 1), :]
+                    dt = dt_row_ref[pl.ds(row + (first + j) * tokens, 1), :]
+                    dx = dx_row_ref[pl.ds(row + (first + j) * tokens, 1), :]
+                    dy = dy_row_ref[pl.ds(row * tiles + first + j, 1), :]
                     g = pend[j] + cb * dy
                     gc = gc + hist_ref[slot, cut(j)] * dy
-                    u8_ref[pl.ds(at_8 + 8 * tokens * j, 8), :] = fold(g * bb)
+                    u8_ref[pl.ds(at_8 + EIGHT * tokens * j, 8), :] = fold(g * bb)
                     gb = gb + g * dx
-                    p = jnp.exp2(rate2[j] * dt) * g
+                    p = keep_ref[slot, cut(j)] * g
                     w = p * hist_ref[prev, cut(j)]
-                    v8_ref[pl.ds(at_8 + 8 * tokens * j, 8), :] = fold(w * rate1[j])
+                    v8_ref[pl.ds(at_8 + EIGHT * tokens * j, 8), :] = fold(w * rate1[j])
                     acc_new.append(acc[j] + w * dt)
                     new.append(p)
                 gb_ref[at, :] = gb
@@ -368,8 +416,8 @@
             rows = pl.ds(pl.multiple_of(block * 8, 8), 8)
 
             def summed(ref, j):
-                begin = block * 64 + 8 * tokens * j
-                return total([ref[pl.ds(begin + r, 8, stride=8), :] for r in range(8)])
+                begin = block * (8 * EIGHT) + EIGHT * tokens * j
+                return total([ref[pl.ds(begin + r, 8, stride=EIGHT), :] for r in range(8)])
 
             for j in range(GROUP):
                 c = cuts[j]
@@ -384,39 +432,54 @@
 
     for ref, at in parts_of(out_refs):
         write_part(ref, 0, x_row_ref[at, :])
+    send(0)
     grad_pre = pre_ref[...]
     gvec_ref[states:, :] = jnp.broadcast_to(
         jnp.sum(grad_pre, axis=0, keepdims=True), (8, inner)
     )
+    send(6)
     grad_pre_b = grad_pre.astype(BF)
     grad_pre_ref[...] = grad_pre_b
-    ones = jnp.ones((LANES, LANES), BF)
-
-    def lane_total(ref):
-        value = ref[...]
-        top = value.astype(BF)
-        rest = (value - top.astype(F32)).astype(BF)
-        return jnp.dot(top, ones, preferred_element_type=F32) + jnp.dot(
-            rest, ones, preferred_element_type=F32
-        )
-
+    send(3)
+    shape = (2 * LANES, LANES)
+    half = lax.broadcasted_iota(jnp.int32, shape, 0) // LANES
+    lane_at = lax.broadcasted_iota(jnp.int32, shape, 1)
+    spread = jnp.where((lane_at - rank) // states == half, 1.0, 0.0).astype(BF)
     shape = (tokens * states, LANES)
     state_at = lax.broadcasted_iota(jnp.int32, shape, 0) % states
     lane_at = lax.broadcasted_iota(jnp.int32, shape, 1)
-    gb_ref[...] = jnp.where(lane_at == state_at + rank, lane_total(gb_ref), 0.0) + jnp.where(
-        lane_at == state_at + rank + states, lane_total(gc_ref), 0.0
-    )
-    grad_maps = total([gb_ref[pl.ds(n, tokens, stride=states), :] for n in range(states)])
+    both = jnp.concatenate([gb_ref[...], gc_ref[...]], axis=1)
+    lanes = halves_product(both, spread, False)
+    kept = jnp.where((lane_at >= rank) & ((lane_at - rank) % states == state_at), lanes, 0.0)
+    shape = (tokens, tokens * states)
+    collect = lax.broadcasted_iota(jnp.int32, shape, 1) // states == lax.broadcasted_iota(
+        jnp.int32, shape, 0
+    )
+    grad_maps = halves_product(kept, jnp.where(collect, 1.0, 0.0).astype(BF), True)
     grad_low = lax.dot_general(grad_pre_b, w_dt, NT, preferred_element_type=F32)
     grad_select_out = (grad_low + grad_maps).astype(BF)
     grad_low_ref[...] = grad_select_out
+    send(5)
     back = dt_ref[...] + lax.dot_general(
         grad_select_out, wsel_ref[...], NT, preferred_element_type=F32
     )
     for j in range(tiles):
-        to_flat(x_row_ref, j, back[:, cut(j)], tiles)
+        to_flat(dy_row_ref, j, back[:, cut(j)], tiles)
     for ref, at in parts_of(out_refs):
-        write_part(ref, 1, x_row_ref[at, :])
+        write_part(ref, 1, dy_row_ref[at, :])
+    send(1)
+
+
+def halves_product(value, other, other_first):
+    top = value.astype(BF)
+    rest = (value - top.astype(F32)).astype(BF)
+    if other_first:
+        return jnp.dot(other, top, preferred_element_type=F32) + jnp.dot(
+            other, rest, preferred_element_type=F32
+        )
+    return jnp.dot(top, other, preferred_element_type=F32) + jnp.dot(
+        rest, other, preferred_element_type=F32
+    )
 
 
 def direction(name, length, row_of, order, place, data, params):
@@ -427,7 +490,7 @@
     plane = ((tokens, inner), F32)
     flat = ((tokens * tiles, LANES), F32)
     maps = ((tokens * states, LANES), F32)
-    eights = ((tokens * 8 * GROUP, LANES), F32)
+    eights = ((tokens * EIGHT * GROUP, LANES), F32)
     results = call(
         functools.partial(scan_kernel, length, row_of, len(data)),
         name,
@@ -438,20 +501,22 @@
         [plane] * 3
         + [flat] * 4
         + [maps] * 4
-        + [(((length + 1) * states, GROUP * LANES), F32)]
+        + [(((length + 1) * states, GROUP * LANES), F32)] * 2
         + [eights] * 3
         + [((states, inner), F32)] * 2,
         VMEM_ALL,
         2e10,
         (order, place, *data, *params),
         smem=(0, 1),
+        late=tuple(2 + len(data) + i for i in (0, 1)),
+        early=tuple(range(len(data) + 5)),
     )
     return results[: len(data)], results[len(data) :]
 
 
 def small_kernel(own_ref, *refs):
     found, refs = [refs[5 * d : 5 * d + 5] for d in range(3)], refs[15:]
-    send_ref, row_ref, turned_ref = refs
+    send_ref, row_ref, turned_ref, held_ref = refs
     inner = found[0][0].shape[1]
     tiles = inner // LANES
     tokens = own_ref.shape[2] // tiles
@@ -477,29 +542,31 @@
     vectors = jnp.where(at > rank + states, 0.0, vectors) + jnp.where(
         at == rank + states + 1, jnp.broadcast_to(skips, at.shape), 0.0
     )
-    turned_ref[0, :inner] = lax.dot_general(x, grad_low, TN, preferred_element_type=F32)
-    turned_ref[1, :inner] = vectors.T + lax.dot_general(
+    turned_ref[0] = lax.dot_general(x, grad_low, TN, preferred_element_type=F32)
+    turned_ref[1] = vectors.T + lax.dot_general(
         grad_pre, low, TN, preferred_element_type=F32
     )
-    turned_ref[:, inner:] = jnp.zeros((2, SLOT - own, LANES), F32)
     for d in range(send_ref.shape[0]):
         for which in (0, 1):
-            send_ref[d, which * SLOT : (which + 1) * SLOT] = turned_ref[
-                which, d * own : d * own + SLOT
-            ].astype(BF)
-
-
-def spread_rows(ref, which, m, own, near):
-    return jnp.concatenate(
-        [ref[which, pl.ds(m * own + i, FAR_SIZE, stride=near * own), :] for i in range(own)],
-        axis=0,
-    ).astype(BF)
+            begin = (2 * d + which) * own
+            held_ref[begin : begin + own, :] = turned_ref[which, d * own : (d + 1) * own, :]
+    send_ref[...] = held_ref[...].reshape(send_ref.shape).astype(BF)
+
+
+def spread_rows(ref, which, own, near, held_ref):
+    for m in range(near):
+        for o in range(FAR_SIZE):
+            begin = (o * near + m) * own
+            at = (m * FAR_SIZE + o) * own
+            held_ref[at : at + own, :] = ref[which, begin : begin + own, :]
+    return held_ref[...].reshape(near, FAR_SIZE * own, LANES).astype(BF)
 
 
 def post_kernel(
-    wait,
+    send,
     place_ref,
-    own_ref,
+    activ_ref,
+    cot_ref,
     time_ref,
     wide_ref,
     slot_0_ref,
@@ -507,28 +574,22 @@
     slot_2_ref,
     slot_3_ref,
     pre_ref,
-    latent_ref,
-    mod_ref,
     skip_ref,
-    w_in_ref,
     mixed_out_ref,
-    normed_grad_ref,
+    grad_act_ref,
     send_ref,
     sum_ref,
-    own_row_ref,
-    plane_ref,
     turned_ref,
-    vec_ref,
+    held_ref,
 ):
-    tokens, width = latent_ref.shape
-    inner = w_in_ref.shape[1]
+    tokens, inner = pre_ref.shape
     tiles = inner // LANES
     flat_shape = (tokens * tiles, LANES)
     near = send_ref.shape[0]
     near_rows = inner // near
     own = near_rows // FAR_SIZE
 
-    def summed(which):
+    def summed(which, own_ref):
         sum_ref[...] = time_ref[0, which].astype(F32) + wide_ref[:, which].reshape(
             flat_shape
         ).astype(F32)
@@ -536,22 +597,43 @@
             chunk = ref.shape[2]
             at = pl.ds(pl.multiple_of((place_ref[0] ^ k) * chunk, chunk), chunk)
             sum_ref[at, :] += ref[0, which].astype(F32)
-        own_row_ref[...] = own_ref[0, which].astype(F32)
-        for j in range(tiles):
-            mine = from_flat(own_row_ref, j, tokens, tiles)
-            plane_ref[:, cut(j)] = from_flat(sum_ref, j, tokens, tiles) + skip_ref[:, cut(j)] * mine
-
-    summed(1)
+        scans = jnp.concatenate([from_flat(sum_ref, j, tokens, tiles) for j in range(tiles)], axis=1)
+        return scans + skip_ref[1:, :] * own_ref[...].astype(F32)
+
+    back = summed(1, cot_ref)
     pre_act = pre_ref[...]
     gate = jax.nn.sigmoid(pre_act)
-    grad_act = (plane_ref[...] * gate * (1.0 + pre_act * (1.0 - gate))).astype(BF)
-    summed(0)
-    mixed = plane_ref[...].astype(BF)
+    grad_act = (back * gate * (1.0 + pre_act * (1.0 - gate))).astype(BF)
+    grad_act_ref[...] = grad_act
+    send(1)
+    turned_ref[1] = grad_act.astype(F32).T
+    mixed = summed(0, activ_ref).astype(BF)
     mixed_out_ref[...] = mixed
-    wait(12)
-    grad_shifted = lax.dot_general(grad_act, w_in_ref[...], NT, preferred_element_type=F32)
-    normed, _ = normalise(latent_ref[...])
-    normed_grad_ref[...] = grad_shifted * (1.0 + mod_ref[:1, width:])
+    send(0)
+    turned_ref[0] = mixed.astype(F32).T
+    send_ref[:, :near_rows] = spread_rows(turned_ref, 0, own, near, held_ref)
+    for m in range(near):
+        send_ref[m, near_rows:] = turned_ref[1, pl.ds(m * near_rows, near_rows), :].astype(BF)
+
+
+def finish_kernel(
+    wait,
+    mixed_ref,
+    grad_act_ref,
+    latent_ref,
+    mod_ref,
+    w_in_ref,
+    w_out_ref,
+    branch_ref,
+    latent_grad_ref,
+    vec_ref,
+):
+    tokens, width = latent_ref.shape
+    normed, inverse = normalise(latent_ref[...])
+    wait(4)
+    grad_shifted = lax.dot_general(
+        grad_act_ref[...], w_in_ref[...], NT, preferred_element_type=F32
+    )
     grad_vec = jnp.concatenate(
         [
             jnp.sum(grad_shifted, axis=0, keepdims=True),
@@ -559,43 +641,24 @@
         ],
         axis=1,
     )
-    devices = near * FAR_SIZE
-    part = 2 * own
+    devices = vec_ref.shape[0]
+    part = 2 * width // devices
     shape = (devices, 2 * width)
     block_at = lax.broadcasted_iota(jnp.int32, shape, 0) * part
     column_at = lax.broadcasted_iota(jnp.int32, shape, 1)
     mine = (column_at >= block_at) & (column_at < block_at + part)
     chosen = jnp.where(mine, jnp.broadcast_to(grad_vec, shape), 0.0)
-    top = chosen.astype(BF)
-    rest = (chosen - top.astype(F32)).astype(BF)
     lane_at = lax.broadcasted_iota(jnp.int32, (2 * width, LANES), 1)
     place = lax.broadcasted_iota(jnp.int32, (2 * width, LANES), 0) % part
     choose = jnp.where(lane_at == place, 1.0, 0.0).astype(BF)
-    vec_ref[...] = jnp.dot(top, choose, preferred_element_type=F32) + jnp.dot(
-        rest, choose, preferred_element_type=F32
-    )
-    turned_ref[0] = mixed.astype(F32).T
-    turned_ref[1] = grad_act.astype(F32).T
-    for m in range(near):
-        send_ref[m, :near_rows] = spread_rows(turned_ref, 0, m, own, near)
-        send_ref[m, near_rows : 2 * near_rows] = turned_ref[
-            1, pl.ds(m * near_rows, near_rows), :
-        ].astype(BF)
-        send_ref[m, 2 * near_rows :] = jnp.concatenate(
-            [vec_ref[pl.ds(m, FAR_SIZE, stride=near), :], jnp.zeros((8, LANES), F32)], axis=0
-        ).astype(BF)
-
-
-def finish_kernel(
-    mixed_ref, normed_grad_ref, latent_ref, w_out_ref, branch_ref, latent_grad_ref
-):
+    vec_ref[...] = halves_product(chosen, choose, False)
+    grad_normed = grad_shifted * (1.0 + mod_ref[:1, width:])
+    product = jnp.mean(grad_normed * normed, axis=1, keepdims=True)
+    latent_grad_ref[...] = (inverse * (grad_normed - normed * product)).astype(BF)
+    wait(5)
     branch_ref[...] = jnp.dot(
         mixed_ref[...], w_out_ref[...], preferred_element_type=F32
     ).astype(BF)
-    normed, inverse = normalise(latent_ref[...])
-    grad_normed = normed_grad_ref[...]
-    product = jnp.mean(grad_normed * normed, axis=1, keepdims=True)
-    latent_grad_ref[...] = (inverse * (grad_normed - normed * product)).astype(BF)
 
 
 def long_product(wait, at, left, right_ref):
@@ -610,20 +673,22 @@
     return total(terms)
 
 
-def in_grad_kernel(wait, recv_ref, both_ref, small_ref, all_ref, right_ref, rows_ref):
+def in_grad_kernel(wait, recv_ref, both_ref, small_ref, vec_ref, all_ref, right_ref, rows_ref):
     near = recv_ref.shape[0]
     rows = right_ref.shape[0]
     width = both_ref.shape[2]
+    devices = all_ref.shape[0]
     own = rows // FAR_SIZE
     for s in range(near):
-        right_ref[:, cut(s)] = recv_ref[s, rows : 2 * rows]
+        right_ref[:, cut(s)] = recv_ref[s, rows:]
     all_ref[:, SLOT:] = small_ref[...]
     product = long_product(wait, 1, right_ref, both_ref)
     turned = jnp.concatenate([product, jnp.zeros((LANES - rows, width), F32)], axis=0).T
-    rows_ref[:width] = turned
-    rows_ref[width:] = jnp.zeros((rows_ref.shape[0] - width, LANES), F32)
-    for d in range(all_ref.shape[0]):
-        all_ref[d, :SLOT] = rows_ref[pl.ds(d * own, SLOT), :].astype(BF)
+    for d in range(devices):
+        rows_ref[d * SLOT : d * SLOT + own, :] = turned[d * own : (d + 1) * own]
+    for n in range(own, SLOT):
+        rows_ref[pl.ds(n, devices, stride=SLOT), :] = vec_ref[...]
+    all_ref[:, :SLOT] = rows_ref[...].reshape(devices, SLOT, LANES).astype(BF)
 
 
 def out_grad_kernel(wait, place_ref, recv_ref, both_ref, *refs):
@@ -636,22 +701,20 @@
     own = rows // far
     for s in range(near):
         left_ref[:, cut(s)] = recv_ref[s, :rows]
-    vec = total([recv_ref[s, 2 * rows :].astype(F32) for s in range(near)])
-    base = own * tiles
-    for o in range(far):
-        out_ref[o, base:, :] = jnp.broadcast_to(vec[o : o + 1], (SLOT, LANES))
     product = long_product(wait, 2, left_ref, both_ref)
     for j in range(tiles):
         half_ref[...] = product[:, cut(j)]
         for o in range(far):
-            out_ref[o, pl.ds(j, own, stride=tiles), :] = half_ref[pl.ds(o, own, stride=far), :]
+            out_ref[o, pl.ds(j, own, stride=tiles), :] = half_ref[o * own : (o + 1) * own, :]
     for k, ref in enumerate(far_refs):
         ref[...] = out_ref[place_ref[0] ^ k].astype(BF)
 
 
 def last_kernel(all_ref, feature_ref, *refs):
     far_refs = refs[:FAR_SIZE]
-    gwo_ref, gwi_ref, gsel_ref, small_ref, gmod_ref, sum_ref, rest_ref = refs[FAR_SIZE:]
+    gwo_ref, gwi_ref, gsel_ref, gdt_ref, galog_ref, gvec_ref, gmod_ref, sum_ref, rest_ref = refs[
+        FAR_SIZE:
+    ]
     far = FAR_SIZE
     own, width = gwo_ref.shape
     tiles = width // LANES
@@ -660,16 +723,22 @@
     sum_ref[...] = total([ref[...].astype(F32) for ref in far_refs])
     for j in range(tiles):
         gwo_ref[:, cut(j)] = sum_ref[pl.ds(j, own, stride=tiles), :]
-    vec = sum_ref[own * tiles : own * tiles + 8, :].T
-    gmod_ref[...] = vec[: 2 * own, :1] * feature_ref[:1, :].astype(F32)
     rest = []
     for m in range(near):
         block = total([all_ref[o * near + m].astype(F32) for o in range(far)])
         gwi_ref[:, part * m : part * (m + 1)] = block[:own, :part]
-        rest.append(block[SLOT:])
+        rest.append(block)
     rest_ref[...] = total(rest)
-    gsel_ref[...] = rest_ref[:own, :]
-    small_ref[...] = rest_ref[SLOT : SLOT + own, :]
+    vec = rest_ref[own : own + 1, :]
+    turned = jnp.broadcast_to(vec, (LANES, LANES)).T
+    gmod_ref[...] = turned[: 2 * own, :1] * feature_ref[:1, :].astype(F32)
+    gsel_ref[...] = rest_ref[SLOT : SLOT + own, :]
+    rank, states = gdt_ref.shape[1], galog_ref.shape[1]
+    base = SLOT + own
+    gdt_ref[...] = rest_ref[base : base + own, :rank]
+    galog_ref[...] = rest_ref[base : base + own, rank : rank + states]
+    turned = jnp.concatenate([rest_ref[base : base + own, :], jnp.zeros((LANES - own, LANES), F32)])
+    gvec_ref[...] = turned.T[rank + states : rank + states + 8, :own]
 
 
 def permute(value, axes, k):
@@ -717,7 +786,7 @@
     slot = ((1, 2, tokens * tiles // n_row, LANES), BF)
     place = lax.axis_index(ROW).astype(jnp.int32)[None]
     far_place = lax.axis_index(FAR).astype(jnp.int32)[None]
-    data_own, data_wide, *slots, both, pre_act, modulation = call(
+    data_own, data_wide, *slots, both, pre_act, modulation, cot = call(
         pre_kernel,
         "norm_project",
         [
@@ -730,21 +799,24 @@
             ((2, tokens, width), BF),
             ((tokens, inner), F32),
             ((8, 2 * width), F32),
+            ((tokens, inner), BF),
         ],
         [((tokens * tiles, LANES), F32)],
         VMEM_ALL,
         7e9,
         (flat_latent, flat_grad, w_in, w_out, w_mod, feature_rows, place),
         smem=(6,),
-        late=(2, 3),
+        late=(1, 2, 3),
+        early=tuple(range(10)),
     )
     data_wide = exchange(data_wide, COL)
     slots = [permute(value, ROW, k) for k, value in enumerate(slots)]
     both_near = lax.all_gather(both, NEAR, axis=0, tiled=False)
+    vectors = jnp.stack([dt_bias, d_skip])
     params = (
         w_select,
         w_dt.T,
-        dt_bias[None, :],
+        vectors,
         a_log.T,
     )
     area = rows * cols
@@ -783,67 +855,60 @@
     (out_time,), grads_time = direction(
         "scan_time", frames, time_row, frame_order, place, [data_time], params
     )
-    mixed, normed_grad, near_send = call(
+    mixed, grad_act, near_send = call(
         post_kernel,
-        "sum_project",
+        "sum_directions",
         [
             ((tokens, inner), BF),
-            ((tokens, width), F32),
-            ((near, 2 * inner // near + 16, LANES), BF),
+            ((tokens, inner), BF),
+            ((near, 2 * inner // near, LANES), BF),
         ],
         [
             ((tokens * tiles, LANES), F32),
-            ((tokens * tiles, LANES), F32),
-            ((tokens, inner), F32),
             ((2, inner, LANES), F32),
-            ((near * far, LANES), F32),
+            ((inner, LANES), F32),
         ],
         VMEM_ALL,
-        8e9,
-        (
-            place,
-            data_own,
-            out_time,
-            out_wide,
-            *out_slots,
-            pre_act,
-            flat_latent,
-            modulation,
-            d_skip[None, :],
-            w_in,
-        ),
+        6e9,
+        (place, grads_time[0], cot, out_time, out_wide, *out_slots, pre_act, vectors),
         smem=(0,),
-        late=(12,),
+        early=(0, 1),
     )
     near_recv = exchange(near_send, NEAR)
     data_own, _ = lax.optimization_barrier((data_own, near_send))
     small_send = call(
         small_kernel,
         "small_sums",
-        [((near * far, 2 * SLOT, LANES), BF)],
-        [((tokens * tiles, LANES), F32), ((2, inner + SLOT - own, LANES), F32)],
+        [((near * far, 2 * own, LANES), BF)],
+        [
+            ((tokens * tiles, LANES), F32),
+            ((2, inner, LANES), F32),
+            ((2 * inner, LANES), F32),
+        ],
         VMEM_ALL,
         3e9,
         (data_own, *grads_time, *grads_wide, *grads_tall),
     )[0]
-    branch, latent_grad = plain_call(
+    branch, latent_grad, vec = call(
         finish_kernel,
-        "out_project",
-        [((tokens, width), BF), ((tokens, width), BF)],
+        "out_projections",
+        [((tokens, width), BF), ((tokens, width), BF), ((near * far, LANES), F32)],
         [],
-        24,
-        2e9,
-        (mixed, normed_grad, flat_latent, w_out),
-    )
-    piece = own * tiles + SLOT
+        VMEM_ALL,
+        6e9,
+        (mixed, grad_act, flat_latent, modulation, w_in, w_out),
+        late=(4, 5),
+    )
+    near_recv, vec, small_send = lax.optimization_barrier((near_recv, vec, small_send))
+    piece = own * tiles
     all_send = call(
         in_grad_kernel,
         "in_weight_grad",
-        [((near * far, 3 * SLOT, LANES), BF)],
-        [((inner // near, near * tokens), BF), ((width + SLOT - own, LANES), F32)],
+        [((near * far, SLOT + 2 * own, LANES), BF)],
+        [((inner // near, near * tokens), BF), ((near * far * SLOT, LANES), F32)],
         VMEM_ALL,
         3e9,
-        (near_recv, both_near, small_send),
+        (near_recv, both_near, small_send, vec),
         late=(1,),
         pieces={1: PIECES},
         choose={1: 0},
@@ -867,32 +932,34 @@
         choose={2: 1},
     )
     far_recv = [permute(value, FAR, k) for k, value in enumerate(far_send)]
-    grad_w_out, grad_w_in, grad_select, small, grad_mod = plain_call(
+    rank = w_dt.shape[1]
+    grad_w_out, grad_w_in, grad_select, grad_dt, grad_alog, grad_vec, grad_mod = plain_call(
         last_kernel,
         "weight_sums",
         [
             ((own, width), F32),
             ((own, width), F32),
             ((own, LANES), F32),
-            ((own, LANES), F32),
+            ((own, rank), F32),
+            ((own, states), F32),
+            ((8, own), F32),
             ((2 * own, features.shape[0]), F32),
         ],
-        [((piece, LANES), F32), ((2 * SLOT, LANES), F32)],
+        [((piece, LANES), F32), ((SLOT + 2 * own, LANES), F32)],
         16,
         1e9,
         (all_recv, feature_rows, *far_recv),
     )
-    rank = w_dt.shape[1]
     return (
         branch.reshape(latent.shape),
         latent_grad.reshape(latent.shape),
         grad_w_in,
         grad_w_out,
         grad_select,
-        small[:, :rank],
-        small[:, rank + states],
-        small[:, rank : rank + states],
-        small[:, rank + states + 1],
+        grad_dt,
+        grad_vec[0],
+        grad_alog,
+        grad_vec[1],
         grad_mod,
     )
 

time: 198 us -> 189 us (0.955)
  local copies, waits for them, and re-layouts: 16.4 us -> 10.2 us
  waiting for transfers between devices: 18 us -> 14.2 us
    slice x2 -> x0, local copies, waits for them, and re-layouts: 2.84 us -> none  [the longest x1 1.47 us: local(): small[:, rank + states + 1]]
    unnamed x24 -> x20, local copies, waits for them, and re-layouts: 6.22 us -> 3.48 us
    pallas_call x8 -> x9, Pallas kernels: 95.1 us -> 94.5 us  [call(): pl.pallas_call(body, out_shape=tuple((jax.ShapeDtypeStruct(s, d) for s, d...]
  transfers between devices with their start and end apart: 18 -> 18, of which waited for: 2 -> 4; matrix products, arithmetic and copies ran while one was open for 2% -> 1% of each run, Pallas kernels for 41% -> 42%
where the time goes in v3:
time: 189 us; the launch traced here: 188 us
  Pallas kernels  96.8 us (51%)
  starting transfers between devices  50.9 us (27%)
  between operations  15 us (8%)
  waiting for transfers between devices  14.2 us (8%)
  local copies, waits for them, and re-layouts  10.2 us (5%)
    pallas_call x9, Pallas kernels, call(): pl.pallas_call(body, out_shape=tuple((jax.ShapeDtypeStruct(s, d) for s, d...  94.5 us
    all_to_all x4, starting transfers between devices, exchange(): return lax.all_to_all(value, axes, split_axis=0, concat_axis=0, tiled=True)  36 us
    ppermute x13, starting transfers between devices, permute(): lax.ppermute(value, axes, [(i, i ^ k) for i in range(lax.axis_size(axes))])  14.8 us
    all_to_all x4, waiting for transfers between devices, exchange(): return lax.all_to_all(value, axes, split_axis=0, concat_axis=0, tiled=True)  7.17 us
    ppermute x13, waiting for transfers between devices, permute(): lax.ppermute(value, axes, [(i, i ^ k) for i in range(lax.axis_size(axes))])  7.02 us
  transfers between devices with their start and end apart: 18, of which 4 were waited for; matrix products, arithmetic and copies ran while one was open for 1% of the time, Pallas kernels for 42%

profile of v3, /device:TPU:1, one launch (start us, length us, event | category | flops | bytes accessed | tf_op | source)
XLA Modules:
  0.0 187.7 jit_solution(1302009050509620808)
XLA Ops:
  7.9 1.9 %reshape.58.refs_0_.refs_2_ = bf16[128,1536]{1,0:T(8,128)(2,1)} reshape(bf16[32,2,2,1536]{3,2,1,0:T(2,128)(2,1)} %param.14) | data formatting | bytes 786432 | tf_op jit(solution)/shard_map/reshape | solution.py:778
  9.8 1.9 %reshape.59.refs_1_ = bf16[128,1536]{1,0:T(8,128)(2,1)} reshape(bf16[32,2,2,1536]{3,2,1,0:T(2,128)(2,1)} %param.15) | data formatting | bytes 786432 | tf_op jit(solution)/shard_map/reshape | solution.py:779
  12.3 9.0 %norm_project.1 = (bf16[1,2,1536,128]{3,2,1,0:T(8,128)(2,1)}, bf16[32,2,48,128]{3,2,1,0:T(8,128)(2,1)}, bf16[1,2,384,128]{3,2,1,0:T(8,128)(2,1)}, bf16[1,2,384,1...) custom-call(bf16[128,1536]{1,0:T(8,128)(2,1)} %reshape.58.refs_0_.re, ...), custom_call_target="tpu_custom_call" | custom-call | flops 7000000000 | bytes 11800580 | tf_op jit(solution)/shard_map/norm_project/pallas_call | solution.py:94
  21.3 1.5 collective-permute-start
  22.8 1.3 collective-permute-start.1
  24.6 10.6 %all-to-all-start = ((bf16[32,2,48,128]{3,2,1,0:T(8,128)(2,1)}), bf16[32,2,48,128]{3,2,1,0:T(8,128)(2,1)S(1)}, u32[]{:S(2)}, u32[]{:S(2)}) async-start(bf16[32,2,48,128]{3,2,1,0:T(8,128)(2,1)} %get-tuple-element.81), calls=%async_computation | async-start | bytes 1572864 | tf_op jit(solution)/shard_map/all_to_all | solution.py:751
  35.8 17.7 %scan_height.1 = (bf16[1,2,384,128]{3,2,1,0:T(8,128)(2,1)}, bf16[1,2,384,128]{3,2,1,0:T(8,128)(2,1)}, bf16[1,2,384,128]{3,2,1,0:T(8,128)(2,1)}, bf16[1,2,384,128...) custom-call(s32[8]{0:T(128)} %refs_0_.3, ...), custom_call_target="tpu_custom_call" | custom-call | flops 20000000000 | bytes 1585188 | tf_op jit(solution)/shard_map/scan_height/pallas_call | solution.py:94
  54.6 1.2 collective-permute-start.5
  56.7 20.4 %scan_width.1 = (bf16[32,2,48,128]{3,2,1,0:T(8,128)(2,1)}, bf16[128,1536]{1,0:T(8,128)(2,1)}, bf16[128,1536]{1,0:T(8,128)(2,1)}, bf16[128,128]{1,0:T(8,128)(2,1)...) custom-call(s32[64]{0:T(128)} %refs_0_.4, s32[1]{0:T(128)} %bitcast.refs_6_.refs_1_.refs_0_, ...), custom_call_target="tpu_custom_call" | custom-call | flops 20000000000 | bytes 1585412 | tf_op jit(solution)/shard_map/scan_width/pallas_call | solution.py:94
  77.2 9.6 %all-to-all-start.1 = ((bf16[32,2,48,128]{3,2,1,0:T(8,128)(2,1)}), bf16[32,2,48,128]{3,2,1,0:T(8,128)(2,1)S(1)}, u32[]{:S(2)}, u32[]{:S(2)}) async-start(bf16[32,2,48,128]{3,2,1,0:T(8,128)(2,1)} %get-tuple-element.83), calls=%async_computation.1 | async-start | bytes 1572864 | tf_op jit(solution)/shard_map/all_to_all | solution.py:751
  86.8 20.5 %scan_time.1 = (bf16[1,2,1536,128]{3,2,1,0:T(8,128)(2,1)}, bf16[128,1536]{1,0:T(8,128)(2,1)}, bf16[128,1536]{1,0:T(8,128)(2,1)}, bf16[128,128]{1,0:T(8,128)(2,1)...) custom-call(s32[32]{0:T(128)} %refs_0_.5, s32[1]{0:T(128)} %bitcast.refs_6_.refs_1_.refs_0_, ...), custom_call_target="tpu_custom_call" | custom-call | flops 20000000000 | bytes 1585284 | tf_op jit(solution)/shard_map/scan_time/pallas_call | solution.py:94
  108.2 4.2 %sum_directions.1 = (bf16[128,1536]{1,0:T(8,128)(2,1)}, bf16[128,1536]{1,0:T(8,128)(2,1)}, bf16[16,192,128]{2,1,0:T(8,128)(2,1)}) custom-call(s32[1]{0:T(128)} %bitcast.refs_6_.refs_1_.refs_0_, bf16[128,1536]{1,0:T(8,128)(2,1)} %get-tuple-element.85.refs_1_, bf16[128,1536]{1,0:T(8,128)(2,1)} %get-tuple-element.86.refs_2_, ...), custom_call_target="tpu_custom_call" | custom-call | flops 6000000000 | bytes 3944452 | tf_op jit(solution)/shard_map/sum_directions/pallas_call | solution.py:94
  112.5 6.8 %all-to-all-start.2 = ((bf16[16,192,128]{2,1,0:T(8,128)(2,1)}), bf16[16,192,128]{2,1,0:T(8,128)(2,1)S(1)}, u32[]{:S(2)}, u32[]{:S(2)}) async-start(bf16[16,192,128]{2,1,0:T(8,128)(2,1)} %get-tuple-element.98), calls=%async_computation.2 | async-start | bytes 1572864 | tf_op jit(solution)/shard_map/all_to_all | solution.py:751
  119.2 4.3 %small_sums.1.refs_2_ = bf16[128,24,128]{2,1,0:T(8,128)(2,1)} custom-call(bf16[1,2,1536,128]{3,2,1,0:T(8,128)(2,1)} %get-tuple-element.100.refs_2_.refs_0_, bf16[128,1536]{1,0:T(8,128)(2,1)} %get-tuple-element.85.refs_1_, bf16[128,1536]{1,0:T(8,128)(2,1)} %get-tuple-element.101.refs_2_, bf16[128,128]{1,0:T(8,128)(2,1)} %get-tuple-element.102.refs_3_, ...), custom_call_target="tpu_custom_call" | custom-call | flops 3000000000 | bytes 3784704 | tf_op jit(solution)/shard_map/small_sums/pallas_call | solution.py:94
  123.6 7.6 %out_projections.1 = (bf16[128,1536]{1,0:T(8,128)(2,1)}, bf16[128,1536]{1,0:T(8,128)(2,1)}, f32[128,128]{1,0:T(8,128)}) custom-call(bf16[128,1536]{1,0:T(8,128)(2,1)} %get-tuple-element.93.refs_0_, bf16[128,1536]{1,0:T(8,128)(2,1)} %get-tuple-element.94.refs_1_, bf16[128,1536]{1,0:T(8,128)(2,1)} %reshape.58.refs_0_.refs_2_, ...), custom_call_target="tpu_custom_call" | custom-call | flops 6000000000 | bytes 10715136 | tf_op jit(solution)/shard_map/out_projections/pallas_call | solution.py:94
  131.2 7.2 %all-to-all-done.2.refs_0_.refs_1_ = bf16[16,192,128]{2,1,0:T(8,128)(2,1)S(1)} async-done(((bf16[16,192,128]{2,1,0:T(8,128)(2,1)}), bf16[16,192,128]{2,1,0:T(8,128)(2,1)S(1)}, u32[]{:S(2)}, u32[]{:S(2)}) %all-to-all-start.2) | async-done | bytes 786464 | tf_op jit(solution)/shard_map/all_to_all | solution.py:751
  139.3 6.0 %in_weight_grad.1 = bf16[128,40,128]{2,1,0:T(8,128)(2,1)} custom-call(bf16[16,192,128]{2,1,0:T(8,128)(2,1)} %copy-done.2, bf16[16,2,128,1536]{3,2,1,0:T(8,128)(2,1)} %bitcast.10, bf16[128,24,128]{2,1,0:T(8,128)(2,1)} %small_sums.1.refs_2_, f32[128,128]{1,0:T(8,128)} %get-tuple-element.118.refs_3_), custom_call_target="tpu_custom_call" | custom-call | flops 3000000000 | bytes 14221312 | tf_op jit(solution)/shard_map/in_weight_grad/pallas_call | solution.py:94
  145.3 9.1 %all-to-all-start.3 = ((bf16[128,40,128]{2,1,0:T(8,128)(2,1)}), bf16[128,40,128]{2,1,0:T(8,128)(2,1)}, u32[]{:S(2)}, u32[]{:S(2)}) async-start(bf16[128,40,128]{2,1,0:T(8,128)(2,1)} %in_weight_grad.1), calls=%async_computation.3 | async-start | bytes 2621440 | tf_op jit(solution)/shard_map/all_to_all | solution.py:751
  154.5 4.7 %out_weight_grad.1 = (bf16[144,128]{1,0:T(8,128)(2,1)}, bf16[144,128]{1,0:T(8,128)(2,1)}, bf16[144,128]{1,0:T(8,128)(2,1)}, bf16[144,128]{1,0:T(8,128)(2,1)}, bf...) custom-call(s32[1]{0:T(128)} %bitcast.5.refs_0_, ...), custom_call_target="tpu_custom_call" | custom-call | flops 4000000000 | bytes 13369348 | tf_op jit(solution)/shard_map/out_weight_grad/pallas_call | solution.py:94
  159.2 2.7 %collective-permute-start.10 = (bf16[144,128]{1,0:T(8,128)(2,1)}, bf16[144,128]{1,0:T(8,128)(2,1)S(1)}, u32[]{:S(2)}, u32[]{:S(2)}) collective-permute-start(bf16[144,128]{1,0:T(8,128)(2,1)} %get-tuple-element.124), channel_id=1, source_target_pairs={{0,80},{16,64},{32,112},{48,96},{64,16},{80,0},{96,48},{112,32},{1... | collective-permute-start | bytes 110600 | tf_op jit(solution)/shard_map/ppermute | solution.py:747
  163.2 2.1 %collective-permute-start.6 = (bf16[144,128]{1,0:T(8,128)(2,1)}, bf16[144,128]{1,0:T(8,128)(2,1)S(1)}, u32[]{:S(2)}, u32[]{:S(2)}) collective-permute-start(bf16[144,128]{1,0:T(8,128)(2,1)} %get-tuple-element.120), channel_id=1, source_target_pairs={{0,16},{16,0},{32,48},{48,32},{64,80},{80,64},{96,112},{112,96},{1... | collective-permute-start | bytes 110600 | tf_op jit(solution)/shard_map/ppermute | solution.py:747
  166.3 5.3 %collective-permute-done.10.refs_5_ = bf16[144,128]{1,0:T(8,128)(2,1)S(1)} collective-permute-done((bf16[144,128]{1,0:T(8,128)(2,1)}, bf16[144,128]{1,0:T(8,128)(2,1)S(1)}, u32[]{:S(2)}, u32[]{:S(2)}) %collective-permute-start.10) | collective-permute-done | bytes 36896 | tf_op jit(solution)/shard_map/ppermute | solution.py:747
  171.6 2.2 %collective-permute-start.8 = (bf16[144,128]{1,0:T(8,128)(2,1)}, bf16[144,128]{1,0:T(8,128)(2,1)S(1)}, u32[]{:S(2)}, u32[]{:S(2)}) collective-permute-start(bf16[144,128]{1,0:T(8,128)(2,1)} %get-tuple-element.122), channel_id=1, source_target_pairs={{0,48},{16,32},{32,16},{48,0},{64,112},{80,96},{96,80},{112,64},{1... | collective-permute-start | bytes 110600 | tf_op jit(solution)/shard_map/ppermute | solution.py:747
  178.1 2.3 %weight_sums.1 = (f32[12,1536]{1,0:T(8,128)}, f32[12,1536]{1,0:T(8,128)}, f32[12,128]{1,0:T(8,128)}, f32[12,96]{1,0:T(8,128)}, f32[12,16]{1,0:T(8,128)}, /*index=5*/f32[8,12]{1,0:T(8,128)S(1)}, f32[24,256]{1,0:T(8,128)}) custom-call(bf16[128,40,128]{2,1,0:T(8,128)(2,1)} %all-to-all-done.3.all_ref, bf16[8,256]{1,0:T(8,128)(2,1)S(1)} %copy-done, ...), custom_call_target="tpu_custom_call" | custom-call | flops 1000000000 | bytes 1609728 | tf_op jit(solution)/shard_map/weight_sums/pallas_call | solution.py:121
  (54 shorter events, 12.7 us)
Async XLA Ops:
  7.2 131.2 %all-gather.3.cloned.1.call-start = ((), (), s32[]{:S(2)}) async-start(), calls=%async_computation.4 | async-start | bytes 13369344 | tf_op jit(solution)/shard_map/all_gather | solution.py:814
  12.3 22.8 %copy-start.7 = (f32[1536]{0:T(1024)S(1)}, f32[1536]{0:T(1024)}, u32[]{:S(2)}) copy-start(f32[1536]{0:T(1024)} %param.22) | copy-start | bytes 18436
  12.3 22.9 %copy-start.8 = (f32[1536]{0:T(1024)S(1)}, f32[1536]{0:T(1024)}, u32[]{:S(2)}) copy-start(f32[1536]{0:T(1024)} %param.20) | copy-start | bytes 18436
  21.3 14.5 %collective-permute-start = (bf16[1,2,384,128]{3,2,1,0:T(8,128)(2,1)}, bf16[1,2,384,128]{3,2,1,0:T(8,128)(2,1)}, u32[]{:S(2)}, u32[]{:S(2)}) collective-permute-start(bf16[1,2,384,128]{3,2,1,0:T(8,128)(2,1)} %get-tuple-element.74), channel_id=1, source_target_pairs={{0,32},{32,0},{64,96},{96,64},{1,33},{33,1},{65,97},{97,65},{2,34}... | collective-permute-start | bytes 589832 | tf_op jit(solution)/shard_map/ppermute | solution.py:747
  22.8 13.0 %collective-permute-start.1 = (bf16[1,2,384,128]{3,2,1,0:T(8,128)(2,1)}, bf16[1,2,384,128]{3,2,1,0:T(8,128)(2,1)}, u32[]{:S(2)}, u32[]{:S(2)}) collective-permute-start(bf16[1,2,384,128]{3,2,1,0:T(8,128)(2,1)} %get-tuple-element.75), channel_id=1, source_target_pairs={{0,64},{32,96},{64,0},{96,32},{1,65},{33,97},{65,1},{97,33},{2,66}... | collective-permute-start | bytes 589832 | tf_op jit(solution)/shard_map/ppermute | solution.py:747
  24.1 11.7 %collective-permute-start.2 = (bf16[1,2,384,128]{3,2,1,0:T(8,128)(2,1)}, bf16[1,2,384,128]{3,2,1,0:T(8,128)(2,1)}, u32[]{:S(2)}, u32[]{:S(2)}) collective-permute-start(bf16[1,2,384,128]{3,2,1,0:T(8,128)(2,1)} %get-tuple-element.76), channel_id=1, source_target_pairs={{0,96},{32,64},{64,32},{96,0},{1,97},{33,65},{65,33},{97,1},{2,98}... | collective-permute-start | bytes 589832 | tf_op jit(solution)/shard_map/ppermute | solution.py:747
  24.6 31.3 %all-to-all-start = ((bf16[32,2,48,128]{3,2,1,0:T(8,128)(2,1)}), bf16[32,2,48,128]{3,2,1,0:T(8,128)(2,1)S(1)}, u32[]{:S(2)}, u32[]{:S(2)}) async-start(bf16[32,2,48,128]{3,2,1,0:T(8,128)(2,1)} %get-tuple-element.81), calls=%async_computation | async-start | bytes 1572864 | tf_op jit(solution)/shard_map/all_to_all | solution.py:751
  53.6 33.1 %collective-permute-start.3 = (bf16[1,2,384,128]{3,2,1,0:T(8,128)(2,1)}, bf16[1,2,384,128]{3,2,1,0:T(8,128)(2,1)S(1)}, u32[]{:S(2)}, u32[]{:S(2)}) collective-permute-start(bf16[1,2,384,128]{3,2,1,0:T(8,128)(2,1)} %get-tuple-element.78), channel_id=1, source_target_pairs={{0,32},{32,0},{64,96},{96,64},{1,33},{33,1},{65,97},{97,65},{2,34}... | collective-permute-start | bytes 589832 | tf_op jit(solution)/shard_map/ppermute | solution.py:747
  54.1 32.6 %collective-permute-start.4 = (bf16[1,2,384,128]{3,2,1,0:T(8,128)(2,1)}, bf16[1,2,384,128]{3,2,1,0:T(8,128)(2,1)}, u32[]{:S(2)}, u32[]{:S(2)}) collective-permute-start(bf16[1,2,384,128]{3,2,1,0:T(8,128)(2,1)} %get-tuple-element.79), channel_id=1, source_target_pairs={{0,64},{32,96},{64,0},{96,32},{1,65},{33,97},{65,1},{97,33},{2,66}... | collective-permute-start | bytes 589832 | tf_op jit(solution)/shard_map/ppermute | solution.py:747
  54.6 32.1 %collective-permute-start.5 = (bf16[1,2,384,128]{3,2,1,0:T(8,128)(2,1)}, bf16[1,2,384,128]{3,2,1,0:T(8,128)(2,1)}, u32[]{:S(2)}, u32[]{:S(2)}) collective-permute-start(bf16[1,2,384,128]{3,2,1,0:T(8,128)(2,1)} %get-tuple-element.80), channel_id=1, source_target_pairs={{0,96},{32,64},{64,32},{96,0},{1,97},{33,65},{65,33},{97,1},{2,98}... | collective-permute-start | bytes 589832 | tf_op jit(solution)/shard_map/ppermute | solution.py:747
  77.2 30.2 %all-to-all-start.1 = ((bf16[32,2,48,128]{3,2,1,0:T(8,128)(2,1)}), bf16[32,2,48,128]{3,2,1,0:T(8,128)(2,1)S(1)}, u32[]{:S(2)}, u32[]{:S(2)}) async-start(bf16[32,2,48,128]{3,2,1,0:T(8,128)(2,1)} %get-tuple-element.83), calls=%async_computation.1 | async-start | bytes 1572864 | tf_op jit(solution)/shard_map/all_to_all | solution.py:751
  86.7 20.6 %copy-start.9 = (bf16[1,2,384,128]{3,2,1,0:T(8,128)(2,1)}, bf16[1,2,384,128]{3,2,1,0:T(8,128)(2,1)S(1)}, u32[]{:S(2)}) copy-start(bf16[1,2,384,128]{3,2,1,0:T(8,128)(2,1)S(1)} %collective-permute-done.3.refs_6_) | copy-start | bytes 589828
  112.5 25.9 %all-to-all-start.2 = ((bf16[16,192,128]{2,1,0:T(8,128)(2,1)}), bf16[16,192,128]{2,1,0:T(8,128)(2,1)S(1)}, u32[]{:S(2)}, u32[]{:S(2)}) async-start(bf16[16,192,128]{2,1,0:T(8,128)(2,1)} %get-tuple-element.98), calls=%async_computation.2 | async-start | bytes 1572864 | tf_op jit(solution)/shard_map/all_to_all | solution.py:751
  145.3 32.0 %all-to-all-start.3 = ((bf16[128,40,128]{2,1,0:T(8,128)(2,1)}), bf16[128,40,128]{2,1,0:T(8,128)(2,1)}, u32[]{:S(2)}, u32[]{:S(2)}) async-start(bf16[128,40,128]{2,1,0:T(8,128)(2,1)} %in_weight_grad.1), calls=%async_computation.3 | async-start | bytes 2621440 | tf_op jit(solution)/shard_map/all_to_all | solution.py:751
  154.4 19.4 %copy-start.6 = (bf16[128,1536]{1,0:T(8,128)(2,1)S(1)}, bf16[128,1536]{1,0:T(8,128)(2,1)}, u32[]{:S(2)}) copy-start(bf16[128,1536]{1,0:T(8,128)(2,1)} %get-tuple-element.96) | copy-start | bytes 1179652
  154.4 20.2 %copy-start.5 = (bf16[128,1536]{1,0:T(8,128)(2,1)S(1)}, bf16[128,1536]{1,0:T(8,128)(2,1)}, u32[]{:S(2)}) copy-start(bf16[128,1536]{1,0:T(8,128)(2,1)} %get-tuple-element.97) | copy-start | bytes 1179652
  154.5 22.8 %copy-start = (bf16[8,256]{1,0:T(8,128)(2,1)S(1)}, bf16[8,256]{1,0:T(8,128)(2,1)}, u32[]{:S(2)}) copy-start(bf16[8,256]{1,0:T(8,128)(2,1)} %broadcast_in_dim.13.refs_5_.feature_ref) | copy-start | bytes 12292
  159.2 12.4 %collective-permute-start.10 = (bf16[144,128]{1,0:T(8,128)(2,1)}, bf16[144,128]{1,0:T(8,128)(2,1)S(1)}, u32[]{:S(2)}, u32[]{:S(2)}) collective-permute-start(bf16[144,128]{1,0:T(8,128)(2,1)} %get-tuple-element.124), channel_id=1, source_target_pairs={{0,80},{16,64},{32,112},{48,96},{64,16},{80,0},{96,48},{112,32},{1... | collective-permute-start | bytes 110600 | tf_op jit(solution)/shard_map/ppermute | solution.py:747
  161.8 11.9 %collective-permute-start.11 = (bf16[144,128]{1,0:T(8,128)(2,1)}, bf16[144,128]{1,0:T(8,128)(2,1)S(1)}, u32[]{:S(2)}, u32[]{:S(2)}) collective-permute-start(bf16[144,128]{1,0:T(8,128)(2,1)} %get-tuple-element.125), channel_id=1, source_target_pairs={{0,96},{16,112},{32,64},{48,80},{64,32},{80,48},{96,0},{112,16},{1... | collective-permute-start | bytes 110600 | tf_op jit(solution)/shard_map/ppermute | solution.py:747
  162.3 13.3 %collective-permute-start.12 = (bf16[144,128]{1,0:T(8,128)(2,1)}, bf16[144,128]{1,0:T(8,128)(2,1)S(1)}, u32[]{:S(2)}, u32[]{:S(2)}) collective-permute-start(bf16[144,128]{1,0:T(8,128)(2,1)} %get-tuple-element.126), channel_id=1, source_target_pairs={{0,112},{16,96},{32,80},{48,64},{64,48},{80,32},{96,16},{112,0},{1... | collective-permute-start | bytes 110600 | tf_op jit(solution)/shard_map/ppermute | solution.py:747
  163.2 12.3 %collective-permute-start.6 = (bf16[144,128]{1,0:T(8,128)(2,1)}, bf16[144,128]{1,0:T(8,128)(2,1)S(1)}, u32[]{:S(2)}, u32[]{:S(2)}) collective-permute-start(bf16[144,128]{1,0:T(8,128)(2,1)} %get-tuple-element.120), channel_id=1, source_target_pairs={{0,16},{16,0},{32,48},{48,32},{64,80},{80,64},{96,112},{112,96},{1... | collective-permute-start | bytes 110600 | tf_op jit(solution)/shard_map/ppermute | solution.py:747
  165.4 10.2 %collective-permute-start.7 = (bf16[144,128]{1,0:T(8,128)(2,1)}, bf16[144,128]{1,0:T(8,128)(2,1)S(1)}, u32[]{:S(2)}, u32[]{:S(2)}) collective-permute-start(bf16[144,128]{1,0:T(8,128)(2,1)} %get-tuple-element.121), channel_id=1, source_target_pairs={{0,32},{16,48},{32,0},{48,16},{64,96},{80,112},{96,64},{112,80},{1... | collective-permute-start | bytes 110600 | tf_op jit(solution)/shard_map/ppermute | solution.py:747
  171.6 5.1 %collective-permute-start.8 = (bf16[144,128]{1,0:T(8,128)(2,1)}, bf16[144,128]{1,0:T(8,128)(2,1)S(1)}, u32[]{:S(2)}, u32[]{:S(2)}) collective-permute-start(bf16[144,128]{1,0:T(8,128)(2,1)} %get-tuple-element.122), channel_id=1, source_target_pairs={{0,48},{16,32},{32,16},{48,0},{64,112},{80,96},{96,80},{112,64},{1... | collective-permute-start | bytes 110600 | tf_op jit(solution)/shard_map/ppermute | solution.py:747
  173.8 3.5 %collective-permute-start.9 = (bf16[144,128]{1,0:T(8,128)(2,1)}, bf16[144,128]{1,0:T(8,128)(2,1)S(1)}, u32[]{:S(2)}, u32[]{:S(2)}) collective-permute-start(bf16[144,128]{1,0:T(8,128)(2,1)} %get-tuple-element.123), channel_id=1, source_target_pairs={{0,64},{16,80},{32,96},{48,112},{64,0},{80,16},{96,32},{112,48},{1... | collective-permute-start | bytes 110600 | tf_op jit(solution)/shard_map/ppermute | solution.py:747
  (4 other events, 3.5 us)
Sparse Core Ops, SparseCore 0:
  21.5 115.4 all-gather.2

commit v4 on v3

--- a/solution.py
+++ b/solution.py
@@ -168,20 +168,24 @@
     pre_ref,
     mod_ref,
     cot_ref,
+    rows_ref,
     flat_ref,
 ):
-    tokens, width = latent_ref.shape
+    tokens, width = rows_ref.shape
     tiles = w_in_ref.shape[1] // LANES
     modulation = lax.dot_general(
         feature_ref[...], w_mod_ref[...], NT, preferred_element_type=F32
     )
     mod_ref[...] = modulation
     send(8)
-    normed, _ = normalise(latent_ref[...])
+    latent = latent_ref[...].astype(F32).reshape(tokens, width)
+    rows_ref[...] = latent.astype(BF)
+    send(10)
+    normed, _ = normalise(latent)
     shifted = (normed * (1.0 + modulation[:1, width:]) + modulation[:1, :width]).astype(BF)
     both_ref[0] = shifted
     wait(1)
-    both_ref[1] = grad_ref[...]
+    both_ref[1] = grad_ref[...].astype(F32).reshape(tokens, width).astype(BF)
     send(6)
     wait(2)
     pre_act = jnp.dot(shifted, w_in_ref[...], preferred_element_type=F32)
@@ -205,7 +209,7 @@
 
     pack(0, activ)
     wait(3)
-    cot = lax.dot_general(grad_ref[...], w_out_ref[...], NT, preferred_element_type=F32).astype(BF)
+    cot = lax.dot_general(both_ref[1], w_out_ref[...], NT, preferred_element_type=F32).astype(BF)
     cot_ref[...] = cot
     send(9)
     pack(1, cot)
@@ -691,9 +695,13 @@
     all_ref[:, :SLOT] = rows_ref[...].reshape(devices, SLOT, LANES).astype(BF)
 
 
-def out_grad_kernel(wait, place_ref, recv_ref, both_ref, *refs):
-    far_refs = refs[:FAR_SIZE]
-    left_ref, out_ref, half_ref = refs[FAR_SIZE:]
+def pair_place(place, core_flip, slot):
+    return place ^ ((slot // 2) * 4 + core_flip * 2 + slot % 2)
+
+
+def out_grad_kernel(
+    wait, place_ref, recv_ref, both_ref, mine_ref, other_ref, left_ref, out_ref, half_ref
+):
     near = recv_ref.shape[0]
     rows = left_ref.shape[0]
     far = FAR_SIZE
@@ -706,14 +714,21 @@
         half_ref[...] = product[:, cut(j)]
         for o in range(far):
             out_ref[o, pl.ds(j, own, stride=tiles), :] = half_ref[o * own : (o + 1) * own, :]
-    for k, ref in enumerate(far_refs):
-        ref[...] = out_ref[place_ref[0] ^ k].astype(BF)
+    for slot in range(far // 2):
+        mine_ref[slot] = out_ref[pair_place(place_ref[0], 0, slot)]
+        other_ref[slot] = out_ref[pair_place(place_ref[0], 1, slot)].astype(BF)
+
+
+def pair_sum_kernel(mine_ref, other_ref, kept_ref, *slot_refs):
+    kept_ref[...] = mine_ref[0] + other_ref[0].astype(F32)
+    for slot, ref in enumerate(slot_refs, 1):
+        ref[...] = (mine_ref[slot] + other_ref[slot].astype(F32)).astype(BF)
 
 
 def last_kernel(all_ref, feature_ref, *refs):
-    far_refs = refs[:FAR_SIZE]
+    far_refs = refs[: FAR_SIZE // 2]
     gwo_ref, gwi_ref, gsel_ref, gdt_ref, galog_ref, gvec_ref, gmod_ref, sum_ref, rest_ref = refs[
-        FAR_SIZE:
+        FAR_SIZE // 2 :
     ]
     far = FAR_SIZE
     own, width = gwo_ref.shape
@@ -775,8 +790,6 @@
     n_row, n_col = lax.axis_size(ROW), lax.axis_size(COL)
     near, far = lax.axis_size(NEAR), lax.axis_size(FAR)
     own = width // (near * far)
-    flat_latent = latent.reshape(tokens, width)
-    flat_grad = out_grad.reshape(tokens, width)
     features = jax.nn.silu(time_features(t_index, w_mod.shape[1])).astype(BF)
     feature_rows = jnp.broadcast_to(features[None, :], (8, features.shape[0]))
 
@@ -786,7 +799,7 @@
     slot = ((1, 2, tokens * tiles // n_row, LANES), BF)
     place = lax.axis_index(ROW).astype(jnp.int32)[None]
     far_place = lax.axis_index(FAR).astype(jnp.int32)[None]
-    data_own, data_wide, *slots, both, pre_act, modulation, cot = call(
+    data_own, data_wide, *slots, both, pre_act, modulation, cot, flat_latent = call(
         pre_kernel,
         "norm_project",
         [
@@ -800,14 +813,15 @@
             ((tokens, inner), F32),
             ((8, 2 * width), F32),
             ((tokens, inner), BF),
+            ((tokens, width), BF),
         ],
         [((tokens * tiles, LANES), F32)],
         VMEM_ALL,
         7e9,
-        (flat_latent, flat_grad, w_in, w_out, w_mod, feature_rows, place),
+        (latent, out_grad, w_in, w_out, w_mod, feature_rows, place),
         smem=(6,),
         late=(1, 2, 3),
-        early=tuple(range(10)),
+        early=tuple(range(11)),
     )
     data_wide = exchange(data_wide, COL)
     slots = [permute(value, ROW, k) for k, value in enumerate(slots)]
@@ -914,10 +928,10 @@
         choose={1: 0},
     )[0]
     all_recv = exchange(all_send, FAR + NEAR)
-    far_send = call(
+    mine, other = call(
         out_grad_kernel,
         "out_weight_grad",
-        [((piece, LANES), BF)] * far,
+        [((far // 2, piece, LANES), F32), ((far // 2, piece, LANES), BF)],
         [
             ((inner // near, near * tokens), BF),
             ((far, piece, LANES), F32),
@@ -931,7 +945,17 @@
         pieces={2: PIECES},
         choose={2: 1},
     )
-    far_recv = [permute(value, FAR, k) for k, value in enumerate(far_send)]
+    other = permute(other, FAR, 2)
+    far_send = plain_call(
+        pair_sum_kernel,
+        "pair_sums",
+        [((piece, LANES), F32)] + [((piece, LANES), BF)] * (far // 2 - 1),
+        [],
+        8,
+        1e9,
+        (mine, other),
+    )
+    far_recv = [permute(value, FAR, (0, 1, 4, 5)[slot]) for slot, value in enumerate(far_send)]
     rank = w_dt.shape[1]
     grad_w_out, grad_w_in, grad_select, grad_dt, grad_alog, grad_vec, grad_mod = plain_call(
         last_kernel,

time: 189 us -> 182 us (0.963)
  starting transfers between devices: 50.9 us -> 46.1 us
  local copies, waits for them, and re-layouts: 10.2 us -> 6.58 us
    ppermute x13 -> x10, starting transfers between devices: 14.8 us -> 10 us  [permute(): lax.ppermute(value, axes, [(i, i ^ k) for i in range(lax.axis_size(axes))])]
    reshape x2 -> x0, local copies, waits for them, and re-layouts: 3.78 us -> none  [the longest x1 1.89 us: local(): flat_latent = latent.reshape(tokens, width)]
    all_to_all x4, waiting for transfers between devices: 7.17 us -> 9.8 us  [exchange(): return lax.all_to_all(value, axes, split_axis=0, concat_axis=0, tiled=True)]
    ppermute x13 -> x10, waiting for transfers between devices: 7.02 us -> 5.79 us  [permute(): lax.ppermute(value, axes, [(i, i ^ k) for i in range(lax.axis_size(axes))])]
  transfers between devices with their start and end apart: 18 -> 15, of which waited for: 4 -> 5; matrix products, arithmetic and copies ran while one was open for 1% -> 1% of each run, Pallas kernels for 42% -> 44%
where the time goes in v4:
time: 182 us; the launch traced here: 181 us
  Pallas kernels  97 us (53%)
  starting transfers between devices  46.1 us (25%)
  waiting for transfers between devices  15.6 us (9%)
  between operations  15 us (8%)
  local copies, waits for them, and re-layouts  6.58 us (4%)
    pallas_call x9, Pallas kernels, call(): pl.pallas_call(body, out_shape=tuple((jax.ShapeDtypeStruct(s, d) for s, d...  94.7 us
    all_to_all x4, starting transfers between devices, exchange(): return lax.all_to_all(value, axes, split_axis=0, concat_axis=0, tiled=True)  36 us
    ppermute x10, starting transfers between devices, permute(): lax.ppermute(value, axes, [(i, i ^ k) for i in range(lax.axis_size(axes))])  10 us
    all_to_all x4, waiting for transfers between devices, exchange(): return lax.all_to_all(value, axes, split_axis=0, concat_axis=0, tiled=True)  9.8 us
    ppermute x10, waiting for transfers between devices, permute(): lax.ppermute(value, axes, [(i, i ^ k) for i in range(lax.axis_size(axes))])  5.79 us
    unnamed x20, local copies, waits for them, and re-layouts  3.65 us
  transfers between devices with their start and end apart: 15, of which 5 were waited for; matrix products, arithmetic and copies ran while one was open for 1% of the time, Pallas kernels for 44%

profile of v4, /device:TPU:1, one launch (start us, length us, event | category | flops | bytes accessed | tf_op | source)
XLA Modules:
  0.0 180.9 jit_solution(14778999192515641935)
XLA Ops:
  8.6 9.2 %norm_project.1 = (bf16[1,2,1536,128]{3,2,1,0:T(8,128)(2,1)}, bf16[32,2,48,128]{3,2,1,0:T(8,128)(2,1)}, bf16[1,2,384,128]{3,2,1,0:T(8,128)(2,1)}, bf16[1,2,384,1...) custom-call(bf16[32,2,2,1536]{3,2,1,0:T(2,128)(2,1)} %refs_0_.4, ...), custom_call_target="tpu_custom_call" | custom-call | flops 7000000000 | bytes 11800580 | tf_op jit(solution)/shard_map/norm_project/pallas_call | solution.py:94
  17.8 1.5 collective-permute-start
  19.3 1.3 collective-permute-start.1
  21.0 10.6 %all-to-all-start = ((bf16[32,2,48,128]{3,2,1,0:T(8,128)(2,1)}), bf16[32,2,48,128]{3,2,1,0:T(8,128)(2,1)S(1)}, u32[]{:S(2)}, u32[]{:S(2)}) async-start(bf16[32,2,48,128]{3,2,1,0:T(8,128)(2,1)} %get-tuple-element.80), calls=%async_computation | async-start | bytes 1572864 | tf_op jit(solution)/shard_map/all_to_all | solution.py:766
  32.3 17.8 %scan_height.1 = (bf16[1,2,384,128]{3,2,1,0:T(8,128)(2,1)}, bf16[1,2,384,128]{3,2,1,0:T(8,128)(2,1)}, bf16[1,2,384,128]{3,2,1,0:T(8,128)(2,1)}, bf16[1,2,384,128...) custom-call(s32[8]{0:T(128)} %refs_0_.5, ...), custom_call_target="tpu_custom_call" | custom-call | flops 20000000000 | bytes 1585188 | tf_op jit(solution)/shard_map/scan_height/pallas_call | solution.py:94
  51.1 1.2 collective-permute-start.5
  53.2 20.3 %scan_width.1 = (bf16[32,2,48,128]{3,2,1,0:T(8,128)(2,1)}, bf16[128,1536]{1,0:T(8,128)(2,1)}, bf16[128,1536]{1,0:T(8,128)(2,1)}, bf16[128,128]{1,0:T(8,128)(2,1)...) custom-call(s32[64]{0:T(128)} %refs_0_.6, s32[1]{0:T(128)} %bitcast.refs_6_.refs_1_.refs_0_, ...), custom_call_target="tpu_custom_call" | custom-call | flops 20000000000 | bytes 1585412 | tf_op jit(solution)/shard_map/scan_width/pallas_call | solution.py:94
  73.5 9.6 %all-to-all-start.1 = ((bf16[32,2,48,128]{3,2,1,0:T(8,128)(2,1)}), bf16[32,2,48,128]{3,2,1,0:T(8,128)(2,1)S(1)}, u32[]{:S(2)}, u32[]{:S(2)}) async-start(bf16[32,2,48,128]{3,2,1,0:T(8,128)(2,1)} %get-tuple-element.82), calls=%async_computation.1 | async-start | bytes 1572864 | tf_op jit(solution)/shard_map/all_to_all | solution.py:766
  83.1 20.6 %scan_time.1 = (bf16[1,2,1536,128]{3,2,1,0:T(8,128)(2,1)}, bf16[128,1536]{1,0:T(8,128)(2,1)}, bf16[128,1536]{1,0:T(8,128)(2,1)}, bf16[128,128]{1,0:T(8,128)(2,1)...) custom-call(s32[32]{0:T(128)} %refs_0_.7, s32[1]{0:T(128)} %bitcast.refs_6_.refs_1_.refs_0_, ...), custom_call_target="tpu_custom_call" | custom-call | flops 20000000000 | bytes 1585284 | tf_op jit(solution)/shard_map/scan_time/pallas_call | solution.py:94
  104.6 4.2 %sum_directions.1 = (bf16[128,1536]{1,0:T(8,128)(2,1)}, bf16[128,1536]{1,0:T(8,128)(2,1)}, bf16[16,192,128]{2,1,0:T(8,128)(2,1)}) custom-call(s32[1]{0:T(128)} %bitcast.refs_6_.refs_1_.refs_0_, bf16[128,1536]{1,0:T(8,128)(2,1)} %get-tuple-element.84.refs_1_, bf16[128,1536]{1,0:T(8,128)(2,1)} %get-tuple-element.85.refs_2_, ...), custom_call_target="tpu_custom_call" | custom-call | flops 6000000000 | bytes 3944452 | tf_op jit(solution)/shard_map/sum_directions/pallas_call | solution.py:94
  108.8 6.8 %all-to-all-start.2 = ((bf16[16,192,128]{2,1,0:T(8,128)(2,1)}), bf16[16,192,128]{2,1,0:T(8,128)(2,1)S(1)}, u32[]{:S(2)}, u32[]{:S(2)}) async-start(bf16[16,192,128]{2,1,0:T(8,128)(2,1)} %get-tuple-element.98), calls=%async_computation.2 | async-start | bytes 1572864 | tf_op jit(solution)/shard_map/all_to_all | solution.py:766
  115.6 4.3 %small_sums.1.refs_2_ = bf16[128,24,128]{2,1,0:T(8,128)(2,1)} custom-call(bf16[1,2,1536,128]{3,2,1,0:T(8,128)(2,1)} %get-tuple-element.100.refs_2_.refs_0_, bf16[128,1536]{1,0:T(8,128)(2,1)} %get-tuple-element.84.refs_1_, bf16[128,1536]{1,0:T(8,128)(2,1)} %get-tuple-element.101.refs_2_, bf16[128,128]{1,0:T(8,128)(2,1)} %get-tuple-element.102.refs_3_, ...), custom_call_target="tpu_custom_call" | custom-call | flops 3000000000 | bytes 3784704 | tf_op jit(solution)/shard_map/small_sums/pallas_call | solution.py:94
  120.0 7.6 %out_projections.1 = (bf16[128,1536]{1,0:T(8,128)(2,1)}, bf16[128,1536]{1,0:T(8,128)(2,1)}, f32[128,128]{1,0:T(8,128)}) custom-call(bf16[128,1536]{1,0:T(8,128)(2,1)} %get-tuple-element.92.refs_0_, bf16[128,1536]{1,0:T(8,128)(2,1)} %get-tuple-element.93.refs_1_, bf16[128,1536]{1,0:T(8,128)(2,1)} %get-tuple-element.94.refs_2_, ...), custom_call_target="tpu_custom_call" | custom-call | flops 6000000000 | bytes 10715136 | tf_op jit(solution)/shard_map/out_projections/pallas_call | solution.py:94
  127.6 7.2 %all-to-all-done.2.refs_0_.refs_1_ = bf16[16,192,128]{2,1,0:T(8,128)(2,1)S(1)} async-done(((bf16[16,192,128]{2,1,0:T(8,128)(2,1)}), bf16[16,192,128]{2,1,0:T(8,128)(2,1)S(1)}, u32[]{:S(2)}, u32[]{:S(2)}) %all-to-all-start.2) | async-done | bytes 786464 | tf_op jit(solution)/shard_map/all_to_all | solution.py:766
  135.7 6.0 %in_weight_grad.1 = bf16[128,40,128]{2,1,0:T(8,128)(2,1)} custom-call(bf16[16,192,128]{2,1,0:T(8,128)(2,1)} %copy-done.2, bf16[16,2,128,1536]{3,2,1,0:T(8,128)(2,1)} %bitcast.10, bf16[128,24,128]{2,1,0:T(8,128)(2,1)} %small_sums.1.refs_2_, f32[128,128]{1,0:T(8,128)} %get-tuple-element.118.refs_3_), custom_call_target="tpu_custom_call" | custom-call | flops 3000000000 | bytes 14221312 | tf_op jit(solution)/shard_map/in_weight_grad/pallas_call | solution.py:94
  141.7 9.1 %all-to-all-start.3 = ((bf16[128,40,128]{2,1,0:T(8,128)(2,1)}), bf16[128,40,128]{2,1,0:T(8,128)(2,1)}, u32[]{:S(2)}, u32[]{:S(2)}) async-start(bf16[128,40,128]{2,1,0:T(8,128)(2,1)} %in_weight_grad.1), calls=%async_computation.3 | async-start | bytes 2621440 | tf_op jit(solution)/shard_map/all_to_all | solution.py:766
  150.9 4.7 %out_weight_grad.1 = (f32[4,144,128]{2,1,0:T(8,128)}, bf16[4,144,128]{2,1,0:T(8,128)(2,1)}) custom-call(s32[1]{0:T(128)} %bitcast.5.refs_0_, bf16[16,192,128]{2,1,0:T(8,128)(2,1)} %copy-done.2, bf16[16,2,128,1536]{3,2,1,0:T(8,128)(2,1)} %bitcast.11), custom_call_target="tpu_custom_call" | custom-call | flops 4000000000 | bytes 13369348 | tf_op jit(solution)/shard_map/out_weight_grad/pallas_call | solution.py:94
  155.6 1.2 collective-permute-start.6
  156.8 1.2 collective-permute-done.6.other_ref
  158.0 1.0 copy-done.1
  159.0 2.2 %collective-permute-start.7 = (bf16[144,128]{1,0:T(8,128)(2,1)S(1)}, bf16[144,128]{1,0:T(8,128)(2,1)S(1)}, u32[]{:S(2)}, u32[]{:S(2)}) collective-permute-start(bf16[144,128]{1,0:T(8,128)(2,1)S(1)} %get-tuple-element.122), channel_id=1, source_target_pairs={{0,16},{16,0},{32,48},{48,32},{64,80},{80,64},{96,112},{112,96},{1... | collective-permute-start | bytes 110600 | tf_op jit(solution)/shard_map/ppermute | solution.py:762
  164.1 4.3 %collective-permute-done.7.refs_1_ = bf16[144,128]{1,0:T(8,128)(2,1)S(1)} collective-permute-done((bf16[144,128]{1,0:T(8,128)(2,1)S(1)}, bf16[144,128]{1,0:T(8,128)(2,1)S(1)}, u32[]{:S(2)}, u32[]{:S(2)}) %collective-permute-start.7) | collective-permute-done | bytes 36896 | tf_op jit(solution)/shard_map/ppermute | solution.py:762
  168.7 2.6 %all-to-all-done.3.all_ref = bf16[128,40,128]{2,1,0:T(8,128)(2,1)} async-done(((bf16[128,40,128]{2,1,0:T(8,128)(2,1)}), bf16[128,40,128]{2,1,0:T(8,128)(2,1)}, u32[]{:S(2)}, u32[]{:S(2)}) %all-to-all-start.3) | async-done | bytes 1310752 | tf_op jit(solution)/shard_map/all_to_all | solution.py:766
  171.3 2.2 %weight_sums.1 = (f32[12,1536]{1,0:T(8,128)}, f32[12,1536]{1,0:T(8,128)}, f32[12,128]{1,0:T(8,128)}, f32[12,96]{1,0:T(8,128)}, f32[12,16]{1,0:T(8,128)}, /*index=5*/f32[8,12]{1,0:T(8,128)S(1)}, f32[24,256]{1,0:T(8,128)}) custom-call(bf16[128,40,128]{2,1,0:T(8,128)(2,1)} %all-to-all-done.3.all_ref, bf16[8,256]{1,0:T(8,128)(2,1)S(1)} %copy-done, ...), custom_call_target="tpu_custom_call" | custom-call | flops 1000000000 | bytes 1499136 | tf_op jit(solution)/shard_map/weight_sums/pallas_call | solution.py:121
  (47 shorter events, 9.3 us)
Async XLA Ops:
  7.2 127.6 %all-gather.3.cloned.1.call-start = ((), (), s32[]{:S(2)}) async-start(), calls=%async_computation.4 | async-start | bytes 13369344 | tf_op jit(solution)/shard_map/all_gather | solution.py:828
  8.6 23.0 %copy-start.7 = (f32[1536]{0:T(1024)S(1)}, f32[1536]{0:T(1024)}, u32[]{:S(2)}) copy-start(f32[1536]{0:T(1024)} %param.22) | copy-start | bytes 18436
  8.6 23.1 %copy-start.8 = (f32[1536]{0:T(1024)S(1)}, f32[1536]{0:T(1024)}, u32[]{:S(2)}) copy-start(f32[1536]{0:T(1024)} %param.20) | copy-start | bytes 18436
  17.8 14.5 %collective-permute-start = (bf16[1,2,384,128]{3,2,1,0:T(8,128)(2,1)}, bf16[1,2,384,128]{3,2,1,0:T(8,128)(2,1)}, u32[]{:S(2)}, u32[]{:S(2)}) collective-permute-start(bf16[1,2,384,128]{3,2,1,0:T(8,128)(2,1)} %get-tuple-element.73), channel_id=1, source_target_pairs={{0,32},{32,0},{64,96},{96,64},{1,33},{33,1},{65,97},{97,65},{2,34}... | collective-permute-start | bytes 589832 | tf_op jit(solution)/shard_map/ppermute | solution.py:762
  19.3 13.0 %collective-permute-start.1 = (bf16[1,2,384,128]{3,2,1,0:T(8,128)(2,1)}, bf16[1,2,384,128]{3,2,1,0:T(8,128)(2,1)}, u32[]{:S(2)}, u32[]{:S(2)}) collective-permute-start(bf16[1,2,384,128]{3,2,1,0:T(8,128)(2,1)} %get-tuple-element.74), channel_id=1, source_target_pairs={{0,64},{32,96},{64,0},{96,32},{1,65},{33,97},{65,1},{97,33},{2,66}... | collective-permute-start | bytes 589832 | tf_op jit(solution)/shard_map/ppermute | solution.py:762
  20.6 11.7 %collective-permute-start.2 = (bf16[1,2,384,128]{3,2,1,0:T(8,128)(2,1)}, bf16[1,2,384,128]{3,2,1,0:T(8,128)(2,1)}, u32[]{:S(2)}, u32[]{:S(2)}) collective-permute-start(bf16[1,2,384,128]{3,2,1,0:T(8,128)(2,1)} %get-tuple-element.75), channel_id=1, source_target_pairs={{0,96},{32,64},{64,32},{96,0},{1,97},{33,65},{65,33},{97,1},{2,98}... | collective-permute-start | bytes 589832 | tf_op jit(solution)/shard_map/ppermute | solution.py:762
  21.0 31.3 %all-to-all-start = ((bf16[32,2,48,128]{3,2,1,0:T(8,128)(2,1)}), bf16[32,2,48,128]{3,2,1,0:T(8,128)(2,1)S(1)}, u32[]{:S(2)}, u32[]{:S(2)}) async-start(bf16[32,2,48,128]{3,2,1,0:T(8,128)(2,1)} %get-tuple-element.80), calls=%async_computation | async-start | bytes 1572864 | tf_op jit(solution)/shard_map/all_to_all | solution.py:766
  50.1 33.1 %collective-permute-start.3 = (bf16[1,2,384,128]{3,2,1,0:T(8,128)(2,1)}, bf16[1,2,384,128]{3,2,1,0:T(8,128)(2,1)S(1)}, u32[]{:S(2)}, u32[]{:S(2)}) collective-permute-start(bf16[1,2,384,128]{3,2,1,0:T(8,128)(2,1)} %get-tuple-element.77), channel_id=1, source_target_pairs={{0,32},{32,0},{64,96},{96,64},{1,33},{33,1},{65,97},{97,65},{2,34}... | collective-permute-start | bytes 589832 | tf_op jit(solution)/shard_map/ppermute | solution.py:762
  50.6 32.5 %collective-permute-start.4 = (bf16[1,2,384,128]{3,2,1,0:T(8,128)(2,1)}, bf16[1,2,384,128]{3,2,1,0:T(8,128)(2,1)}, u32[]{:S(2)}, u32[]{:S(2)}) collective-permute-start(bf16[1,2,384,128]{3,2,1,0:T(8,128)(2,1)} %get-tuple-element.78), channel_id=1, source_target_pairs={{0,64},{32,96},{64,0},{96,32},{1,65},{33,97},{65,1},{97,33},{2,66}... | collective-permute-start | bytes 589832 | tf_op jit(solution)/shard_map/ppermute | solution.py:762
  51.1 32.0 %collective-permute-start.5 = (bf16[1,2,384,128]{3,2,1,0:T(8,128)(2,1)}, bf16[1,2,384,128]{3,2,1,0:T(8,128)(2,1)}, u32[]{:S(2)}, u32[]{:S(2)}) collective-permute-start(bf16[1,2,384,128]{3,2,1,0:T(8,128)(2,1)} %get-tuple-element.79), channel_id=1, source_target_pairs={{0,96},{32,64},{64,32},{96,0},{1,97},{33,65},{65,33},{97,1},{2,98}... | collective-permute-start | bytes 589832 | tf_op jit(solution)/shard_map/ppermute | solution.py:762
  52.3 0.9 copy-start.3
  73.5 30.2 %all-to-all-start.1 = ((bf16[32,2,48,128]{3,2,1,0:T(8,128)(2,1)}), bf16[32,2,48,128]{3,2,1,0:T(8,128)(2,1)S(1)}, u32[]{:S(2)}, u32[]{:S(2)}) async-start(bf16[32,2,48,128]{3,2,1,0:T(8,128)(2,1)} %get-tuple-element.82), calls=%async_computation.1 | async-start | bytes 1572864 | tf_op jit(solution)/shard_map/all_to_all | solution.py:766
  83.1 20.6 %copy-start.9 = (bf16[1,2,384,128]{3,2,1,0:T(8,128)(2,1)}, bf16[1,2,384,128]{3,2,1,0:T(8,128)(2,1)S(1)}, u32[]{:S(2)}) copy-start(bf16[1,2,384,128]{3,2,1,0:T(8,128)(2,1)S(1)} %collective-permute-done.3.refs_6_) | copy-start | bytes 589828
  108.8 26.0 %all-to-all-start.2 = ((bf16[16,192,128]{2,1,0:T(8,128)(2,1)}), bf16[16,192,128]{2,1,0:T(8,128)(2,1)S(1)}, u32[]{:S(2)}, u32[]{:S(2)}) async-start(bf16[16,192,128]{2,1,0:T(8,128)(2,1)} %get-tuple-element.98), calls=%async_computation.2 | async-start | bytes 1572864 | tf_op jit(solution)/shard_map/all_to_all | solution.py:766
  134.8 0.9 copy-start.2
  141.7 29.5 %all-to-all-start.3 = ((bf16[128,40,128]{2,1,0:T(8,128)(2,1)}), bf16[128,40,128]{2,1,0:T(8,128)(2,1)}, u32[]{:S(2)}, u32[]{:S(2)}) async-start(bf16[128,40,128]{2,1,0:T(8,128)(2,1)} %in_weight_grad.1), calls=%async_computation.3 | async-start | bytes 2621440 | tf_op jit(solution)/shard_map/all_to_all | solution.py:766
  150.9 11.5 %copy-start.6 = (bf16[128,1536]{1,0:T(8,128)(2,1)S(1)}, bf16[128,1536]{1,0:T(8,128)(2,1)}, u32[]{:S(2)}) copy-start(bf16[128,1536]{1,0:T(8,128)(2,1)} %get-tuple-element.96) | copy-start | bytes 1179652
  150.9 12.4 %copy-start.5 = (bf16[128,1536]{1,0:T(8,128)(2,1)S(1)}, bf16[128,1536]{1,0:T(8,128)(2,1)}, u32[]{:S(2)}) copy-start(bf16[128,1536]{1,0:T(8,128)(2,1)} %get-tuple-element.97) | copy-start | bytes 1179652
  155.6 15.7 %copy-start = (bf16[8,256]{1,0:T(8,128)(2,1)S(1)}, bf16[8,256]{1,0:T(8,128)(2,1)}, u32[]{:S(2)}) copy-start(bf16[8,256]{1,0:T(8,128)(2,1)} %broadcast_in_dim.13.refs_5_.feature_ref) | copy-start | bytes 12292
  155.6 2.4 %collective-permute-start.6 = (bf16[4,144,128]{2,1,0:T(8,128)(2,1)}, bf16[4,144,128]{2,1,0:T(8,128)(2,1)S(1)}, u32[]{:S(2)}, u32[]{:S(2)}) collective-permute-start(bf16[4,144,128]{2,1,0:T(8,128)(2,1)} %get-tuple-element.120), channel_id=1, source_target_pairs={{0,32},{16,48},{32,0},{48,16},{64,96},{80,112},{96,64},{112,80},{1... | collective-permute-start | bytes 442376 | tf_op jit(solution)/shard_map/ppermute | solution.py:762
  158.0 1.0 copy-start.1
  159.0 9.4 %collective-permute-start.7 = (bf16[144,128]{1,0:T(8,128)(2,1)S(1)}, bf16[144,128]{1,0:T(8,128)(2,1)S(1)}, u32[]{:S(2)}, u32[]{:S(2)}) collective-permute-start(bf16[144,128]{1,0:T(8,128)(2,1)S(1)} %get-tuple-element.122), channel_id=1, source_target_pairs={{0,16},{16,0},{32,48},{48,32},{64,80},{80,64},{96,112},{112,96},{1... | collective-permute-start | bytes 110600 | tf_op jit(solution)/shard_map/ppermute | solution.py:762
  161.2 7.2 %collective-permute-start.8 = (bf16[144,128]{1,0:T(8,128)(2,1)S(1)}, bf16[144,128]{1,0:T(8,128)(2,1)S(1)}, u32[]{:S(2)}, u32[]{:S(2)}) collective-permute-start(bf16[144,128]{1,0:T(8,128)(2,1)S(1)} %get-tuple-element.123), channel_id=1, source_target_pairs={{0,64},{16,80},{32,96},{48,112},{64,0},{80,16},{96,32},{112,48},{1... | collective-permute-start | bytes 110600 | tf_op jit(solution)/shard_map/ppermute | solution.py:762
  161.5 7.2 %collective-permute-start.9 = (bf16[144,128]{1,0:T(8,128)(2,1)S(1)}, bf16[144,128]{1,0:T(8,128)(2,1)S(1)}, u32[]{:S(2)}, u32[]{:S(2)}) collective-permute-start(bf16[144,128]{1,0:T(8,128)(2,1)S(1)} %get-tuple-element.124), channel_id=1, source_target_pairs={{0,80},{16,64},{32,112},{48,96},{64,16},{80,0},{96,48},{112,32},{1... | collective-permute-start | bytes 110600 | tf_op jit(solution)/shard_map/ppermute | solution.py:762
  (1 other events, 0.9 us)
Sparse Core Ops, SparseCore 0:
  17.9 115.6 all-gather.2

commit v5 on v4

--- a/solution.py
+++ b/solution.py
@@ -16,7 +16,7 @@
 EIGHT = 9
 LOG2E = math.log2(math.e)
 MEGA = 1024 * 1024
-VMEM_ALL = 63
+VMEM_ALL = 60
 PIECES = 4
 SLOT = 16
 AXES = ("xl", "core", "xh", "y", "z")
@@ -151,13 +151,13 @@
 def pre_kernel(
     wait,
     send,
-    latent_ref,
-    grad_ref,
-    w_in_ref,
-    w_out_ref,
+    place_ref,
     w_mod_ref,
     feature_ref,
-    place_ref,
+    latent_ref,
+    w_in_ref,
+    grad_ref,
+    w_out_ref,
     own_ref,
     wide_ref,
     slot_0_ref,
@@ -178,19 +178,20 @@
     )
     mod_ref[...] = modulation
     send(8)
+    wait(3)
     latent = latent_ref[...].astype(F32).reshape(tokens, width)
     rows_ref[...] = latent.astype(BF)
     send(10)
     normed, _ = normalise(latent)
     shifted = (normed * (1.0 + modulation[:1, width:]) + modulation[:1, :width]).astype(BF)
     both_ref[0] = shifted
-    wait(1)
-    both_ref[1] = grad_ref[...].astype(F32).reshape(tokens, width).astype(BF)
-    send(6)
-    wait(2)
+    wait(4)
     pre_act = jnp.dot(shifted, w_in_ref[...], preferred_element_type=F32)
     pre_ref[...] = pre_act
     send(7)
+    wait(5)
+    both_ref[1] = grad_ref[...].astype(F32).reshape(tokens, width).astype(BF)
+    send(6)
     activ = (pre_act * jax.nn.sigmoid(pre_act)).astype(BF)
 
     def pack(which, value):
@@ -208,7 +209,7 @@
             send(n, which)
 
     pack(0, activ)
-    wait(3)
+    wait(6)
     cot = lax.dot_general(both_ref[1], w_out_ref[...], NT, preferred_element_type=F32).astype(BF)
     cot_ref[...] = cot
     send(9)
@@ -326,6 +327,7 @@
     low_ref[...] = low
     send(4)
     wait(1)
+    wait(2)
     w_dt = jnp.concatenate([wdt_ref[...], jnp.zeros((2 * states, inner), BF)], axis=0)
     pre = jnp.dot(low, w_dt, preferred_element_type=F32) + bias_ref[:1, :]
     pre_ref[...] = pre
@@ -335,6 +337,7 @@
         at = slice(j * tokens, (j + 1) * tokens)
         dt_row_ref[at, :] = spacing[:, cut(j)]
         dx_row_ref[at, :] = spacing[:, cut(j)] * xf_ref[:, cut(j)]
+    wait(3)
     rates = -jnp.exp(alog_ref[...])
     rate_ref[...] = rates
     rate2_ref[...] = rates * LOG2E
@@ -512,7 +515,7 @@
         2e10,
         (order, place, *data, *params),
         smem=(0, 1),
-        late=tuple(2 + len(data) + i for i in (0, 1)),
+        late=tuple(2 + len(data) + i for i in range(4)),
         early=tuple(range(len(data) + 5)),
     )
     return results[: len(data)], results[len(data) :]
@@ -658,11 +661,11 @@
     vec_ref[...] = halves_product(chosen, choose, False)
     grad_normed = grad_shifted * (1.0 + mod_ref[:1, width:])
     product = jnp.mean(grad_normed * normed, axis=1, keepdims=True)
-    latent_grad_ref[...] = (inverse * (grad_normed - normed * product)).astype(BF)
+    result = inverse * (grad_normed - normed * product)
+    latent_grad_ref[...] = result.reshape(latent_grad_ref.shape).astype(BF)
     wait(5)
-    branch_ref[...] = jnp.dot(
-        mixed_ref[...], w_out_ref[...], preferred_element_type=F32
-    ).astype(BF)
+    result = jnp.dot(mixed_ref[...], w_out_ref[...], preferred_element_type=F32)
+    branch_ref[...] = result.reshape(branch_ref.shape).astype(BF)
 
 
 def long_product(wait, at, left, right_ref):
@@ -685,8 +688,10 @@
     own = rows // FAR_SIZE
     for s in range(near):
         right_ref[:, cut(s)] = recv_ref[s, rows:]
+    product = long_product(wait, 1, right_ref, both_ref)
+    wait(2)
+    wait(3)
     all_ref[:, SLOT:] = small_ref[...]
-    product = long_product(wait, 1, right_ref, both_ref)
     turned = jnp.concatenate([product, jnp.zeros((LANES - rows, width), F32)], axis=0).T
     for d in range(devices):
         rows_ref[d * SLOT : d * SLOT + own, :] = turned[d * own : (d + 1) * own]
@@ -818,9 +823,9 @@
         [((tokens * tiles, LANES), F32)],
         VMEM_ALL,
         7e9,
-        (latent, out_grad, w_in, w_out, w_mod, feature_rows, place),
-        smem=(6,),
-        late=(1, 2, 3),
+        (place, w_mod, feature_rows, latent, w_in, out_grad, w_out),
+        smem=(0,),
+        late=(3, 4, 5, 6),
         early=tuple(range(11)),
     )
     data_wide = exchange(data_wide, COL)
@@ -906,7 +911,7 @@
     branch, latent_grad, vec = call(
         finish_kernel,
         "out_projections",
-        [((tokens, width), BF), ((tokens, width), BF), ((near * far, LANES), F32)],
+        [(latent.shape, BF), (latent.shape, BF), ((near * far, LANES), F32)],
         [],
         VMEM_ALL,
         6e9,
@@ -923,7 +928,7 @@
         VMEM_ALL,
         3e9,
         (near_recv, both_near, small_send, vec),
-        late=(1,),
+        late=(1, 2, 3),
         pieces={1: PIECES},
         choose={1: 0},
     )[0]
@@ -975,8 +980,8 @@
         (all_recv, feature_rows, *far_recv),
     )
     return (
-        branch.reshape(latent.shape),
-        latent_grad.reshape(latent.shape),
+        branch,
+        latent_grad,
         grad_w_in,
         grad_w_out,
         grad_select,

time: 182 us -> 178 us (0.978)
  Pallas kernels: 97 us -> 94.5 us
    ppermute x10, waiting for transfers between devices: 5.79 us -> 7.99 us  [permute(): lax.ppermute(value, axes, [(i, i ^ k) for i in range(lax.axis_size(axes))])]
    unnamed x20 -> x26, local copies, waits for them, and re-layouts: 3.65 us -> 4.53 us
  transfers between devices with their start and end apart: 15 -> 15, of which waited for: 5 -> 5; matrix products, arithmetic and copies ran while one was open for 1% -> 0% of each run, Pallas kernels for 44% -> 46%
where the time goes in v5:
time: 178 us; the launch traced here: 177 us
  Pallas kernels  94.5 us (53%)
  starting transfers between devices  44.9 us (25%)
  waiting for transfers between devices  16.4 us (9%)
  between operations  15 us (8%)
  local copies, waits for them, and re-layouts  5.66 us (3%)
    pallas_call x9, Pallas kernels, call(): pl.pallas_call(body, out_shape=tuple((jax.ShapeDtypeStruct(s, d) for s, d...  93.6 us
    all_to_all x4, starting transfers between devices, exchange(): return lax.all_to_all(value, axes, split_axis=0, concat_axis=0, tiled=True)  34.9 us
    ppermute x10, starting transfers between devices, permute(): lax.ppermute(value, axes, [(i, i ^ k) for i in range(lax.axis_size(axes))])  9.96 us
    all_to_all x4, waiting for transfers between devices, exchange(): return lax.all_to_all(value, axes, split_axis=0, concat_axis=0, tiled=True)  8.37 us
    ppermute x10, waiting for transfers between devices, permute(): lax.ppermute(value, axes, [(i, i ^ k) for i in range(lax.axis_size(axes))])  7.99 us
    unnamed x26, local copies, waits for them, and re-layouts  4.53 us
  transfers between devices with their start and end apart: 15, of which 5 were waited for; matrix products, arithmetic and copies ran while one was open for 0% of the time, Pallas kernels for 46%

profile of v5, /device:TPU:1, one launch (start us, length us, event | category | flops | bytes accessed | tf_op | source)
XLA Modules:
  0.0 177.2 jit_solution(10750446774577361063)
XLA Ops:
  8.6 7.7 %norm_project.1 = (bf16[1,2,1536,128]{3,2,1,0:T(8,128)(2,1)}, bf16[32,2,48,128]{3,2,1,0:T(8,128)(2,1)}, bf16[1,2,384,128]{3,2,1,0:T(8,128)(2,1)}, bf16[1,2,384,1...) custom-call(s32[1]{0:T(128)} %bitcast.refs_0_.refs_1_, ...), custom_call_target="tpu_custom_call" | custom-call | flops 7000000000 | bytes 11800580 | tf_op jit(solution)/shard_map/norm_project/pallas_call | solution.py:94
  16.3 1.5 collective-permute-start
  17.8 1.3 collective-permute-start.1
  19.5 10.6 %all-to-all-start = ((bf16[32,2,48,128]{3,2,1,0:T(8,128)(2,1)}), bf16[32,2,48,128]{3,2,1,0:T(8,128)(2,1)S(1)}, u32[]{:S(2)}, u32[]{:S(2)}) async-start(bf16[32,2,48,128]{3,2,1,0:T(8,128)(2,1)} %get-tuple-element.80), calls=%async_computation | async-start | bytes 1572864 | tf_op jit(solution)/shard_map/all_to_all | solution.py:771
  31.6 17.9 %scan_height.1 = (bf16[1,2,384,128]{3,2,1,0:T(8,128)(2,1)}, bf16[1,2,384,128]{3,2,1,0:T(8,128)(2,1)}, bf16[1,2,384,128]{3,2,1,0:T(8,128)(2,1)}, bf16[1,2,384,128...) custom-call(s32[8]{0:T(128)} %refs_0_.3, ...), custom_call_target="tpu_custom_call" | custom-call | flops 20000000000 | bytes 1585188 | tf_op jit(solution)/shard_map/scan_height/pallas_call | solution.py:94
  50.4 1.4 collective-permute-start.5
  52.7 20.5 %scan_width.1 = (bf16[32,2,48,128]{3,2,1,0:T(8,128)(2,1)}, bf16[128,1536]{1,0:T(8,128)(2,1)}, bf16[128,1536]{1,0:T(8,128)(2,1)}, bf16[128,128]{1,0:T(8,128)(2,1)...) custom-call(s32[64]{0:T(128)} %refs_0_.4, s32[1]{0:T(128)} %bitcast.refs_0_.refs_1_, bf16[32,2,48,128]{3,2,1,0:T(8,128)(2,1)} %copy-done.3, ...), custom_call_target="tpu_custom_call" | custom-call | flops 20000000000 | bytes 1585412 | tf_op jit(solution)/shard_map/scan_width/pallas_call | solution.py:94
  73.2 9.6 %all-to-all-start.1 = ((bf16[32,2,48,128]{3,2,1,0:T(8,128)(2,1)}), bf16[32,2,48,128]{3,2,1,0:T(8,128)(2,1)S(1)}, u32[]{:S(2)}, u32[]{:S(2)}) async-start(bf16[32,2,48,128]{3,2,1,0:T(8,128)(2,1)} %get-tuple-element.82), calls=%async_computation.1 | async-start | bytes 1572864 | tf_op jit(solution)/shard_map/all_to_all | solution.py:771
  82.9 20.7 %scan_time.1 = (bf16[1,2,1536,128]{3,2,1,0:T(8,128)(2,1)}, bf16[128,1536]{1,0:T(8,128)(2,1)}, bf16[128,1536]{1,0:T(8,128)(2,1)}, bf16[128,128]{1,0:T(8,128)(2,1)...) custom-call(s32[32]{0:T(128)} %refs_0_.5, s32[1]{0:T(128)} %bitcast.refs_0_.refs_1_, ...), custom_call_target="tpu_custom_call" | custom-call | flops 20000000000 | bytes 1585284 | tf_op jit(solution)/shard_map/scan_time/pallas_call | solution.py:94
  104.5 4.4 %sum_directions.1 = (bf16[128,1536]{1,0:T(8,128)(2,1)}, bf16[128,1536]{1,0:T(8,128)(2,1)}, bf16[16,192,128]{2,1,0:T(8,128)(2,1)}) custom-call(s32[1]{0:T(128)} %bitcast.refs_0_.refs_1_, bf16[128,1536]{1,0:T(8,128)(2,1)} %get-tuple-element.84.refs_1_, bf16[128,1536]{1,0:T(8,128)(2,1)} %get-tuple-element.85.refs_2_, ...), custom_call_target="tpu_custom_call" | custom-call | flops 6000000000 | bytes 3944452 | tf_op jit(solution)/shard_map/sum_directions/pallas_call | solution.py:94
  108.9 6.4 %all-to-all-start.2 = ((bf16[16,192,128]{2,1,0:T(8,128)(2,1)}), bf16[16,192,128]{2,1,0:T(8,128)(2,1)S(1)}, u32[]{:S(2)}, u32[]{:S(2)}) async-start(bf16[16,192,128]{2,1,0:T(8,128)(2,1)} %get-tuple-element.98), calls=%async_computation.2 | async-start | bytes 1572864 | tf_op jit(solution)/shard_map/all_to_all | solution.py:771
  115.3 4.3 %small_sums.1.refs_2_ = bf16[128,24,128]{2,1,0:T(8,128)(2,1)} custom-call(bf16[1,2,1536,128]{3,2,1,0:T(8,128)(2,1)} %get-tuple-element.100.refs_2_.refs_0_, bf16[128,1536]{1,0:T(8,128)(2,1)} %get-tuple-element.84.refs_1_, bf16[128,1536]{1,0:T(8,128)(2,1)} %get-tuple-element.101.refs_2_, bf16[128,128]{1,0:T(8,128)(2,1)} %get-tuple-element.102.refs_3_, ...), custom_call_target="tpu_custom_call" | custom-call | flops 3000000000 | bytes 3784704 | tf_op jit(solution)/shard_map/small_sums/pallas_call | solution.py:94
  119.7 8.2 %out_projections.1 = (bf16[32,2,2,1536]{3,2,1,0:T(2,128)(2,1)}, bf16[32,2,2,1536]{3,2,1,0:T(2,128)(2,1)}, f32[128,128]{1,0:T(8,128)}) custom-call(bf16[128,1536]{1,0:T(8,128)(2,1)} %get-tuple-element.92.refs_0_, bf16[128,1536]{1,0:T(8,128)(2,1)} %get-tuple-element.93.refs_1_, bf16[128,1536]{1,0:T(8,128)(2,1)} %get-tuple-element.94.refs_2_, ...), custom_call_target="tpu_custom_call" | custom-call | flops 6000000000 | bytes 10715136 | tf_op jit(solution)/shard_map/out_projections/pallas_call | solution.py:94
  127.8 5.8 %all-to-all-done.2.refs_0_.refs_1_ = bf16[16,192,128]{2,1,0:T(8,128)(2,1)S(1)} async-done(((bf16[16,192,128]{2,1,0:T(8,128)(2,1)}), bf16[16,192,128]{2,1,0:T(8,128)(2,1)S(1)}, u32[]{:S(2)}, u32[]{:S(2)}) %all-to-all-start.2) | async-done | bytes 786464 | tf_op jit(solution)/shard_map/all_to_all | solution.py:771
  134.5 5.2 %in_weight_grad.1 = bf16[128,40,128]{2,1,0:T(8,128)(2,1)} custom-call(bf16[16,192,128]{2,1,0:T(8,128)(2,1)} %copy-done.2, bf16[16,2,128,1536]{3,2,1,0:T(8,128)(2,1)} %bitcast.10, bf16[128,24,128]{2,1,0:T(8,128)(2,1)} %small_sums.1.refs_2_, f32[128,128]{1,0:T(8,128)} %get-tuple-element.118.refs_3_), custom_call_target="tpu_custom_call" | custom-call | flops 3000000000 | bytes 14221312 | tf_op jit(solution)/shard_map/in_weight_grad/pallas_call | solution.py:94
  139.8 8.4 %all-to-all-start.3 = ((bf16[128,40,128]{2,1,0:T(8,128)(2,1)}), bf16[128,40,128]{2,1,0:T(8,128)(2,1)S(1)}, u32[]{:S(2)}, u32[]{:S(2)}) async-start(bf16[128,40,128]{2,1,0:T(8,128)(2,1)} %in_weight_grad.1), calls=%async_computation.3 | async-start | bytes 2621440 | tf_op jit(solution)/shard_map/all_to_all | solution.py:771
  148.2 4.7 %out_weight_grad.1 = (f32[4,144,128]{2,1,0:T(8,128)}, bf16[4,144,128]{2,1,0:T(8,128)(2,1)}) custom-call(s32[1]{0:T(128)} %bitcast.5.refs_0_, bf16[16,192,128]{2,1,0:T(8,128)(2,1)} %copy-done.2, bf16[16,2,128,1536]{3,2,1,0:T(8,128)(2,1)} %bitcast.11), custom_call_target="tpu_custom_call" | custom-call | flops 4000000000 | bytes 13369348 | tf_op jit(solution)/shard_map/out_weight_grad/pallas_call | solution.py:94
  152.9 1.1 collective-permute-start.6
  154.0 1.2 collective-permute-done.6.other_ref
  155.2 1.0 copy-done.1
  156.2 2.3 %collective-permute-start.7 = (bf16[144,128]{1,0:T(8,128)(2,1)S(1)}, bf16[144,128]{1,0:T(8,128)(2,1)S(1)}, u32[]{:S(2)}, u32[]{:S(2)}) collective-permute-start(bf16[144,128]{1,0:T(8,128)(2,1)S(1)} %get-tuple-element.122), channel_id=1, source_target_pairs={{0,16},{16,0},{32,48},{48,32},{64,80},{80,64},{96,112},{112,96},{1... | collective-permute-start | bytes 110600 | tf_op jit(solution)/shard_map/ppermute | solution.py:767
  159.6 6.4 %collective-permute-done.7.refs_1_ = bf16[144,128]{1,0:T(8,128)(2,1)S(1)} collective-permute-done((bf16[144,128]{1,0:T(8,128)(2,1)S(1)}, bf16[144,128]{1,0:T(8,128)(2,1)S(1)}, u32[]{:S(2)}, u32[]{:S(2)}) %collective-permute-start.7) | collective-permute-done | bytes 36896 | tf_op jit(solution)/shard_map/ppermute | solution.py:767
  166.3 2.6 %all-to-all-done.3.all_ref = bf16[128,40,128]{2,1,0:T(8,128)(2,1)S(1)} async-done(((bf16[128,40,128]{2,1,0:T(8,128)(2,1)}), bf16[128,40,128]{2,1,0:T(8,128)(2,1)S(1)}, u32[]{:S(2)}, u32[]{:S(2)}) %all-to-all-start.3) | async-done | bytes 1310752 | tf_op jit(solution)/shard_map/all_to_all | solution.py:771
  168.9 0.9 weight_sums.1
  (51 shorter events, 8.2 us)
Async XLA Ops:
  7.2 126.5 %all-gather.3.cloned.1.call-start = ((), (), s32[]{:S(2)}) async-start(), calls=%async_computation.4 | async-start | bytes 13369344 | tf_op jit(solution)/shard_map/all_gather | solution.py:833
  8.6 21.5 %copy-start.5 = (f32[1536]{0:T(1024)S(1)}, f32[1536]{0:T(1024)}, u32[]{:S(2)}) copy-start(f32[1536]{0:T(1024)} %param.22) | copy-start | bytes 18436
  8.6 21.6 %copy-start.6 = (f32[1536]{0:T(1024)S(1)}, f32[1536]{0:T(1024)}, u32[]{:S(2)}) copy-start(f32[1536]{0:T(1024)} %param.20) | copy-start | bytes 18436
  16.3 14.5 %collective-permute-start = (bf16[1,2,384,128]{3,2,1,0:T(8,128)(2,1)}, bf16[1,2,384,128]{3,2,1,0:T(8,128)(2,1)S(1)}, u32[]{:S(2)}, u32[]{:S(2)}) collective-permute-start(bf16[1,2,384,128]{3,2,1,0:T(8,128)(2,1)} %get-tuple-element.73), channel_id=1, source_target_pairs={{0,32},{32,0},{64,96},{96,64},{1,33},{33,1},{65,97},{97,65},{2,34}... | collective-permute-start | bytes 589832 | tf_op jit(solution)/shard_map/ppermute | solution.py:767
  17.8 13.0 %collective-permute-start.1 = (bf16[1,2,384,128]{3,2,1,0:T(8,128)(2,1)}, bf16[1,2,384,128]{3,2,1,0:T(8,128)(2,1)S(1)}, u32[]{:S(2)}, u32[]{:S(2)}) collective-permute-start(bf16[1,2,384,128]{3,2,1,0:T(8,128)(2,1)} %get-tuple-element.74), channel_id=1, source_target_pairs={{0,64},{32,96},{64,0},{96,32},{1,65},{33,97},{65,1},{97,33},{2,66}... | collective-permute-start | bytes 589832 | tf_op jit(solution)/shard_map/ppermute | solution.py:767
  19.1 11.7 %collective-permute-start.2 = (bf16[1,2,384,128]{3,2,1,0:T(8,128)(2,1)}, bf16[1,2,384,128]{3,2,1,0:T(8,128)(2,1)S(1)}, u32[]{:S(2)}, u32[]{:S(2)}) collective-permute-start(bf16[1,2,384,128]{3,2,1,0:T(8,128)(2,1)} %get-tuple-element.75), channel_id=1, source_target_pairs={{0,96},{32,64},{64,32},{96,0},{1,97},{33,65},{65,33},{97,1},{2,98}... | collective-permute-start | bytes 589832 | tf_op jit(solution)/shard_map/ppermute | solution.py:767
  19.5 32.3 %all-to-all-start = ((bf16[32,2,48,128]{3,2,1,0:T(8,128)(2,1)}), bf16[32,2,48,128]{3,2,1,0:T(8,128)(2,1)S(1)}, u32[]{:S(2)}, u32[]{:S(2)}) async-start(bf16[32,2,48,128]{3,2,1,0:T(8,128)(2,1)} %get-tuple-element.80), calls=%async_computation | async-start | bytes 1572864 | tf_op jit(solution)/shard_map/all_to_all | solution.py:771
  49.5 33.3 %collective-permute-start.3 = (bf16[1,2,384,128]{3,2,1,0:T(8,128)(2,1)}, bf16[1,2,384,128]{3,2,1,0:T(8,128)(2,1)S(1)}, u32[]{:S(2)}, u32[]{:S(2)}) collective-permute-start(bf16[1,2,384,128]{3,2,1,0:T(8,128)(2,1)} %get-tuple-element.77), channel_id=1, source_target_pairs={{0,32},{32,0},{64,96},{96,64},{1,33},{33,1},{65,97},{97,65},{2,34}... | collective-permute-start | bytes 589832 | tf_op jit(solution)/shard_map/ppermute | solution.py:767
  50.1 32.7 %collective-permute-start.4 = (bf16[1,2,384,128]{3,2,1,0:T(8,128)(2,1)}, bf16[1,2,384,128]{3,2,1,0:T(8,128)(2,1)S(1)}, u32[]{:S(2)}, u32[]{:S(2)}) collective-permute-start(bf16[1,2,384,128]{3,2,1,0:T(8,128)(2,1)} %get-tuple-element.78), channel_id=1, source_target_pairs={{0,64},{32,96},{64,0},{96,32},{1,65},{33,97},{65,1},{97,33},{2,66}... | collective-permute-start | bytes 589832 | tf_op jit(solution)/shard_map/ppermute | solution.py:767
  50.4 32.4 %collective-permute-start.5 = (bf16[1,2,384,128]{3,2,1,0:T(8,128)(2,1)}, bf16[1,2,384,128]{3,2,1,0:T(8,128)(2,1)S(1)}, u32[]{:S(2)}, u32[]{:S(2)}) collective-permute-start(bf16[1,2,384,128]{3,2,1,0:T(8,128)(2,1)} %get-tuple-element.79), channel_id=1, source_target_pairs={{0,96},{32,64},{64,32},{96,0},{1,97},{33,65},{65,33},{97,1},{2,98}... | collective-permute-start | bytes 589832 | tf_op jit(solution)/shard_map/ppermute | solution.py:767
  51.8 0.9 copy-start.3
  73.2 30.3 %all-to-all-start.1 = ((bf16[32,2,48,128]{3,2,1,0:T(8,128)(2,1)}), bf16[32,2,48,128]{3,2,1,0:T(8,128)(2,1)S(1)}, u32[]{:S(2)}, u32[]{:S(2)}) async-start(bf16[32,2,48,128]{3,2,1,0:T(8,128)(2,1)} %get-tuple-element.82), calls=%async_computation.1 | async-start | bytes 1572864 | tf_op jit(solution)/shard_map/all_to_all | solution.py:771
  82.8 20.7 %copy-start.7 = (bf16[1,2,384,128]{3,2,1,0:T(8,128)(2,1)}, bf16[1,2,384,128]{3,2,1,0:T(8,128)(2,1)S(1)}, u32[]{:S(2)}) copy-start(bf16[1,2,384,128]{3,2,1,0:T(8,128)(2,1)S(1)} %collective-permute-done.3.refs_6_) | copy-start | bytes 589828
  82.8 20.7 %copy-start.8 = (bf16[1,2,384,128]{3,2,1,0:T(8,128)(2,1)}, bf16[1,2,384,128]{3,2,1,0:T(8,128)(2,1)S(1)}, u32[]{:S(2)}) copy-start(bf16[1,2,384,128]{3,2,1,0:T(8,128)(2,1)S(1)} %collective-permute-done.4.refs_7_) | copy-start | bytes 589828
  82.8 20.7 %copy-start.9 = (bf16[1,2,384,128]{3,2,1,0:T(8,128)(2,1)}, bf16[1,2,384,128]{3,2,1,0:T(8,128)(2,1)S(1)}, u32[]{:S(2)}) copy-start(bf16[1,2,384,128]{3,2,1,0:T(8,128)(2,1)S(1)} %collective-permute-done.5.refs_8_) | copy-start | bytes 589828
  108.9 24.7 %all-to-all-start.2 = ((bf16[16,192,128]{2,1,0:T(8,128)(2,1)}), bf16[16,192,128]{2,1,0:T(8,128)(2,1)S(1)}, u32[]{:S(2)}, u32[]{:S(2)}) async-start(bf16[16,192,128]{2,1,0:T(8,128)(2,1)} %get-tuple-element.98), calls=%async_computation.2 | async-start | bytes 1572864 | tf_op jit(solution)/shard_map/all_to_all | solution.py:771
  133.6 0.9 copy-start.2
  139.8 29.1 %all-to-all-start.3 = ((bf16[128,40,128]{2,1,0:T(8,128)(2,1)}), bf16[128,40,128]{2,1,0:T(8,128)(2,1)S(1)}, u32[]{:S(2)}, u32[]{:S(2)}) async-start(bf16[128,40,128]{2,1,0:T(8,128)(2,1)} %in_weight_grad.1), calls=%async_computation.3 | async-start | bytes 2621440 | tf_op jit(solution)/shard_map/all_to_all | solution.py:771
  148.2 20.7 %copy-start = (bf16[8,256]{1,0:T(8,128)(2,1)S(1)}, bf16[8,256]{1,0:T(8,128)(2,1)}, u32[]{:S(2)}) copy-start(bf16[8,256]{1,0:T(8,128)(2,1)} %broadcast_in_dim.13.refs_2_.feature_ref) | copy-start | bytes 12292
  152.9 2.4 %collective-permute-start.6 = (bf16[4,144,128]{2,1,0:T(8,128)(2,1)}, bf16[4,144,128]{2,1,0:T(8,128)(2,1)S(1)}, u32[]{:S(2)}, u32[]{:S(2)}) collective-permute-start(bf16[4,144,128]{2,1,0:T(8,128)(2,1)} %get-tuple-element.120), channel_id=1, source_target_pairs={{0,32},{16,48},{32,0},{48,16},{64,96},{80,112},{96,64},{112,80},{1... | collective-permute-start | bytes 442376 | tf_op jit(solution)/shard_map/ppermute | solution.py:767
  155.2 1.0 copy-start.1
  156.2 9.8 %collective-permute-start.7 = (bf16[144,128]{1,0:T(8,128)(2,1)S(1)}, bf16[144,128]{1,0:T(8,128)(2,1)S(1)}, u32[]{:S(2)}, u32[]{:S(2)}) collective-permute-start(bf16[144,128]{1,0:T(8,128)(2,1)S(1)} %get-tuple-element.122), channel_id=1, source_target_pairs={{0,16},{16,0},{32,48},{48,32},{64,80},{80,64},{96,112},{112,96},{1... | collective-permute-start | bytes 110600 | tf_op jit(solution)/shard_map/ppermute | solution.py:767
  158.5 7.5 %collective-permute-start.8 = (bf16[144,128]{1,0:T(8,128)(2,1)S(1)}, bf16[144,128]{1,0:T(8,128)(2,1)S(1)}, u32[]{:S(2)}, u32[]{:S(2)}) collective-permute-start(bf16[144,128]{1,0:T(8,128)(2,1)S(1)} %get-tuple-element.123), channel_id=1, source_target_pairs={{0,64},{16,80},{32,96},{48,112},{64,0},{80,16},{96,32},{112,48},{1... | collective-permute-start | bytes 110600 | tf_op jit(solution)/shard_map/ppermute | solution.py:767
  158.8 7.5 %collective-permute-start.9 = (bf16[144,128]{1,0:T(8,128)(2,1)S(1)}, bf16[144,128]{1,0:T(8,128)(2,1)S(1)}, u32[]{:S(2)}, u32[]{:S(2)}) collective-permute-start(bf16[144,128]{1,0:T(8,128)(2,1)S(1)} %get-tuple-element.124), channel_id=1, source_target_pairs={{0,80},{16,64},{32,112},{48,96},{64,16},{80,0},{96,48},{112,32},{1... | collective-permute-start | bytes 110600 | tf_op jit(solution)/shard_map/ppermute | solution.py:767
  (4 other events, 3.2 us)
Sparse Core Ops, SparseCore 0:
  16.4 115.2 all-gather.2

commit v6 on v5

--- a/solution.py
+++ b/solution.py
@@ -174,7 +174,10 @@
     tokens, width = rows_ref.shape
     tiles = w_in_ref.shape[1] // LANES
     modulation = lax.dot_general(
-        feature_ref[...], w_mod_ref[...], NT, preferred_element_type=F32
+        jnp.broadcast_to(feature_ref[...].reshape(1, -1), (8, feature_ref.shape[0])),
+        w_mod_ref[...],
+        NT,
+        preferred_element_type=F32,
     )
     mod_ref[...] = modulation
     send(8)
@@ -329,7 +332,7 @@
     wait(1)
     wait(2)
     w_dt = jnp.concatenate([wdt_ref[...], jnp.zeros((2 * states, inner), BF)], axis=0)
-    pre = jnp.dot(low, w_dt, preferred_element_type=F32) + bias_ref[:1, :]
+    pre = jnp.dot(low, w_dt, preferred_element_type=F32) + bias_ref[...].reshape(1, inner)
     pre_ref[...] = pre
     spacing = jnp.maximum(pre, 0.0) + jnp.log1p(jnp.exp(-jnp.abs(pre)))
     dt_ref[...] = spacing
@@ -353,6 +356,16 @@
     hist_ref[pl.ds(0, states), :] = jnp.zeros((states, GROUP * LANES), F32)
     unroll = min(length, 8)
 
+    def repeat(step, carry):
+        def block(n, carry):
+            for inside in range(unroll):
+                carry = step(n, inside, carry)
+            return carry
+
+        if length == unroll:
+            return block(0, carry)
+        return lax.fori_loop(0, length // unroll, block, carry)
+
     def fold(value):
         return value[:8] + value[8:]
 
@@ -363,14 +376,16 @@
         rate1 = [rate_ref[:, c] for c in cuts]
 
         def one_line(line, grads):
-            def places(step):
-                row = row_of(order_ref[step], line, place_ref[0])
+            def places(block, inside):
+                row = row_of(order_ref[block * unroll + inside], line, place_ref[0])
                 at = pl.ds(pl.multiple_of(row * states, states), states)
-                slot = pl.ds(pl.multiple_of((step + 1) * states, states), states)
-                return row, row * EIGHT, at, slot
-
-            def forward(step, carry):
-                row, at_8, at, slot = places(step)
+                base = pl.multiple_of(block * (unroll * states), unroll * states)
+                slot = pl.ds(base + (inside + 1) * states, states)
+                prev = pl.ds(base + inside * states, states)
+                return row, row * EIGHT, at, slot, prev
+
+            def forward(block, inside, carry):
+                row, at_8, at, slot, _ = places(block, inside)
                 bb, cb = bb_ref[at, :], cb_ref[at, :]
                 new = []
                 for j in range(GROUP):
@@ -384,12 +399,11 @@
                     new.append(h)
                 return tuple(new)
 
-            lax.fori_loop(0, length, forward, (zero,) * GROUP, unroll=unroll)
-
-            def backward(back_step, carry):
-                step = length - 1 - back_step
-                row, at_8, at, slot = places(step)
-                prev = pl.ds(pl.multiple_of(step * states, states), states)
+            repeat(forward, (zero,) * GROUP)
+
+            def backward(block, inside, carry):
+                last = length // unroll - 1
+                row, at_8, at, slot, prev = places(last - block, unroll - 1 - inside)
                 bb, cb = bb_ref[at, :], cb_ref[at, :]
                 pend, acc = carry
                 gb = gb_ref[at, :]
@@ -413,7 +427,7 @@
                 return tuple(new), tuple(acc_new)
 
             start = ((zero,) * GROUP, grads)
-            return lax.fori_loop(0, length, backward, start, unroll=unroll)[1]
+            return repeat(backward, start)[1]
 
         grads = lax.fori_loop(0, lines, one_line, (zero,) * GROUP)
         for j in range(GROUP):
@@ -521,13 +535,12 @@
     return results[: len(data)], results[len(data) :]
 
 
-def small_kernel(own_ref, *refs):
+def small_kernel(place_ref, own_ref, *refs):
     found, refs = [refs[5 * d : 5 * d + 5] for d in range(3)], refs[15:]
-    send_ref, row_ref, turned_ref, held_ref = refs
+    mine_ref, other_ref, row_ref, turned_ref = refs
     inner = found[0][0].shape[1]
     tiles = inner // LANES
     tokens = own_ref.shape[2] // tiles
-    own = inner // send_ref.shape[0]
     states = found[0][4].shape[0] - 8
     rank = LANES - 2 * states
     row_ref[...] = own_ref[0, 0].astype(F32) * own_ref[0, 1].astype(F32)
@@ -553,11 +566,9 @@
     turned_ref[1] = vectors.T + lax.dot_general(
         grad_pre, low, TN, preferred_element_type=F32
     )
-    for d in range(send_ref.shape[0]):
-        for which in (0, 1):
-            begin = (2 * d + which) * own
-            held_ref[begin : begin + own, :] = turned_ref[which, d * own : (d + 1) * own, :]
-    send_ref[...] = held_ref[...].reshape(send_ref.shape).astype(BF)
+    core = place_ref[0] & 1
+    mine_ref[...] = turned_ref[core]
+    other_ref[...] = turned_ref[1 - core].astype(BF)
 
 
 def spread_rows(ref, which, own, near, held_ref):
@@ -605,7 +616,7 @@
             at = pl.ds(pl.multiple_of((place_ref[0] ^ k) * chunk, chunk), chunk)
             sum_ref[at, :] += ref[0, which].astype(F32)
         scans = jnp.concatenate([from_flat(sum_ref, j, tokens, tiles) for j in range(tiles)], axis=1)
-        return scans + skip_ref[1:, :] * own_ref[...].astype(F32)
+        return scans + skip_ref[...].reshape(1, inner) * own_ref[...].astype(F32)
 
     back = summed(1, cot_ref)
     pre_act = pre_ref[...]
@@ -680,7 +691,9 @@
     return total(terms)
 
 
-def in_grad_kernel(wait, recv_ref, both_ref, small_ref, vec_ref, all_ref, right_ref, rows_ref):
+def in_grad_kernel(
+    wait, recv_ref, both_ref, mine_ref, other_ref, vec_ref, all_ref, right_ref, rows_ref
+):
     near = recv_ref.shape[0]
     rows = right_ref.shape[0]
     width = both_ref.shape[2]
@@ -689,15 +702,19 @@
     for s in range(near):
         right_ref[:, cut(s)] = recv_ref[s, rows:]
     product = long_product(wait, 1, right_ref, both_ref)
-    wait(2)
-    wait(3)
-    all_ref[:, SLOT:] = small_ref[...]
+    for n in (2, 3, 4):
+        wait(n)
+    mine_ref[...] += other_ref[...].astype(F32)
     turned = jnp.concatenate([product, jnp.zeros((LANES - rows, width), F32)], axis=0).T
+    step = 2 * SLOT
     for d in range(devices):
-        rows_ref[d * SLOT : d * SLOT + own, :] = turned[d * own : (d + 1) * own]
+        begin = d * step
+        rows_ref[begin : begin + own, :] = turned[d * own : (d + 1) * own]
+        rows_ref[begin + SLOT : begin + SLOT + own, :] = mine_ref[d * own : (d + 1) * own, :]
     for n in range(own, SLOT):
-        rows_ref[pl.ds(n, devices, stride=SLOT), :] = vec_ref[...]
-    all_ref[:, :SLOT] = rows_ref[...].reshape(devices, SLOT, LANES).astype(BF)
+        rows_ref[pl.ds(n, devices, stride=step), :] = vec_ref[...]
+        rows_ref[pl.ds(SLOT + n, devices, stride=step), :] = jnp.zeros((devices, LANES), F32)
+    all_ref[...] = rows_ref[...].reshape(devices, step, LANES).astype(BF)
 
 
 def pair_place(place, core_flip, slot):
@@ -745,16 +762,20 @@
         gwo_ref[:, cut(j)] = sum_ref[pl.ds(j, own, stride=tiles), :]
     rest = []
     for m in range(near):
-        block = total([all_ref[o * near + m].astype(F32) for o in range(far)])
-        gwi_ref[:, part * m : part * (m + 1)] = block[:own, :part]
-        rest.append(block)
-    rest_ref[...] = total(rest)
-    vec = rest_ref[own : own + 1, :]
+        cores = [
+            total([all_ref[o * near + m].astype(F32) for o in range(far) if o // 2 % 2 == core])
+            for core in (0, 1)
+        ]
+        gwi_ref[:, part * m : part * (m + 1)] = (cores[0] + cores[1])[:own, :part]
+        rest.append(cores)
+    rest_ref[: 2 * SLOT, :] = total([c[0] for c in rest])
+    rest_ref[2 * SLOT :, :] = total([c[1] for c in rest])
+    vec = rest_ref[own : own + 1, :] + rest_ref[2 * SLOT + own : 2 * SLOT + own + 1, :]
     turned = jnp.broadcast_to(vec, (LANES, LANES)).T
-    gmod_ref[...] = turned[: 2 * own, :1] * feature_ref[:1, :].astype(F32)
+    gmod_ref[...] = turned[: 2 * own, :1] * feature_ref[...].reshape(1, -1).astype(F32)
     gsel_ref[...] = rest_ref[SLOT : SLOT + own, :]
     rank, states = gdt_ref.shape[1], galog_ref.shape[1]
-    base = SLOT + own
+    base = 3 * SLOT
     gdt_ref[...] = rest_ref[base : base + own, :rank]
     galog_ref[...] = rest_ref[base : base + own, rank : rank + states]
     turned = jnp.concatenate([rest_ref[base : base + own, :], jnp.zeros((LANES - own, LANES), F32)])
@@ -796,7 +817,6 @@
     near, far = lax.axis_size(NEAR), lax.axis_size(FAR)
     own = width // (near * far)
     features = jax.nn.silu(time_features(t_index, w_mod.shape[1])).astype(BF)
-    feature_rows = jnp.broadcast_to(features[None, :], (8, features.shape[0]))
 
     def packed(parts):
         return ((parts, 2, tokens * tiles // parts, LANES), BF)
@@ -823,7 +843,7 @@
         [((tokens * tiles, LANES), F32)],
         VMEM_ALL,
         7e9,
-        (place, w_mod, feature_rows, latent, w_in, out_grad, w_out),
+        (place, w_mod, features, latent, w_in, out_grad, w_out),
         smem=(0,),
         late=(3, 4, 5, 6),
         early=tuple(range(11)),
@@ -831,11 +851,10 @@
     data_wide = exchange(data_wide, COL)
     slots = [permute(value, ROW, k) for k, value in enumerate(slots)]
     both_near = lax.all_gather(both, NEAR, axis=0, tiled=False)
-    vectors = jnp.stack([dt_bias, d_skip])
     params = (
         w_select,
         w_dt.T,
-        vectors,
+        dt_bias,
         a_log.T,
     )
     area = rows * cols
@@ -889,25 +908,23 @@
         ],
         VMEM_ALL,
         6e9,
-        (place, grads_time[0], cot, out_time, out_wide, *out_slots, pre_act, vectors),
+        (place, grads_time[0], cot, out_time, out_wide, *out_slots, pre_act, d_skip),
         smem=(0,),
         early=(0, 1),
     )
     near_recv = exchange(near_send, NEAR)
     data_own, _ = lax.optimization_barrier((data_own, near_send))
-    small_send = call(
+    mine, other = call(
         small_kernel,
         "small_sums",
-        [((near * far, 2 * own, LANES), BF)],
-        [
-            ((tokens * tiles, LANES), F32),
-            ((2, inner, LANES), F32),
-            ((2 * inner, LANES), F32),
-        ],
+        [((inner, LANES), F32), ((inner, LANES), BF)],
+        [((tokens * tiles, LANES), F32), ((2, inner, LANES), F32)],
         VMEM_ALL,
         3e9,
-        (data_own, *grads_time, *grads_wide, *grads_tall),
-    )[0]
+        (place, data_own, *grads_time, *grads_wide, *grads_tall),
+        smem=(0,),
+    )
+    other = permute(other, ROW, 1)
     branch, latent_grad, vec = call(
         finish_kernel,
         "out_projections",
@@ -918,17 +935,17 @@
         (mixed, grad_act, flat_latent, modulation, w_in, w_out),
         late=(4, 5),
     )
-    near_recv, vec, small_send = lax.optimization_barrier((near_recv, vec, small_send))
+    near_recv, vec, mine, other = lax.optimization_barrier((near_recv, vec, mine, other))
     piece = own * tiles
     all_send = call(
         in_grad_kernel,
         "in_weight_grad",
-        [((near * far, SLOT + 2 * own, LANES), BF)],
-        [((inner // near, near * tokens), BF), ((near * far * SLOT, LANES), F32)],
+        [((near * far, 2 * SLOT, LANES), BF)],
+        [((inner // near, near * tokens), BF), ((near * far * 2 * SLOT, LANES), F32)],
         VMEM_ALL,
         3e9,
-        (near_recv, both_near, small_send, vec),
-        late=(1, 2, 3),
+        (near_recv, both_near, mine, other, vec),
+        late=(1, 2, 3, 4),
         pieces={1: PIECES},
         choose={1: 0},
     )[0]
@@ -974,10 +991,10 @@
             ((8, own), F32),
             ((2 * own, features.shape[0]), F32),
         ],
-        [((piece, LANES), F32), ((SLOT + 2 * own, LANES), F32)],
+        [((piece, LANES), F32), ((4 * SLOT, LANES), F32)],
         16,
         1e9,
-        (all_recv, feature_rows, *far_recv),
+        (all_recv, features, *far_recv),
     )
     return (
         branch,

time: 178 us -> 176 us (0.989)
  waiting for transfers between devices: 16.4 us -> 13.3 us
    ppermute x10 -> x11, waiting for transfers between devices: 7.99 us -> 5.36 us  [permute(): lax.ppermute(value, axes, [(i, i ^ k) for i in range(lax.axis_size(axes))])]
    ppermute x10 -> x11, starting transfers between devices: 9.96 us -> 11 us  [permute(): lax.ppermute(value, axes, [(i, i ^ k) for i in range(lax.axis_size(axes))])]
    unnamed x26 -> x24, local copies, waits for them, and re-layouts: 4.53 us -> 4.46 us
  transfers between devices with their start and end apart: 15 -> 16, of which waited for: 5 -> 5; matrix products, arithmetic and copies ran while one was open for 0% -> 0% of each run, Pallas kernels for 46% -> 46%
where the time goes in v6:
time: 176 us; the launch traced here: 175 us
  Pallas kernels  94.5 us (54%)
  starting transfers between devices  46.6 us (26%)
  between operations  15 us (9%)
  waiting for transfers between devices  13.3 us (8%)
  local copies, waits for them, and re-layouts  4.98 us (3%)
    pallas_call x9, Pallas kernels, call(): pl.pallas_call(body, out_shape=tuple((jax.ShapeDtypeStruct(s, d) for s, d...  93.6 us
    all_to_all x4, starting transfers between devices, exchange(): return lax.all_to_all(value, axes, split_axis=0, concat_axis=0, tiled=True)  35.6 us
    ppermute x11, starting transfers between devices, permute(): lax.ppermute(value, axes, [(i, i ^ k) for i in range(lax.axis_size(axes))])  11 us
    all_to_all x4, waiting for transfers between devices, exchange(): return lax.all_to_all(value, axes, split_axis=0, concat_axis=0, tiled=True)  7.94 us
    ppermute x11, waiting for transfers between devices, permute(): lax.ppermute(value, axes, [(i, i ^ k) for i in range(lax.axis_size(axes))])  5.36 us
    unnamed x24, local copies, waits for them, and re-layouts  4.46 us
  transfers between devices with their start and end apart: 16, of which 5 were waited for; matrix products, arithmetic and copies ran while one was open for 0% of the time, Pallas kernels for 46%

profile of v6, /device:TPU:1, one launch (start us, length us, event | category | flops | bytes accessed | tf_op | source)
XLA Modules:
  0.0 175.0 jit_solution(11897341660687598938)
XLA Ops:
  8.5 7.6 %norm_project.1 = (bf16[1,2,1536,128]{3,2,1,0:T(8,128)(2,1)}, bf16[32,2,48,128]{3,2,1,0:T(8,128)(2,1)}, bf16[1,2,384,128]{3,2,1,0:T(8,128)(2,1)}, bf16[1,2,384,1...) custom-call(s32[1]{0:T(128)} %bitcast.refs_0_.refs_1_, ...), custom_call_target="tpu_custom_call" | custom-call | flops 7000000000 | bytes 11796996 | tf_op jit(solution)/shard_map/norm_project/pallas_call | solution.py:94
  16.1 1.5 collective-permute-start
  17.6 1.3 collective-permute-start.1
  19.4 10.6 %all-to-all-start = ((bf16[32,2,48,128]{3,2,1,0:T(8,128)(2,1)}), bf16[32,2,48,128]{3,2,1,0:T(8,128)(2,1)S(1)}, u32[]{:S(2)}, u32[]{:S(2)}) async-start(bf16[32,2,48,128]{3,2,1,0:T(8,128)(2,1)} %get-tuple-element.83), calls=%async_computation | async-start | bytes 1572864 | tf_op jit(solution)/shard_map/all_to_all | solution.py:792
  30.8 17.8 %scan_height.1 = (bf16[1,2,384,128]{3,2,1,0:T(8,128)(2,1)}, bf16[1,2,384,128]{3,2,1,0:T(8,128)(2,1)}, bf16[1,2,384,128]{3,2,1,0:T(8,128)(2,1)}, bf16[1,2,384,128...) custom-call(s32[8]{0:T(128)} %refs_0_.3, ...), custom_call_target="tpu_custom_call" | custom-call | flops 20000000000 | bytes 1579044 | tf_op jit(solution)/shard_map/scan_height/pallas_call | solution.py:94
  49.6 1.3 collective-permute-start.5
  51.8 20.5 %scan_width.1 = (bf16[32,2,48,128]{3,2,1,0:T(8,128)(2,1)}, bf16[128,1536]{1,0:T(8,128)(2,1)}, bf16[128,1536]{1,0:T(8,128)(2,1)}, bf16[128,128]{1,0:T(8,128)(2,1)...) custom-call(s32[64]{0:T(128)} %refs_0_.4, s32[1]{0:T(128)} %bitcast.refs_0_.refs_1_, bf16[32,2,48,128]{3,2,1,0:T(8,128)(2,1)} %copy-done.3, ...), custom_call_target="tpu_custom_call" | custom-call | flops 20000000000 | bytes 1579268 | tf_op jit(solution)/shard_map/scan_width/pallas_call | solution.py:94
  72.3 9.6 %all-to-all-start.1 = ((bf16[32,2,48,128]{3,2,1,0:T(8,128)(2,1)}), bf16[32,2,48,128]{3,2,1,0:T(8,128)(2,1)S(1)}, u32[]{:S(2)}, u32[]{:S(2)}) async-start(bf16[32,2,48,128]{3,2,1,0:T(8,128)(2,1)} %get-tuple-element.85), calls=%async_computation.1 | async-start | bytes 1572864 | tf_op jit(solution)/shard_map/all_to_all | solution.py:792
  81.9 20.5 %scan_time.1 = (bf16[1,2,1536,128]{3,2,1,0:T(8,128)(2,1)}, bf16[128,1536]{1,0:T(8,128)(2,1)}, bf16[128,1536]{1,0:T(8,128)(2,1)}, bf16[128,128]{1,0:T(8,128)(2,1)...) custom-call(s32[32]{0:T(128)} %refs_0_.5, s32[1]{0:T(128)} %bitcast.refs_0_.refs_1_, ...), custom_call_target="tpu_custom_call" | custom-call | flops 20000000000 | bytes 1579140 | tf_op jit(solution)/shard_map/scan_time/pallas_call | solution.py:94
  103.3 4.3 %sum_directions.1 = (bf16[128,1536]{1,0:T(8,128)(2,1)}, bf16[128,1536]{1,0:T(8,128)(2,1)}, bf16[16,192,128]{2,1,0:T(8,128)(2,1)}) custom-call(s32[1]{0:T(128)} %bitcast.refs_0_.refs_1_, bf16[128,1536]{1,0:T(8,128)(2,1)} %get-tuple-element.87.refs_1_.refs_2_, bf16[128,1536]{1,0:T(8,128)(2,1)} %get-tuple-element.88.refs_2_, ...), custom_call_target="tpu_custom_call" | custom-call | flops 6000000000 | bytes 3938308 | tf_op jit(solution)/shard_map/sum_directions/pallas_call | solution.py:94
  107.6 6.7 %all-to-all-start.2 = ((bf16[16,192,128]{2,1,0:T(8,128)(2,1)}), bf16[16,192,128]{2,1,0:T(8,128)(2,1)S(1)}, u32[]{:S(2)}, u32[]{:S(2)}) async-start(bf16[16,192,128]{2,1,0:T(8,128)(2,1)} %get-tuple-element.101), calls=%async_computation.2 | async-start | bytes 1572864 | tf_op jit(solution)/shard_map/all_to_all | solution.py:792
  114.3 4.5 %small_sums.1 = (f32[1536,128]{1,0:T(8,128)}, bf16[1536,128]{1,0:T(8,128)(2,1)}) custom-call(s32[1]{0:T(128)} %bitcast.refs_0_.refs_1_, bf16[1,2,1536,128]{3,2,1,0:T(8,128)(2,1)} %get-tuple-element.103.refs_2_.refs_1_, bf16[128,1536]{1,0:T(8,128)(2,1)} %get-tuple-element.87.refs_1_.refs_2_, bf16[128,1536]{1,0:T(8,128)(2,1)} %get-tuple-element.104.refs_3_, ...), custom_call_target="tpu_custom_call" | custom-call | flops 3000000000 | bytes 3784708 | tf_op jit(solution)/shard_map/small_sums/pallas_call | solution.py:94
  118.8 1.1 collective-permute-start.6
  119.9 8.2 %out_projections.1 = (bf16[32,2,2,1536]{3,2,1,0:T(2,128)(2,1)}, bf16[32,2,2,1536]{3,2,1,0:T(2,128)(2,1)}, f32[128,128]{1,0:T(8,128)}) custom-call(bf16[128,1536]{1,0:T(8,128)(2,1)} %get-tuple-element.95.refs_0_, bf16[128,1536]{1,0:T(8,128)(2,1)} %get-tuple-element.96.refs_1_, bf16[128,1536]{1,0:T(8,128)(2,1)} %get-tuple-element.97.refs_2_, ...), custom_call_target="tpu_custom_call" | custom-call | flops 6000000000 | bytes 10715136 | tf_op jit(solution)/shard_map/out_projections/pallas_call | solution.py:94
  128.1 5.0 %all-to-all-done.2.refs_0_.refs_1_ = bf16[16,192,128]{2,1,0:T(8,128)(2,1)S(1)} async-done(((bf16[16,192,128]{2,1,0:T(8,128)(2,1)}), bf16[16,192,128]{2,1,0:T(8,128)(2,1)S(1)}, u32[]{:S(2)}, u32[]{:S(2)}) %all-to-all-start.2) | async-done | bytes 786464 | tf_op jit(solution)/shard_map/all_to_all | solution.py:792
  134.1 5.6 %in_weight_grad.1 = bf16[128,32,128]{2,1,0:T(8,128)(2,1)} custom-call(bf16[16,192,128]{2,1,0:T(8,128)(2,1)} %copy-done.2, bf16[16,2,128,1536]{3,2,1,0:T(8,128)(2,1)} %bitcast.10, f32[1536,128]{1,0:T(8,128)} %get-tuple-element.122.refs_2_, bf16[1536,128]{1,0:T(8,128)(2,1)} %copy-done.5, f32[128,128]{1,0:T(8,128)} %get-tuple-element.124.refs_4_), custom_call_target="tpu_custom_call" | custom-call | flops 3000000000 | bytes 14614528 | tf_op jit(solution)/shard_map/in_weight_grad/pallas_call | solution.py:94
  139.7 8.7 %all-to-all-start.3 = ((bf16[128,32,128]{2,1,0:T(8,128)(2,1)}), bf16[128,32,128]{2,1,0:T(8,128)(2,1)S(1)}, u32[]{:S(2)}, u32[]{:S(2)}) async-start(bf16[128,32,128]{2,1,0:T(8,128)(2,1)} %in_weight_grad.1), calls=%async_computation.3 | async-start | bytes 2097152 | tf_op jit(solution)/shard_map/all_to_all | solution.py:792
  148.4 4.6 %out_weight_grad.1 = (f32[4,144,128]{2,1,0:T(8,128)}, bf16[4,144,128]{2,1,0:T(8,128)(2,1)}) custom-call(s32[1]{0:T(128)} %bitcast.5.refs_0_, bf16[16,192,128]{2,1,0:T(8,128)(2,1)} %copy-done.2, bf16[16,2,128,1536]{3,2,1,0:T(8,128)(2,1)} %bitcast.11), custom_call_target="tpu_custom_call" | custom-call | flops 4000000000 | bytes 13369348 | tf_op jit(solution)/shard_map/out_weight_grad/pallas_call | solution.py:94
  153.0 1.1 collective-permute-start.7
  154.2 1.2 collective-permute-done.7.other_ref
  155.4 1.0 copy-done.1
  156.4 2.3 %collective-permute-start.8 = (bf16[144,128]{1,0:T(8,128)(2,1)S(1)}, bf16[144,128]{1,0:T(8,128)(2,1)S(1)}, u32[]{:S(2)}, u32[]{:S(2)}) collective-permute-start(bf16[144,128]{1,0:T(8,128)(2,1)S(1)} %get-tuple-element.128), channel_id=1, source_target_pairs={{0,16},{16,0},{32,48},{48,32},{64,80},{80,64},{96,112},{112,96},{1... | collective-permute-start | bytes 110600 | tf_op jit(solution)/shard_map/ppermute | solution.py:788
  159.7 3.7 %collective-permute-done.8.refs_1_ = bf16[144,128]{1,0:T(8,128)(2,1)S(1)} collective-permute-done((bf16[144,128]{1,0:T(8,128)(2,1)S(1)}, bf16[144,128]{1,0:T(8,128)(2,1)S(1)}, u32[]{:S(2)}, u32[]{:S(2)}) %collective-permute-start.8) | collective-permute-done | bytes 36896 | tf_op jit(solution)/shard_map/ppermute | solution.py:788
  163.8 2.9 %all-to-all-done.3.all_ref = bf16[128,32,128]{2,1,0:T(8,128)(2,1)S(1)} async-done(((bf16[128,32,128]{2,1,0:T(8,128)(2,1)}), bf16[128,32,128]{2,1,0:T(8,128)(2,1)S(1)}, u32[]{:S(2)}, u32[]{:S(2)}) %all-to-all-start.3) | async-done | bytes 1048608 | tf_op jit(solution)/shard_map/all_to_all | solution.py:792
  (47 shorter events, 8.5 us)
Async XLA Ops:
  7.2 126.0 %all-gather.3.cloned.1.call-start = ((), (), s32[]{:S(2)}) async-start(), calls=%async_computation.4 | async-start | bytes 13369344 | tf_op jit(solution)/shard_map/all_gather | solution.py:853
  16.1 13.8 %collective-permute-start = (bf16[1,2,384,128]{3,2,1,0:T(8,128)(2,1)}, bf16[1,2,384,128]{3,2,1,0:T(8,128)(2,1)S(1)}, u32[]{:S(2)}, u32[]{:S(2)}) collective-permute-start(bf16[1,2,384,128]{3,2,1,0:T(8,128)(2,1)} %get-tuple-element.76), channel_id=1, source_target_pairs={{0,32},{32,0},{64,96},{96,64},{1,33},{33,1},{65,97},{97,65},{2,34}... | collective-permute-start | bytes 589832 | tf_op jit(solution)/shard_map/ppermute | solution.py:788
  17.6 12.4 %collective-permute-start.1 = (bf16[1,2,384,128]{3,2,1,0:T(8,128)(2,1)}, bf16[1,2,384,128]{3,2,1,0:T(8,128)(2,1)S(1)}, u32[]{:S(2)}, u32[]{:S(2)}) collective-permute-start(bf16[1,2,384,128]{3,2,1,0:T(8,128)(2,1)} %get-tuple-element.77), channel_id=1, source_target_pairs={{0,64},{32,96},{64,0},{96,32},{1,65},{33,97},{65,1},{97,33},{2,66}... | collective-permute-start | bytes 589832 | tf_op jit(solution)/shard_map/ppermute | solution.py:788
  19.0 11.1 %collective-permute-start.2 = (bf16[1,2,384,128]{3,2,1,0:T(8,128)(2,1)}, bf16[1,2,384,128]{3,2,1,0:T(8,128)(2,1)S(1)}, u32[]{:S(2)}, u32[]{:S(2)}) collective-permute-start(bf16[1,2,384,128]{3,2,1,0:T(8,128)(2,1)} %get-tuple-element.78), channel_id=1, source_target_pairs={{0,96},{32,64},{64,32},{96,0},{1,97},{33,65},{65,33},{97,1},{2,98}... | collective-permute-start | bytes 589832 | tf_op jit(solution)/shard_map/ppermute | solution.py:788
  19.4 31.5 %all-to-all-start = ((bf16[32,2,48,128]{3,2,1,0:T(8,128)(2,1)}), bf16[32,2,48,128]{3,2,1,0:T(8,128)(2,1)S(1)}, u32[]{:S(2)}, u32[]{:S(2)}) async-start(bf16[32,2,48,128]{3,2,1,0:T(8,128)(2,1)} %get-tuple-element.83), calls=%async_computation | async-start | bytes 1572864 | tf_op jit(solution)/shard_map/all_to_all | solution.py:792
  48.6 33.3 %collective-permute-start.3 = (bf16[1,2,384,128]{3,2,1,0:T(8,128)(2,1)}, bf16[1,2,384,128]{3,2,1,0:T(8,128)(2,1)S(1)}, u32[]{:S(2)}, u32[]{:S(2)}) collective-permute-start(bf16[1,2,384,128]{3,2,1,0:T(8,128)(2,1)} %get-tuple-element.80), channel_id=1, source_target_pairs={{0,32},{32,0},{64,96},{96,64},{1,33},{33,1},{65,97},{97,65},{2,34}... | collective-permute-start | bytes 589832 | tf_op jit(solution)/shard_map/ppermute | solution.py:788
  49.1 32.8 %collective-permute-start.4 = (bf16[1,2,384,128]{3,2,1,0:T(8,128)(2,1)}, bf16[1,2,384,128]{3,2,1,0:T(8,128)(2,1)S(1)}, u32[]{:S(2)}, u32[]{:S(2)}) collective-permute-start(bf16[1,2,384,128]{3,2,1,0:T(8,128)(2,1)} %get-tuple-element.81), channel_id=1, source_target_pairs={{0,64},{32,96},{64,0},{96,32},{1,65},{33,97},{65,1},{97,33},{2,66}... | collective-permute-start | bytes 589832 | tf_op jit(solution)/shard_map/ppermute | solution.py:788
  49.6 32.3 %collective-permute-start.5 = (bf16[1,2,384,128]{3,2,1,0:T(8,128)(2,1)}, bf16[1,2,384,128]{3,2,1,0:T(8,128)(2,1)S(1)}, u32[]{:S(2)}, u32[]{:S(2)}) collective-permute-start(bf16[1,2,384,128]{3,2,1,0:T(8,128)(2,1)} %get-tuple-element.82), channel_id=1, source_target_pairs={{0,96},{32,64},{64,32},{96,0},{1,97},{33,65},{65,33},{97,1},{2,98}... | collective-permute-start | bytes 589832 | tf_op jit(solution)/shard_map/ppermute | solution.py:788
  50.9 0.9 copy-start.3
  72.3 30.1 %all-to-all-start.1 = ((bf16[32,2,48,128]{3,2,1,0:T(8,128)(2,1)}), bf16[32,2,48,128]{3,2,1,0:T(8,128)(2,1)S(1)}, u32[]{:S(2)}, u32[]{:S(2)}) async-start(bf16[32,2,48,128]{3,2,1,0:T(8,128)(2,1)} %get-tuple-element.85), calls=%async_computation.1 | async-start | bytes 1572864 | tf_op jit(solution)/shard_map/all_to_all | solution.py:792
  81.9 20.5 %copy-start.6 = (bf16[1,2,384,128]{3,2,1,0:T(8,128)(2,1)}, bf16[1,2,384,128]{3,2,1,0:T(8,128)(2,1)S(1)}, u32[]{:S(2)}) copy-start(bf16[1,2,384,128]{3,2,1,0:T(8,128)(2,1)S(1)} %collective-permute-done.3.refs_6_) | copy-start | bytes 589828
  81.9 20.5 %copy-start.7 = (bf16[1,2,384,128]{3,2,1,0:T(8,128)(2,1)}, bf16[1,2,384,128]{3,2,1,0:T(8,128)(2,1)S(1)}, u32[]{:S(2)}) copy-start(bf16[1,2,384,128]{3,2,1,0:T(8,128)(2,1)S(1)} %collective-permute-done.4.refs_7_) | copy-start | bytes 589828
  81.9 20.5 %copy-start.8 = (bf16[1,2,384,128]{3,2,1,0:T(8,128)(2,1)}, bf16[1,2,384,128]{3,2,1,0:T(8,128)(2,1)S(1)}, u32[]{:S(2)}) copy-start(bf16[1,2,384,128]{3,2,1,0:T(8,128)(2,1)S(1)} %collective-permute-done.5.refs_8_) | copy-start | bytes 589828
  107.6 25.5 %all-to-all-start.2 = ((bf16[16,192,128]{2,1,0:T(8,128)(2,1)}), bf16[16,192,128]{2,1,0:T(8,128)(2,1)S(1)}, u32[]{:S(2)}, u32[]{:S(2)}) async-start(bf16[16,192,128]{2,1,0:T(8,128)(2,1)} %get-tuple-element.101), calls=%async_computation.2 | async-start | bytes 1572864 | tf_op jit(solution)/shard_map/all_to_all | solution.py:792
  118.8 9.3 %collective-permute-start.6 = (bf16[1536,128]{1,0:T(8,128)(2,1)}, bf16[1536,128]{1,0:T(8,128)(2,1)S(1)}, u32[]{:S(2)}, u32[]{:S(2)}) collective-permute-start(bf16[1536,128]{1,0:T(8,128)(2,1)} %get-tuple-element.119), channel_id=1, source_target_pairs={{0,32},{32,0},{64,96},{96,64},{1,33},{33,1},{65,97},{97,65},{2,34}... | collective-permute-start | bytes 1179656 | tf_op jit(solution)/shard_map/ppermute | solution.py:788
  128.1 5.1 %copy-start.5 = (bf16[1536,128]{1,0:T(8,128)(2,1)}, bf16[1536,128]{1,0:T(8,128)(2,1)S(1)}, u32[]{:S(2)}) copy-start(bf16[1536,128]{1,0:T(8,128)(2,1)S(1)} %collective-permute-done.6.refs_3_) | copy-start | bytes 1179652
  133.2 0.9 copy-start.2
  139.7 27.1 %all-to-all-start.3 = ((bf16[128,32,128]{2,1,0:T(8,128)(2,1)}), bf16[128,32,128]{2,1,0:T(8,128)(2,1)S(1)}, u32[]{:S(2)}, u32[]{:S(2)}) async-start(bf16[128,32,128]{2,1,0:T(8,128)(2,1)} %in_weight_grad.1), calls=%async_computation.3 | async-start | bytes 2097152 | tf_op jit(solution)/shard_map/all_to_all | solution.py:792
  148.4 18.3 %copy-start = (bf16[256]{0:T(256)(128)(2,1)S(1)}, bf16[256]{0:T(256)(128)(2,1)}, u32[]{:S(2)}) copy-start(bf16[256]{0:T(256)(128)(2,1)} %fusion.refs_2_.feature_ref) | copy-start | bytes 1540
  153.0 2.4 %collective-permute-start.7 = (bf16[4,144,128]{2,1,0:T(8,128)(2,1)}, bf16[4,144,128]{2,1,0:T(8,128)(2,1)S(1)}, u32[]{:S(2)}, u32[]{:S(2)}) collective-permute-start(bf16[4,144,128]{2,1,0:T(8,128)(2,1)} %get-tuple-element.126), channel_id=1, source_target_pairs={{0,32},{16,48},{32,0},{48,16},{64,96},{80,112},{96,64},{112,80},{1... | collective-permute-start | bytes 442376 | tf_op jit(solution)/shard_map/ppermute | solution.py:788
  155.4 1.0 copy-start.1
  156.4 7.0 %collective-permute-start.8 = (bf16[144,128]{1,0:T(8,128)(2,1)S(1)}, bf16[144,128]{1,0:T(8,128)(2,1)S(1)}, u32[]{:S(2)}, u32[]{:S(2)}) collective-permute-start(bf16[144,128]{1,0:T(8,128)(2,1)S(1)} %get-tuple-element.128), channel_id=1, source_target_pairs={{0,16},{16,0},{32,48},{48,32},{64,80},{80,64},{96,112},{112,96},{1... | collective-permute-start | bytes 110600 | tf_op jit(solution)/shard_map/ppermute | solution.py:788
  158.6 4.8 %collective-permute-start.9 = (bf16[144,128]{1,0:T(8,128)(2,1)S(1)}, bf16[144,128]{1,0:T(8,128)(2,1)S(1)}, u32[]{:S(2)}, u32[]{:S(2)}) collective-permute-start(bf16[144,128]{1,0:T(8,128)(2,1)S(1)} %get-tuple-element.129), channel_id=1, source_target_pairs={{0,64},{16,80},{32,96},{48,112},{64,0},{80,16},{96,32},{112,48},{1... | collective-permute-start | bytes 110600 | tf_op jit(solution)/shard_map/ppermute | solution.py:788
  158.9 4.9 %collective-permute-start.10 = (bf16[144,128]{1,0:T(8,128)(2,1)S(1)}, bf16[144,128]{1,0:T(8,128)(2,1)S(1)}, u32[]{:S(2)}, u32[]{:S(2)}) collective-permute-start(bf16[144,128]{1,0:T(8,128)(2,1)S(1)} %get-tuple-element.130), channel_id=1, source_target_pairs={{0,80},{16,64},{32,112},{48,96},{64,16},{80,0},{96,48},{112,32},{1... | collective-permute-start | bytes 110600 | tf_op jit(solution)/shard_map/ppermute | solution.py:788
  (4 other events, 3.1 us)
Sparse Core Ops, SparseCore 0:
  16.3 115.3 all-gather.2

commit v7 on v6

--- a/solution.py
+++ b/solution.py
@@ -17,7 +17,7 @@
 LOG2E = math.log2(math.e)
 MEGA = 1024 * 1024
 VMEM_ALL = 60
-PIECES = 4
+PIECES = 8
 SLOT = 16
 AXES = ("xl", "core", "xh", "y", "z")
 ROW = ("xl", "core")

time: 176 us -> 175 us (level)
  no operation moved by 1% of the time
where the time goes in v7:
time: 175 us
  Pallas kernels  94 us (54%)
  starting transfers between devices  46.6 us (27%)
  between operations  15 us (9%)
  waiting for transfers between devices  13.5 us (8%)
  local copies, waits for them, and re-layouts  4.98 us (3%)
    pallas_call x9, Pallas kernels, call(): pl.pallas_call(body, out_shape=tuple((jax.ShapeDtypeStruct(s, d) for s, d...  93.1 us
    all_to_all x4, starting transfers between devices, exchange(): return lax.all_to_all(value, axes, split_axis=0, concat_axis=0, tiled=True)  35.6 us
    ppermute x11, starting transfers between devices, permute(): lax.ppermute(value, axes, [(i, i ^ k) for i in range(lax.axis_size(axes))])  11 us
    all_to_all x4, waiting for transfers between devices, exchange(): return lax.all_to_all(value, axes, split_axis=0, concat_axis=0, tiled=True)  8.02 us
    ppermute x11, waiting for transfers between devices, permute(): lax.ppermute(value, axes, [(i, i ^ k) for i in range(lax.axis_size(axes))])  5.5 us
    unnamed x24, local copies, waits for them, and re-layouts  4.46 us
  transfers between devices with their start and end apart: 16, of which 5 were waited for; matrix products, arithmetic and copies ran while one was open for 0% of the time, Pallas kernels for 46%

profile of v7, /device:TPU:1, one launch (start us, length us, event | category | flops | bytes accessed | tf_op | source)
XLA Modules:
  0.0 174.7 jit_solution(7112642334762807949)
XLA Ops:
  8.5 7.6 %norm_project.1 = (bf16[1,2,1536,128]{3,2,1,0:T(8,128)(2,1)}, bf16[32,2,48,128]{3,2,1,0:T(8,128)(2,1)}, bf16[1,2,384,128]{3,2,1,0:T(8,128)(2,1)}, bf16[1,2,384,1...) custom-call(s32[1]{0:T(128)} %bitcast.refs_0_.refs_1_, ...), custom_call_target="tpu_custom_call" | custom-call | flops 7000000000 | bytes 11796996 | tf_op jit(solution)/shard_map/norm_project/pallas_call | solution.py:94
  16.1 1.5 collective-permute-start
  17.6 1.3 collective-permute-start.1
  19.4 10.6 %all-to-all-start = ((bf16[32,2,48,128]{3,2,1,0:T(8,128)(2,1)}), bf16[32,2,48,128]{3,2,1,0:T(8,128)(2,1)S(1)}, u32[]{:S(2)}, u32[]{:S(2)}) async-start(bf16[32,2,48,128]{3,2,1,0:T(8,128)(2,1)} %get-tuple-element.83), calls=%async_computation | async-start | bytes 1572864 | tf_op jit(solution)/shard_map/all_to_all | solution.py:792
  30.8 17.8 %scan_height.1 = (bf16[1,2,384,128]{3,2,1,0:T(8,128)(2,1)}, bf16[1,2,384,128]{3,2,1,0:T(8,128)(2,1)}, bf16[1,2,384,128]{3,2,1,0:T(8,128)(2,1)}, bf16[1,2,384,128...) custom-call(s32[8]{0:T(128)} %refs_0_.3, ...), custom_call_target="tpu_custom_call" | custom-call | flops 20000000000 | bytes 1579044 | tf_op jit(solution)/shard_map/scan_height/pallas_call | solution.py:94
  49.6 1.3 collective-permute-start.5
  51.8 20.6 %scan_width.1 = (bf16[32,2,48,128]{3,2,1,0:T(8,128)(2,1)}, bf16[128,1536]{1,0:T(8,128)(2,1)}, bf16[128,1536]{1,0:T(8,128)(2,1)}, bf16[128,128]{1,0:T(8,128)(2,1)...) custom-call(s32[64]{0:T(128)} %refs_0_.4, s32[1]{0:T(128)} %bitcast.refs_0_.refs_1_, bf16[32,2,48,128]{3,2,1,0:T(8,128)(2,1)} %copy-done.3, ...), custom_call_target="tpu_custom_call" | custom-call | flops 20000000000 | bytes 1579268 | tf_op jit(solution)/shard_map/scan_width/pallas_call | solution.py:94
  72.3 9.6 %all-to-all-start.1 = ((bf16[32,2,48,128]{3,2,1,0:T(8,128)(2,1)}), bf16[32,2,48,128]{3,2,1,0:T(8,128)(2,1)S(1)}, u32[]{:S(2)}, u32[]{:S(2)}) async-start(bf16[32,2,48,128]{3,2,1,0:T(8,128)(2,1)} %get-tuple-element.85), calls=%async_computation.1 | async-start | bytes 1572864 | tf_op jit(solution)/shard_map/all_to_all | solution.py:792
  82.0 20.5 %scan_time.1 = (bf16[1,2,1536,128]{3,2,1,0:T(8,128)(2,1)}, bf16[128,1536]{1,0:T(8,128)(2,1)}, bf16[128,1536]{1,0:T(8,128)(2,1)}, bf16[128,128]{1,0:T(8,128)(2,1)...) custom-call(s32[32]{0:T(128)} %refs_0_.5, s32[1]{0:T(128)} %bitcast.refs_0_.refs_1_, ...), custom_call_target="tpu_custom_call" | custom-call | flops 20000000000 | bytes 1579140 | tf_op jit(solution)/shard_map/scan_time/pallas_call | solution.py:94
  103.4 4.3 %sum_directions.1 = (bf16[128,1536]{1,0:T(8,128)(2,1)}, bf16[128,1536]{1,0:T(8,128)(2,1)}, bf16[16,192,128]{2,1,0:T(8,128)(2,1)}) custom-call(s32[1]{0:T(128)} %bitcast.refs_0_.refs_1_, bf16[128,1536]{1,0:T(8,128)(2,1)} %get-tuple-element.87.refs_1_.refs_2_, bf16[128,1536]{1,0:T(8,128)(2,1)} %get-tuple-element.88.refs_2_, ...), custom_call_target="tpu_custom_call" | custom-call | flops 6000000000 | bytes 3938308 | tf_op jit(solution)/shard_map/sum_directions/pallas_call | solution.py:94
  107.7 6.7 %all-to-all-start.2 = ((bf16[16,192,128]{2,1,0:T(8,128)(2,1)}), bf16[16,192,128]{2,1,0:T(8,128)(2,1)S(1)}, u32[]{:S(2)}, u32[]{:S(2)}) async-start(bf16[16,192,128]{2,1,0:T(8,128)(2,1)} %get-tuple-element.101), calls=%async_computation.2 | async-start | bytes 1572864 | tf_op jit(solution)/shard_map/all_to_all | solution.py:792
  114.4 4.5 %small_sums.1 = (f32[1536,128]{1,0:T(8,128)}, bf16[1536,128]{1,0:T(8,128)(2,1)}) custom-call(s32[1]{0:T(128)} %bitcast.refs_0_.refs_1_, bf16[1,2,1536,128]{3,2,1,0:T(8,128)(2,1)} %get-tuple-element.103.refs_2_.refs_1_, bf16[128,1536]{1,0:T(8,128)(2,1)} %get-tuple-element.87.refs_1_.refs_2_, bf16[128,1536]{1,0:T(8,128)(2,1)} %get-tuple-element.104.refs_3_, ...), custom_call_target="tpu_custom_call" | custom-call | flops 3000000000 | bytes 3784708 | tf_op jit(solution)/shard_map/small_sums/pallas_call | solution.py:94
  118.9 1.1 collective-permute-start.6
  120.0 8.2 %out_projections.1 = (bf16[32,2,2,1536]{3,2,1,0:T(2,128)(2,1)}, bf16[32,2,2,1536]{3,2,1,0:T(2,128)(2,1)}, f32[128,128]{1,0:T(8,128)}) custom-call(bf16[128,1536]{1,0:T(8,128)(2,1)} %get-tuple-element.95.refs_0_, bf16[128,1536]{1,0:T(8,128)(2,1)} %get-tuple-element.96.refs_1_, bf16[128,1536]{1,0:T(8,128)(2,1)} %get-tuple-element.97.refs_2_, ...), custom_call_target="tpu_custom_call" | custom-call | flops 6000000000 | bytes 10715136 | tf_op jit(solution)/shard_map/out_projections/pallas_call | solution.py:94
  128.2 5.0 %all-to-all-done.2.refs_0_.refs_1_ = bf16[16,192,128]{2,1,0:T(8,128)(2,1)S(1)} async-done(((bf16[16,192,128]{2,1,0:T(8,128)(2,1)}), bf16[16,192,128]{2,1,0:T(8,128)(2,1)S(1)}, u32[]{:S(2)}, u32[]{:S(2)}) %all-to-all-start.2) | async-done | bytes 786464 | tf_op jit(solution)/shard_map/all_to_all | solution.py:792
  134.1 5.3 %in_weight_grad.1 = bf16[128,32,128]{2,1,0:T(8,128)(2,1)} custom-call(bf16[16,192,128]{2,1,0:T(8,128)(2,1)} %copy-done.2, bf16[16,2,128,1536]{3,2,1,0:T(8,128)(2,1)} %bitcast.10, f32[1536,128]{1,0:T(8,128)} %get-tuple-element.122.refs_2_, bf16[1536,128]{1,0:T(8,128)(2,1)} %copy-done.5, f32[128,128]{1,0:T(8,128)} %get-tuple-element.124.refs_4_), custom_call_target="tpu_custom_call" | custom-call | flops 3000000000 | bytes 14614528 | tf_op jit(solution)/shard_map/in_weight_grad/pallas_call | solution.py:94
  139.4 8.7 %all-to-all-start.3 = ((bf16[128,32,128]{2,1,0:T(8,128)(2,1)}), bf16[128,32,128]{2,1,0:T(8,128)(2,1)S(1)}, u32[]{:S(2)}, u32[]{:S(2)}) async-start(bf16[128,32,128]{2,1,0:T(8,128)(2,1)} %in_weight_grad.1), calls=%async_computation.3 | async-start | bytes 2097152 | tf_op jit(solution)/shard_map/all_to_all | solution.py:792
  148.1 4.3 %out_weight_grad.1 = (f32[4,144,128]{2,1,0:T(8,128)}, bf16[4,144,128]{2,1,0:T(8,128)(2,1)}) custom-call(s32[1]{0:T(128)} %bitcast.5.refs_0_, bf16[16,192,128]{2,1,0:T(8,128)(2,1)} %copy-done.2, bf16[16,2,128,1536]{3,2,1,0:T(8,128)(2,1)} %bitcast.11), custom_call_target="tpu_custom_call" | custom-call | flops 4000000000 | bytes 13369348 | tf_op jit(solution)/shard_map/out_weight_grad/pallas_call | solution.py:94
  152.5 1.1 collective-permute-start.7
  153.6 1.2 collective-permute-done.7.other_ref
  154.9 1.0 copy-done.1
  155.8 2.3 %collective-permute-start.8 = (bf16[144,128]{1,0:T(8,128)(2,1)S(1)}, bf16[144,128]{1,0:T(8,128)(2,1)S(1)}, u32[]{:S(2)}, u32[]{:S(2)}) collective-permute-start(bf16[144,128]{1,0:T(8,128)(2,1)S(1)} %get-tuple-element.128), channel_id=1, source_target_pairs={{0,16},{16,0},{32,48},{48,32},{64,80},{80,64},{96,112},{112,96},{1... | collective-permute-start | bytes 110600 | tf_op jit(solution)/shard_map/ppermute | solution.py:788
  159.2 4.0 %collective-permute-done.8.refs_1_ = bf16[144,128]{1,0:T(8,128)(2,1)S(1)} collective-permute-done((bf16[144,128]{1,0:T(8,128)(2,1)S(1)}, bf16[144,128]{1,0:T(8,128)(2,1)S(1)}, u32[]{:S(2)}, u32[]{:S(2)}) %collective-permute-start.8) | collective-permute-done | bytes 36896 | tf_op jit(solution)/shard_map/ppermute | solution.py:788
  163.4 3.0 %all-to-all-done.3.all_ref = bf16[128,32,128]{2,1,0:T(8,128)(2,1)S(1)} async-done(((bf16[128,32,128]{2,1,0:T(8,128)(2,1)}), bf16[128,32,128]{2,1,0:T(8,128)(2,1)S(1)}, u32[]{:S(2)}, u32[]{:S(2)}) %all-to-all-start.3) | async-done | bytes 1048608 | tf_op jit(solution)/shard_map/all_to_all | solution.py:792
  (47 shorter events, 8.3 us)
Async XLA Ops:
  7.2 126.0 %all-gather.3.cloned.1.call-start = ((), (), s32[]{:S(2)}) async-start(), calls=%async_computation.4 | async-start | bytes 13369344 | tf_op jit(solution)/shard_map/all_gather | solution.py:853
  16.1 13.8 %collective-permute-start = (bf16[1,2,384,128]{3,2,1,0:T(8,128)(2,1)}, bf16[1,2,384,128]{3,2,1,0:T(8,128)(2,1)S(1)}, u32[]{:S(2)}, u32[]{:S(2)}) collective-permute-start(bf16[1,2,384,128]{3,2,1,0:T(8,128)(2,1)} %get-tuple-element.76), channel_id=1, source_target_pairs={{0,32},{32,0},{64,96},{96,64},{1,33},{33,1},{65,97},{97,65},{2,34}... | collective-permute-start | bytes 589832 | tf_op jit(solution)/shard_map/ppermute | solution.py:788
  17.6 12.4 %collective-permute-start.1 = (bf16[1,2,384,128]{3,2,1,0:T(8,128)(2,1)}, bf16[1,2,384,128]{3,2,1,0:T(8,128)(2,1)S(1)}, u32[]{:S(2)}, u32[]{:S(2)}) collective-permute-start(bf16[1,2,384,128]{3,2,1,0:T(8,128)(2,1)} %get-tuple-element.77), channel_id=1, source_target_pairs={{0,64},{32,96},{64,0},{96,32},{1,65},{33,97},{65,1},{97,33},{2,66}... | collective-permute-start | bytes 589832 | tf_op jit(solution)/shard_map/ppermute | solution.py:788
  19.0 11.1 %collective-permute-start.2 = (bf16[1,2,384,128]{3,2,1,0:T(8,128)(2,1)}, bf16[1,2,384,128]{3,2,1,0:T(8,128)(2,1)S(1)}, u32[]{:S(2)}, u32[]{:S(2)}) collective-permute-start(bf16[1,2,384,128]{3,2,1,0:T(8,128)(2,1)} %get-tuple-element.78), channel_id=1, source_target_pairs={{0,96},{32,64},{64,32},{96,0},{1,97},{33,65},{65,33},{97,1},{2,98}... | collective-permute-start | bytes 589832 | tf_op jit(solution)/shard_map/ppermute | solution.py:788
  19.4 31.5 %all-to-all-start = ((bf16[32,2,48,128]{3,2,1,0:T(8,128)(2,1)}), bf16[32,2,48,128]{3,2,1,0:T(8,128)(2,1)S(1)}, u32[]{:S(2)}, u32[]{:S(2)}) async-start(bf16[32,2,48,128]{3,2,1,0:T(8,128)(2,1)} %get-tuple-element.83), calls=%async_computation | async-start | bytes 1572864 | tf_op jit(solution)/shard_map/all_to_all | solution.py:792
  48.6 33.3 %collective-permute-start.3 = (bf16[1,2,384,128]{3,2,1,0:T(8,128)(2,1)}, bf16[1,2,384,128]{3,2,1,0:T(8,128)(2,1)S(1)}, u32[]{:S(2)}, u32[]{:S(2)}) collective-permute-start(bf16[1,2,384,128]{3,2,1,0:T(8,128)(2,1)} %get-tuple-element.80), channel_id=1, source_target_pairs={{0,32},{32,0},{64,96},{96,64},{1,33},{33,1},{65,97},{97,65},{2,34}... | collective-permute-start | bytes 589832 | tf_op jit(solution)/shard_map/ppermute | solution.py:788
  49.1 32.8 %collective-permute-start.4 = (bf16[1,2,384,128]{3,2,1,0:T(8,128)(2,1)}, bf16[1,2,384,128]{3,2,1,0:T(8,128)(2,1)S(1)}, u32[]{:S(2)}, u32[]{:S(2)}) collective-permute-start(bf16[1,2,384,128]{3,2,1,0:T(8,128)(2,1)} %get-tuple-element.81), channel_id=1, source_target_pairs={{0,64},{32,96},{64,0},{96,32},{1,65},{33,97},{65,1},{97,33},{2,66}... | collective-permute-start | bytes 589832 | tf_op jit(solution)/shard_map/ppermute | solution.py:788
  49.6 32.4 %collective-permute-start.5 = (bf16[1,2,384,128]{3,2,1,0:T(8,128)(2,1)}, bf16[1,2,384,128]{3,2,1,0:T(8,128)(2,1)S(1)}, u32[]{:S(2)}, u32[]{:S(2)}) collective-permute-start(bf16[1,2,384,128]{3,2,1,0:T(8,128)(2,1)} %get-tuple-element.82), channel_id=1, source_target_pairs={{0,96},{32,64},{64,32},{96,0},{1,97},{33,65},{65,33},{97,1},{2,98}... | collective-permute-start | bytes 589832 | tf_op jit(solution)/shard_map/ppermute | solution.py:788
  50.9 0.9 copy-start.3
  72.3 30.1 %all-to-all-start.1 = ((bf16[32,2,48,128]{3,2,1,0:T(8,128)(2,1)}), bf16[32,2,48,128]{3,2,1,0:T(8,128)(2,1)S(1)}, u32[]{:S(2)}, u32[]{:S(2)}) async-start(bf16[32,2,48,128]{3,2,1,0:T(8,128)(2,1)} %get-tuple-element.85), calls=%async_computation.1 | async-start | bytes 1572864 | tf_op jit(solution)/shard_map/all_to_all | solution.py:792
  81.9 20.5 %copy-start.6 = (bf16[1,2,384,128]{3,2,1,0:T(8,128)(2,1)}, bf16[1,2,384,128]{3,2,1,0:T(8,128)(2,1)S(1)}, u32[]{:S(2)}) copy-start(bf16[1,2,384,128]{3,2,1,0:T(8,128)(2,1)S(1)} %collective-permute-done.3.refs_6_) | copy-start | bytes 589828
  81.9 20.5 %copy-start.7 = (bf16[1,2,384,128]{3,2,1,0:T(8,128)(2,1)}, bf16[1,2,384,128]{3,2,1,0:T(8,128)(2,1)S(1)}, u32[]{:S(2)}) copy-start(bf16[1,2,384,128]{3,2,1,0:T(8,128)(2,1)S(1)} %collective-permute-done.4.refs_7_) | copy-start | bytes 589828
  82.0 20.5 %copy-start.8 = (bf16[1,2,384,128]{3,2,1,0:T(8,128)(2,1)}, bf16[1,2,384,128]{3,2,1,0:T(8,128)(2,1)S(1)}, u32[]{:S(2)}) copy-start(bf16[1,2,384,128]{3,2,1,0:T(8,128)(2,1)S(1)} %collective-permute-done.5.refs_8_) | copy-start | bytes 589828
  107.7 25.5 %all-to-all-start.2 = ((bf16[16,192,128]{2,1,0:T(8,128)(2,1)}), bf16[16,192,128]{2,1,0:T(8,128)(2,1)S(1)}, u32[]{:S(2)}, u32[]{:S(2)}) async-start(bf16[16,192,128]{2,1,0:T(8,128)(2,1)} %get-tuple-element.101), calls=%async_computation.2 | async-start | bytes 1572864 | tf_op jit(solution)/shard_map/all_to_all | solution.py:792
  118.9 9.3 %collective-permute-start.6 = (bf16[1536,128]{1,0:T(8,128)(2,1)}, bf16[1536,128]{1,0:T(8,128)(2,1)S(1)}, u32[]{:S(2)}, u32[]{:S(2)}) collective-permute-start(bf16[1536,128]{1,0:T(8,128)(2,1)} %get-tuple-element.119), channel_id=1, source_target_pairs={{0,32},{32,0},{64,96},{96,64},{1,33},{33,1},{65,97},{97,65},{2,34}... | collective-permute-start | bytes 1179656 | tf_op jit(solution)/shard_map/ppermute | solution.py:788
  128.2 5.0 %copy-start.5 = (bf16[1536,128]{1,0:T(8,128)(2,1)}, bf16[1536,128]{1,0:T(8,128)(2,1)S(1)}, u32[]{:S(2)}) copy-start(bf16[1536,128]{1,0:T(8,128)(2,1)S(1)} %collective-permute-done.6.refs_3_) | copy-start | bytes 1179652
  133.2 0.9 copy-start.2
  139.4 27.1 %all-to-all-start.3 = ((bf16[128,32,128]{2,1,0:T(8,128)(2,1)}), bf16[128,32,128]{2,1,0:T(8,128)(2,1)S(1)}, u32[]{:S(2)}, u32[]{:S(2)}) async-start(bf16[128,32,128]{2,1,0:T(8,128)(2,1)} %in_weight_grad.1), calls=%async_computation.3 | async-start | bytes 2097152 | tf_op jit(solution)/shard_map/all_to_all | solution.py:792
  148.1 18.3 %copy-start = (bf16[256]{0:T(256)(128)(2,1)S(1)}, bf16[256]{0:T(256)(128)(2,1)}, u32[]{:S(2)}) copy-start(bf16[256]{0:T(256)(128)(2,1)} %fusion.refs_2_.feature_ref) | copy-start | bytes 1540
  152.5 2.4 %collective-permute-start.7 = (bf16[4,144,128]{2,1,0:T(8,128)(2,1)}, bf16[4,144,128]{2,1,0:T(8,128)(2,1)S(1)}, u32[]{:S(2)}, u32[]{:S(2)}) collective-permute-start(bf16[4,144,128]{2,1,0:T(8,128)(2,1)} %get-tuple-element.126), channel_id=1, source_target_pairs={{0,32},{16,48},{32,0},{48,16},{64,96},{80,112},{96,64},{112,80},{1... | collective-permute-start | bytes 442376 | tf_op jit(solution)/shard_map/ppermute | solution.py:788
  154.8 1.0 copy-start.1
  155.8 7.3 %collective-permute-start.8 = (bf16[144,128]{1,0:T(8,128)(2,1)S(1)}, bf16[144,128]{1,0:T(8,128)(2,1)S(1)}, u32[]{:S(2)}, u32[]{:S(2)}) collective-permute-start(bf16[144,128]{1,0:T(8,128)(2,1)S(1)} %get-tuple-element.128), channel_id=1, source_target_pairs={{0,16},{16,0},{32,48},{48,32},{64,80},{80,64},{96,112},{112,96},{1... | collective-permute-start | bytes 110600 | tf_op jit(solution)/shard_map/ppermute | solution.py:788
  158.1 5.0 %collective-permute-start.9 = (bf16[144,128]{1,0:T(8,128)(2,1)S(1)}, bf16[144,128]{1,0:T(8,128)(2,1)S(1)}, u32[]{:S(2)}, u32[]{:S(2)}) collective-permute-start(bf16[144,128]{1,0:T(8,128)(2,1)S(1)} %get-tuple-element.129), channel_id=1, source_target_pairs={{0,64},{16,80},{32,96},{48,112},{64,0},{80,16},{96,32},{112,48},{1... | collective-permute-start | bytes 110600 | tf_op jit(solution)/shard_map/ppermute | solution.py:788
  158.4 5.0 %collective-permute-start.10 = (bf16[144,128]{1,0:T(8,128)(2,1)S(1)}, bf16[144,128]{1,0:T(8,128)(2,1)S(1)}, u32[]{:S(2)}, u32[]{:S(2)}) collective-permute-start(bf16[144,128]{1,0:T(8,128)(2,1)S(1)} %get-tuple-element.130), channel_id=1, source_target_pairs={{0,80},{16,64},{32,112},{48,96},{64,16},{80,0},{96,48},{112,32},{1... | collective-permute-start | bytes 110600 | tf_op jit(solution)/shard_map/ppermute | solution.py:788
  (4 other events, 3.1 us)
Sparse Core Ops, SparseCore 0:
  16.3 115.3 all-gather.2
